TPU v7x, 128 devices: a whole 4x4x4 slice. The times are simulated.
128 devices in a mesh: row: 8 (over z_lo, y), col: 16 (over x, z_hi, core).
Axes of the slice: x: 4, y: 4, z: 4 (z_hi: 2, z_lo: 2; z = z_hi * 2 + z_lo), core: 2. Of those that a mesh axis runs over, the one named last changes fastest.
Arguments:
- features: bfloat16 [32768, 512], P(('row', 'col')), may hold values from -6 to 6
- weight: bfloat16 [512, 512], replicated, may hold values from -0.25 to 0.25
- cotangent: bfloat16 [32768, 512], P(('row', 'col')), may hold values from -6 to 6
- tile_coords: int32 [8, 16, 192, 2], P('row', 'col'), may hold values from 0 to 31, as said below
- tile_values: bfloat16 [8, 16, 192, 128, 128], P('row', 'col'), may hold values from -0.09375 to 0.09375
- tile_count: int32 [8, 16], P('row', 'col'), may hold values from 24 to 192, as said below
Outputs:
- output: bfloat16 [32768, 512], P(('row', 'col'))
- features_grad: bfloat16 [32768, 512], P(('row', 'col'))
- weight_grad: float32 [512, 512], replicated
Inputs may be any that keep to these rules, and one draw needn't show every extreme that they name: `tile_coords`: within one device the slots name distinct tiles, and each of its 32 tile rows is named by exactly 6 slots; tile columns lie below 16. `tile_count`: exactly one device in each draw has all 192 slots live.
All inputs are finite; a program needn't handle non-finite values.
Results may differ from a plain program's by a relative error of at most 0.023.
Values may be sent and summed in bfloat16 or wider, within the bound.
No kernel may reach another device: no remote copies, remote signals or barrier semaphores. Data moves between devices by JAX's collectives and lax.ppermute only.
A program may use at most 128 MiB of HBM per device.

v0:
```python
import jax
import jax.numpy as jnp
from jax import lax
from jax.sharding import PartitionSpec as P

TILE = 128


slot_group = 32


def tile_sum(values, coords, count, source, src_pick, dst_pick, out_tiles, form):
    width = source.shape[-1]
    tiles = source.reshape(-1, TILE, width)
    src_tiles = tiles.shape[0]
    total = jnp.zeros((out_tiles, TILE, width), jnp.float32)

    def add_group(group_index, total):
        start = group_index * slot_group
        vals = lax.dynamic_slice_in_dim(values, start, slot_group, 0)
        crd = lax.dynamic_slice_in_dim(coords, start, slot_group, 0)
        src_onehot = (
            crd[:, src_pick][:, None] == jnp.arange(src_tiles, dtype=jnp.int32)[None, :]
        ).astype(jnp.bfloat16)
        picked = jnp.einsum(
            "sk,kjf->sjf", src_onehot, tiles, preferred_element_type=jnp.float32
        ).astype(jnp.bfloat16)
        prod = jnp.einsum(form, vals, picked, preferred_element_type=jnp.float32)
        live = start + jnp.arange(slot_group, dtype=jnp.int32) < count
        dst_match = crd[:, dst_pick][:, None] == jnp.arange(out_tiles, dtype=jnp.int32)[None, :]
        dst_onehot = jnp.logical_and(dst_match, live[:, None]).astype(jnp.bfloat16)
        upper = prod.astype(jnp.bfloat16)
        lower = (prod - upper.astype(jnp.float32)).astype(jnp.bfloat16)
        added = jnp.einsum("sk,sif->kif", dst_onehot, upper, preferred_element_type=jnp.float32)
        added = added + jnp.einsum(
            "sk,sif->kif", dst_onehot, lower, preferred_element_type=jnp.float32
        )
        return total + added

    steps = values.shape[0] // slot_group
    return lax.fori_loop(0, steps, add_group, total)


def per_device(features, weight, cotangent, tile_coords, tile_values, tile_count):
    values = tile_values[0, 0]
    coords = tile_coords[0, 0]
    count = tile_count[0, 0]
    span, width = features.shape
    row_tiles = lax.axis_size("col") * span // TILE
    col_tiles = lax.axis_size("row") * span // TILE
    projected = jnp.dot(features, weight, preferred_element_type=jnp.float32).astype(jnp.bfloat16)
    column_panel = lax.all_gather(projected, "row", axis=0, tiled=True)
    partial_value = tile_sum(values, coords, count, column_panel, 1, 0, row_tiles, "sij,sjf->sif")
    output = lax.psum_scatter(
        partial_value.reshape(row_tiles * TILE, width).astype(jnp.bfloat16),
        "col",
        scatter_dimension=0,
        tiled=True,
    )
    cot_panel = lax.all_gather(cotangent, "col", axis=0, tiled=True)
    back = tile_sum(values, coords, count, cot_panel, 0, 1, col_tiles, "sji,sjf->sif")
    agg_grad = lax.psum_scatter(
        back.reshape(col_tiles * TILE, width).astype(jnp.bfloat16),
        "row",
        scatter_dimension=0,
        tiled=True,
    )
    features_grad = jnp.dot(agg_grad, weight.T, preferred_element_type=jnp.float32).astype(
        jnp.bfloat16
    )
    local_term = lax.dot_general(
        features, agg_grad, (((0,), (0,)), ((), ())), preferred_element_type=jnp.float32
    )
    total_nodes = span * lax.axis_size("row") * lax.axis_size("col")
    weight_grad = lax.psum(local_term, ("row", "col")) * total_nodes ** (-0.5)
    return (output, features_grad, weight_grad)


def solution(mesh):
    return jax.shard_map(
        per_device,
        mesh=mesh,
        in_specs=(
            P(("row", "col"), None),
            P(),
            P(("row", "col"), None),
            P("row", "col", None, None),
            P("row", "col", None, None, None),
            P("row", "col"),
        ),
        out_specs=(P(("row", "col"), None), P(("row", "col"), None), P()),
        check_vma=False,
    )
```

profile of v0, /device:TPU:1, one launch (start us, length us, event | category | flops | bytes accessed | tf_op | source)
XLA Modules:
  0.0 593.1 jit_solution(8543333982111801195)
XLA Ops:
  8.0 8.7 %copy.21 = bf16[1,1,192,128,128]{3,4,2,1,0:T(8,128)(2,1)} copy(bf16[1,1,192,128,128]{4,3,2,1,0:T(8,128)(2,1)} %param.14) | data formatting | bytes 12582912 | tf_op args[4]
  16.6 53.5 %all-gather.5.cloned.1.call-done = bf16[4096,512]{1,0:T(8,128)(2,1)} async-done(((bf16[256,512]{1,0:T(8,128)(2,1)}), bf16[4096,512]{1,0:T(8,128)(2,1)}) %all-gather.5.cloned.1.call-update) | async-done | bytes 4194320 | tf_op jit(solution)/shard_map/all_gather | solution.py:60
  70.1 159.3 %while.29 = (s32[]{:T(128)}, f32[16,128,512]{2,0,1:T(8,128)}, s32[192,2]{0,1:T(2,128)S(1)}, s32[]{:T(128)}, bf16[192,128,128]{1,2,0:T(8,128)(2,1)}, /*index=5*/b...) while((s32[]{:T(128)}, f32[16,128,512]{2,0,1:T(8,128)}, ...), condition=%wide.region_4.0_spmd.clone, body=%wide.region_3.0_spmd.clone.sunk | while | flops 816843840 | bytes 47187604 | solution.py:41
  70.2 5.5 fusion.80
  75.7 6.0 %subtract_convert_fusion.5 = (bf16[32,128,512]{2,1,0:T(8,128)(2,1)S(1)}, bf16[32,128,512]{2,1,0:T(8,128)(2,1)}) fusion(bf16[32,128,512]{2,0,1:T(8,128)(2,1)S(1)} %fusion.80, bf16[192,128,128]{1,2,0:T(8,128)(2,1)} %get-tuple-element.459, s32[]{:T(128)S(6)} %select_n.21), kind=kOutput, calls=%fused_computation.27.clone.1 | convolution fusion | flops 545259520 | bytes 13631492 | tf_op jit(solution)/shard_map/while/body/eval_jaxpr/sji,sjf->sif/dot_general | solution.py:28
  82.3 4.8 fusion.81
  87.1 8.6 %select_add_fusion.5 = f32[16,128,512]{2,0,1:T(8,128)} fusion(f32[16,128,512]{2,0,1:T(8,128)} %get-tuple-element.446, f32[16,128,512]{2,0,1:T(8,128)} %fusion.81, bf16[32,128,512]{2,1,0:T(8,128)(2,1)} %get-tuple-element.404, pred[]{:T(512)S(6)} %compare.7, s32[32]{0:T(128)S(1)} %get-tuple-element.403, pred[32]{0:T(512)(128)(4,1)S(1)} %add_compare_fusion.5), kind=kOutput, calls=%fused_computation.35.clone.1 | convolution fusion | flops 70255616 | bytes 16777376 | tf_op jit(solution)/shard_map/while/body/eval_jaxpr/sk,sif->kif/dot_general | solution.py:34
  95.8 5.5 fusion.80
  101.2 6.0 %subtract_convert_fusion.5 = (bf16[32,128,512]{2,1,0:T(8,128)(2,1)S(1)}, bf16[32,128,512]{2,1,0:T(8,128)(2,1)}) fusion(bf16[32,128,512]{2,0,1:T(8,128)(2,1)S(1)} %fusion.80, bf16[192,128,128]{1,2,0:T(8,128)(2,1)} %get-tuple-element.459, s32[]{:T(128)S(6)} %select_n.21), kind=kOutput, calls=%fused_computation.27.clone.1 | convolution fusion | flops 545259520 | bytes 13631492 | tf_op jit(solution)/shard_map/while/body/eval_jaxpr/sji,sjf->sif/dot_general | solution.py:28
  107.9 4.8 fusion.81
  112.7 9.8 %select_add_fusion.5 = f32[16,128,512]{2,0,1:T(8,128)} fusion(f32[16,128,512]{2,0,1:T(8,128)} %get-tuple-element.446, f32[16,128,512]{2,0,1:T(8,128)} %fusion.81, bf16[32,128,512]{2,1,0:T(8,128)(2,1)} %get-tuple-element.404, pred[]{:T(512)S(6)} %compare.7, s32[32]{0:T(128)S(1)} %get-tuple-element.403, pred[32]{0:T(512)(128)(4,1)S(1)} %add_compare_fusion.5), kind=kOutput, calls=%fused_computation.35.clone.1 | convolution fusion | flops 70255616 | bytes 16777376 | tf_op jit(solution)/shard_map/while/body/eval_jaxpr/sk,sif->kif/dot_general | solution.py:34
  122.5 5.4 fusion.80
  128.0 6.0 %subtract_convert_fusion.5 = (bf16[32,128,512]{2,1,0:T(8,128)(2,1)S(1)}, bf16[32,128,512]{2,1,0:T(8,128)(2,1)}) fusion(bf16[32,128,512]{2,0,1:T(8,128)(2,1)S(1)} %fusion.80, bf16[192,128,128]{1,2,0:T(8,128)(2,1)} %get-tuple-element.459, s32[]{:T(128)S(6)} %select_n.21), kind=kOutput, calls=%fused_computation.27.clone.1 | convolution fusion | flops 545259520 | bytes 13631492 | tf_op jit(solution)/shard_map/while/body/eval_jaxpr/sji,sjf->sif/dot_general | solution.py:28
  139.4 9.8 %select_add_fusion.5 = f32[16,128,512]{2,0,1:T(8,128)} fusion(f32[16,128,512]{2,0,1:T(8,128)} %get-tuple-element.446, f32[16,128,512]{2,0,1:T(8,128)} %fusion.81, bf16[32,128,512]{2,1,0:T(8,128)(2,1)} %get-tuple-element.404, pred[]{:T(512)S(6)} %compare.7, s32[32]{0:T(128)S(1)} %get-tuple-element.403, pred[32]{0:T(512)(128)(4,1)S(1)} %add_compare_fusion.5), kind=kOutput, calls=%fused_computation.35.clone.1 | convolution fusion | flops 70255616 | bytes 16777376 | tf_op jit(solution)/shard_map/while/body/eval_jaxpr/sk,sif->kif/dot_general | solution.py:34
  149.3 5.4 fusion.80
  154.7 6.0 %subtract_convert_fusion.5 = (bf16[32,128,512]{2,1,0:T(8,128)(2,1)S(1)}, bf16[32,128,512]{2,1,0:T(8,128)(2,1)}) fusion(bf16[32,128,512]{2,0,1:T(8,128)(2,1)S(1)} %fusion.80, bf16[192,128,128]{1,2,0:T(8,128)(2,1)} %get-tuple-element.459, s32[]{:T(128)S(6)} %select_n.21), kind=kOutput, calls=%fused_computation.27.clone.1 | convolution fusion | flops 545259520 | bytes 13631492 | tf_op jit(solution)/shard_map/while/body/eval_jaxpr/sji,sjf->sif/dot_general | solution.py:28
  161.4 4.8 fusion.81
  166.2 9.8 %select_add_fusion.5 = f32[16,128,512]{2,0,1:T(8,128)} fusion(f32[16,128,512]{2,0,1:T(8,128)} %get-tuple-element.446, f32[16,128,512]{2,0,1:T(8,128)} %fusion.81, bf16[32,128,512]{2,1,0:T(8,128)(2,1)} %get-tuple-element.404, pred[]{:T(512)S(6)} %compare.7, s32[32]{0:T(128)S(1)} %get-tuple-element.403, pred[32]{0:T(512)(128)(4,1)S(1)} %add_compare_fusion.5), kind=kOutput, calls=%fused_computation.35.clone.1 | convolution fusion | flops 70255616 | bytes 16777376 | tf_op jit(solution)/shard_map/while/body/eval_jaxpr/sk,sif->kif/dot_general | solution.py:34
  176.0 5.4 fusion.80
  181.5 6.0 %subtract_convert_fusion.5 = (bf16[32,128,512]{2,1,0:T(8,128)(2,1)S(1)}, bf16[32,128,512]{2,1,0:T(8,128)(2,1)}) fusion(bf16[32,128,512]{2,0,1:T(8,128)(2,1)S(1)} %fusion.80, bf16[192,128,128]{1,2,0:T(8,128)(2,1)} %get-tuple-element.459, s32[]{:T(128)S(6)} %select_n.21), kind=kOutput, calls=%fused_computation.27.clone.1 | convolution fusion | flops 545259520 | bytes 13631492 | tf_op jit(solution)/shard_map/while/body/eval_jaxpr/sji,sjf->sif/dot_general | solution.py:28
  188.1 4.8 fusion.81
  192.9 9.8 %select_add_fusion.5 = f32[16,128,512]{2,0,1:T(8,128)} fusion(f32[16,128,512]{2,0,1:T(8,128)} %get-tuple-element.446, f32[16,128,512]{2,0,1:T(8,128)} %fusion.81, bf16[32,128,512]{2,1,0:T(8,128)(2,1)} %get-tuple-element.404, pred[]{:T(512)S(6)} %compare.7, s32[32]{0:T(128)S(1)} %get-tuple-element.403, pred[32]{0:T(512)(128)(4,1)S(1)} %add_compare_fusion.5), kind=kOutput, calls=%fused_computation.35.clone.1 | convolution fusion | flops 70255616 | bytes 16777376 | tf_op jit(solution)/shard_map/while/body/eval_jaxpr/sk,sif->kif/dot_general | solution.py:34
  202.8 5.4 fusion.80
  208.2 6.0 %subtract_convert_fusion.5 = (bf16[32,128,512]{2,1,0:T(8,128)(2,1)S(1)}, bf16[32,128,512]{2,1,0:T(8,128)(2,1)}) fusion(bf16[32,128,512]{2,0,1:T(8,128)(2,1)S(1)} %fusion.80, bf16[192,128,128]{1,2,0:T(8,128)(2,1)} %get-tuple-element.459, s32[]{:T(128)S(6)} %select_n.21), kind=kOutput, calls=%fused_computation.27.clone.1 | convolution fusion | flops 545259520 | bytes 13631492 | tf_op jit(solution)/shard_map/while/body/eval_jaxpr/sji,sjf->sif/dot_general | solution.py:28
  219.7 9.8 %select_add_fusion.5 = f32[16,128,512]{2,0,1:T(8,128)} fusion(f32[16,128,512]{2,0,1:T(8,128)} %get-tuple-element.446, f32[16,128,512]{2,0,1:T(8,128)} %fusion.81, bf16[32,128,512]{2,1,0:T(8,128)(2,1)} %get-tuple-element.404, pred[]{:T(512)S(6)} %compare.7, s32[32]{0:T(128)S(1)} %get-tuple-element.403, pred[32]{0:T(512)(128)(4,1)S(1)} %add_compare_fusion.5), kind=kOutput, calls=%fused_computation.35.clone.1 | convolution fusion | flops 70255616 | bytes 16777376 | tf_op jit(solution)/shard_map/while/body/eval_jaxpr/sk,sif->kif/dot_general | solution.py:34
  229.5 5.8 copy.52
  236.4 34.6 %reduce-scatter.5.cloned.1.call-done = bf16[256,512]{1,0:T(8,128)(2,1)} async-done(((bf16[2048,512]{1,0:T(8,128)(2,1)}), bf16[256,512]{1,0:T(8,128)(2,1)}) %reduce-scatter.5.cloned.1.call-update) | async-done | bytes 262160 | tf_op jit(solution)/shard_map/reduce_scatter | solution.py:62
  273.3 40.5 %all-gather.3.cloned.1.call-done = bf16[2048,512]{1,0:T(8,128)(2,1)} async-done(((bf16[256,512]{1,0:T(8,128)(2,1)}), bf16[2048,512]{1,0:T(8,128)(2,1)}) %all-gather.3.cloned.1.call-update) | async-done | bytes 2097168 | tf_op jit(solution)/shard_map/all_gather | solution.py:52
  313.8 181.2 %while.28 = (s32[]{:T(128)}, f32[32,128,512]{2,0,1:T(8,128)}, s32[192,2]{0,1:T(2,128)S(1)}, s32[]{:T(128)}, bf16[192,128,128]{2,1,0:T(8,128)(2,1)}, /*index=5*/b...) while((s32[]{:T(128)}, f32[32,128,512]{2,0,1:T(8,128)}, ...), condition=%wide.region_1.0_spmd.clone, body=%wide.region_0.0_spmd.clone.sunk | while | flops 887099968 | bytes 61867668 | solution.py:41
  317.0 6.0 %subtract_convert_fusion.4 = (bf16[32,128,512]{2,1,0:T(8,128)(2,1)S(1)}, bf16[32,128,512]{2,1,0:T(8,128)(2,1)}) fusion(bf16[32,128,512]{2,0,1:T(8,128)(2,1)S(1)} %fusion.72, bf16[192,128,128]{2,1,0:T(8,128)(2,1)} %get-tuple-element.429, s32[]{:T(128)S(6)} %select_n.20), kind=kOutput, calls=%fused_computation.2.clone.1 | convolution fusion | flops 545259520 | bytes 13631492 | tf_op jit(solution)/shard_map/while/body/eval_jaxpr/sij,sjf->sif/dot_general | solution.py:28
  323.7 6.5 %fusion.73 = f32[32,128,512]{2,0,1:T(8,128)} fusion(bf16[32,128,512]{2,1,0:T(8,128)(2,1)S(1)} %get-tuple-element.392, s32[32]{0:T(128)S(1)} %get-tuple-element.393, pred[32]{0:T(512)(128)(4,1)S(1)} %add_compare_fusion.4), kind=kOutput, calls=%fused_computation.4.clone.1 | convolution fusion | flops 134219776 | bytes 12583072 | tf_op jit(solution)/shard_map/while/body/eval_jaxpr/sk,sif->kif/dot_general | solution.py:35
  330.2 11.9 %select_add_fusion.4 = f32[32,128,512]{2,0,1:T(8,128)} fusion(f32[32,128,512]{2,0,1:T(8,128)} %get-tuple-element.416, f32[32,128,512]{2,0,1:T(8,128)} %fusion.73, pred[]{:T(512)S(6)} %compare.6, bf16[32,128,512]{2,1,0:T(8,128)(2,1)} %get-tuple-element.394, s32[32]{0:T(128)S(1)} %get-tuple-element.393, pred[32]{0:T(512)(128)(4,1)S(1)} %add_compare_fusion.4), kind=kOutput, calls=%fused_computation.1.clone.1 | convolution fusion | flops 140511232 | bytes 29360288 | tf_op jit(solution)/shard_map/while/body/eval_jaxpr/sk,sif->kif/dot_general | solution.py:34
  345.3 6.0 %subtract_convert_fusion.4 = (bf16[32,128,512]{2,1,0:T(8,128)(2,1)S(1)}, bf16[32,128,512]{2,1,0:T(8,128)(2,1)}) fusion(bf16[32,128,512]{2,0,1:T(8,128)(2,1)S(1)} %fusion.72, bf16[192,128,128]{2,1,0:T(8,128)(2,1)} %get-tuple-element.429, s32[]{:T(128)S(6)} %select_n.20), kind=kOutput, calls=%fused_computation.2.clone.1 | convolution fusion | flops 545259520 | bytes 13631492 | tf_op jit(solution)/shard_map/while/body/eval_jaxpr/sij,sjf->sif/dot_general | solution.py:28
  352.0 6.5 %fusion.73 = f32[32,128,512]{2,0,1:T(8,128)} fusion(bf16[32,128,512]{2,1,0:T(8,128)(2,1)S(1)} %get-tuple-element.392, s32[32]{0:T(128)S(1)} %get-tuple-element.393, pred[32]{0:T(512)(128)(4,1)S(1)} %add_compare_fusion.4), kind=kOutput, calls=%fused_computation.4.clone.1 | convolution fusion | flops 134219776 | bytes 12583072 | tf_op jit(solution)/shard_map/while/body/eval_jaxpr/sk,sif->kif/dot_general | solution.py:35
  358.5 14.2 %select_add_fusion.4 = f32[32,128,512]{2,0,1:T(8,128)} fusion(f32[32,128,512]{2,0,1:T(8,128)} %get-tuple-element.416, f32[32,128,512]{2,0,1:T(8,128)} %fusion.73, pred[]{:T(512)S(6)} %compare.6, bf16[32,128,512]{2,1,0:T(8,128)(2,1)} %get-tuple-element.394, s32[32]{0:T(128)S(1)} %get-tuple-element.393, pred[32]{0:T(512)(128)(4,1)S(1)} %add_compare_fusion.4), kind=kOutput, calls=%fused_computation.1.clone.1 | convolution fusion | flops 140511232 | bytes 29360288 | tf_op jit(solution)/shard_map/while/body/eval_jaxpr/sk,sif->kif/dot_general | solution.py:34
  375.9 6.0 %subtract_convert_fusion.4 = (bf16[32,128,512]{2,1,0:T(8,128)(2,1)S(1)}, bf16[32,128,512]{2,1,0:T(8,128)(2,1)}) fusion(bf16[32,128,512]{2,0,1:T(8,128)(2,1)S(1)} %fusion.72, bf16[192,128,128]{2,1,0:T(8,128)(2,1)} %get-tuple-element.429, s32[]{:T(128)S(6)} %select_n.20), kind=kOutput, calls=%fused_computation.2.clone.1 | convolution fusion | flops 545259520 | bytes 13631492 | tf_op jit(solution)/shard_map/while/body/eval_jaxpr/sij,sjf->sif/dot_general | solution.py:28
  382.6 6.5 %fusion.73 = f32[32,128,512]{2,0,1:T(8,128)} fusion(bf16[32,128,512]{2,1,0:T(8,128)(2,1)S(1)} %get-tuple-element.392, s32[32]{0:T(128)S(1)} %get-tuple-element.393, pred[32]{0:T(512)(128)(4,1)S(1)} %add_compare_fusion.4), kind=kOutput, calls=%fused_computation.4.clone.1 | convolution fusion | flops 134219776 | bytes 12583072 | tf_op jit(solution)/shard_map/while/body/eval_jaxpr/sk,sif->kif/dot_general | solution.py:35
  389.1 14.2 %select_add_fusion.4 = f32[32,128,512]{2,0,1:T(8,128)} fusion(f32[32,128,512]{2,0,1:T(8,128)} %get-tuple-element.416, f32[32,128,512]{2,0,1:T(8,128)} %fusion.73, pred[]{:T(512)S(6)} %compare.6, bf16[32,128,512]{2,1,0:T(8,128)(2,1)} %get-tuple-element.394, s32[32]{0:T(128)S(1)} %get-tuple-element.393, pred[32]{0:T(512)(128)(4,1)S(1)} %add_compare_fusion.4), kind=kOutput, calls=%fused_computation.1.clone.1 | convolution fusion | flops 140511232 | bytes 29360288 | tf_op jit(solution)/shard_map/while/body/eval_jaxpr/sk,sif->kif/dot_general | solution.py:34
  406.5 6.0 %subtract_convert_fusion.4 = (bf16[32,128,512]{2,1,0:T(8,128)(2,1)S(1)}, bf16[32,128,512]{2,1,0:T(8,128)(2,1)}) fusion(bf16[32,128,512]{2,0,1:T(8,128)(2,1)S(1)} %fusion.72, bf16[192,128,128]{2,1,0:T(8,128)(2,1)} %get-tuple-element.429, s32[]{:T(128)S(6)} %select_n.20), kind=kOutput, calls=%fused_computation.2.clone.1 | convolution fusion | flops 545259520 | bytes 13631492 | tf_op jit(solution)/shard_map/while/body/eval_jaxpr/sij,sjf->sif/dot_general | solution.py:28
  413.2 6.5 %fusion.73 = f32[32,128,512]{2,0,1:T(8,128)} fusion(bf16[32,128,512]{2,1,0:T(8,128)(2,1)S(1)} %get-tuple-element.392, s32[32]{0:T(128)S(1)} %get-tuple-element.393, pred[32]{0:T(512)(128)(4,1)S(1)} %add_compare_fusion.4), kind=kOutput, calls=%fused_computation.4.clone.1 | convolution fusion | flops 134219776 | bytes 12583072 | tf_op jit(solution)/shard_map/while/body/eval_jaxpr/sk,sif->kif/dot_general | solution.py:35
  419.7 14.3 %select_add_fusion.4 = f32[32,128,512]{2,0,1:T(8,128)} fusion(f32[32,128,512]{2,0,1:T(8,128)} %get-tuple-element.416, f32[32,128,512]{2,0,1:T(8,128)} %fusion.73, pred[]{:T(512)S(6)} %compare.6, bf16[32,128,512]{2,1,0:T(8,128)(2,1)} %get-tuple-element.394, s32[32]{0:T(128)S(1)} %get-tuple-element.393, pred[32]{0:T(512)(128)(4,1)S(1)} %add_compare_fusion.4), kind=kOutput, calls=%fused_computation.1.clone.1 | convolution fusion | flops 140511232 | bytes 29360288 | tf_op jit(solution)/shard_map/while/body/eval_jaxpr/sk,sif->kif/dot_general | solution.py:34
  437.1 6.0 %subtract_convert_fusion.4 = (bf16[32,128,512]{2,1,0:T(8,128)(2,1)S(1)}, bf16[32,128,512]{2,1,0:T(8,128)(2,1)}) fusion(bf16[32,128,512]{2,0,1:T(8,128)(2,1)S(1)} %fusion.72, bf16[192,128,128]{2,1,0:T(8,128)(2,1)} %get-tuple-element.429, s32[]{:T(128)S(6)} %select_n.20), kind=kOutput, calls=%fused_computation.2.clone.1 | convolution fusion | flops 545259520 | bytes 13631492 | tf_op jit(solution)/shard_map/while/body/eval_jaxpr/sij,sjf->sif/dot_general | solution.py:28
  443.8 6.5 %fusion.73 = f32[32,128,512]{2,0,1:T(8,128)} fusion(bf16[32,128,512]{2,1,0:T(8,128)(2,1)S(1)} %get-tuple-element.392, s32[32]{0:T(128)S(1)} %get-tuple-element.393, pred[32]{0:T(512)(128)(4,1)S(1)} %add_compare_fusion.4), kind=kOutput, calls=%fused_computation.4.clone.1 | convolution fusion | flops 134219776 | bytes 12583072 | tf_op jit(solution)/shard_map/while/body/eval_jaxpr/sk,sif->kif/dot_general | solution.py:35
  450.3 14.2 %select_add_fusion.4 = f32[32,128,512]{2,0,1:T(8,128)} fusion(f32[32,128,512]{2,0,1:T(8,128)} %get-tuple-element.416, f32[32,128,512]{2,0,1:T(8,128)} %fusion.73, pred[]{:T(512)S(6)} %compare.6, bf16[32,128,512]{2,1,0:T(8,128)(2,1)} %get-tuple-element.394, s32[32]{0:T(128)S(1)} %get-tuple-element.393, pred[32]{0:T(512)(128)(4,1)S(1)} %add_compare_fusion.4), kind=kOutput, calls=%fused_computation.1.clone.1 | convolution fusion | flops 140511232 | bytes 29360288 | tf_op jit(solution)/shard_map/while/body/eval_jaxpr/sk,sif->kif/dot_general | solution.py:34
  467.7 6.0 %subtract_convert_fusion.4 = (bf16[32,128,512]{2,1,0:T(8,128)(2,1)S(1)}, bf16[32,128,512]{2,1,0:T(8,128)(2,1)}) fusion(bf16[32,128,512]{2,0,1:T(8,128)(2,1)S(1)} %fusion.72, bf16[192,128,128]{2,1,0:T(8,128)(2,1)} %get-tuple-element.429, s32[]{:T(128)S(6)} %select_n.20), kind=kOutput, calls=%fused_computation.2.clone.1 | convolution fusion | flops 545259520 | bytes 13631492 | tf_op jit(solution)/shard_map/while/body/eval_jaxpr/sij,sjf->sif/dot_general | solution.py:28
  474.4 6.5 %fusion.73 = f32[32,128,512]{2,0,1:T(8,128)} fusion(bf16[32,128,512]{2,1,0:T(8,128)(2,1)S(1)} %get-tuple-element.392, s32[32]{0:T(128)S(1)} %get-tuple-element.393, pred[32]{0:T(512)(128)(4,1)S(1)} %add_compare_fusion.4), kind=kOutput, calls=%fused_computation.4.clone.1 | convolution fusion | flops 134219776 | bytes 12583072 | tf_op jit(solution)/shard_map/while/body/eval_jaxpr/sk,sif->kif/dot_general | solution.py:35
  480.9 14.2 %select_add_fusion.4 = f32[32,128,512]{2,0,1:T(8,128)} fusion(f32[32,128,512]{2,0,1:T(8,128)} %get-tuple-element.416, f32[32,128,512]{2,0,1:T(8,128)} %fusion.73, pred[]{:T(512)S(6)} %compare.6, bf16[32,128,512]{2,1,0:T(8,128)(2,1)} %get-tuple-element.394, s32[32]{0:T(128)S(1)} %get-tuple-element.393, pred[32]{0:T(512)(128)(4,1)S(1)} %add_compare_fusion.4), kind=kOutput, calls=%fused_computation.1.clone.1 | convolution fusion | flops 140511232 | bytes 29360288 | tf_op jit(solution)/shard_map/while/body/eval_jaxpr/sk,sif->kif/dot_general | solution.py:34
  508.1 78.5 %reduce-scatter.3.cloned.1.call-done = bf16[256,512]{1,0:T(8,128)(2,1)} async-done(((bf16[4096,512]{1,0:T(8,128)(2,1)}), bf16[256,512]{1,0:T(8,128)(2,1)}) %reduce-scatter.3.cloned.1.call-update) | async-done | bytes 262160 | tf_op jit(solution)/shard_map/reduce_scatter | solution.py:54
  (72 shorter events, 54.3 us)
Async XLA Ops:
  7.2 228.2 %copy-start = (bf16[512,512]{1,0:T(8,128)(2,1)S(1)}, bf16[512,512]{1,0:T(8,128)(2,1)}, u32[]{:S(2)}) copy-start(bf16[512,512]{1,0:T(8,128)(2,1)} %param.11) | copy-start | bytes 1572868
  7.2 62.9 %all-gather.5.cloned.1.call-start = ((), (), s32[]{:S(2)}) async-start(), calls=%async_computation.4 | async-start | bytes 4456448 | tf_op jit(solution)/shard_map/all_gather | solution.py:60
  7.9 263.1 %reduce-scatter.5.cloned.1.call-start = ((), (), s32[]{:S(2)}) async-start(), calls=%async_computation.5 | async-start | bytes 2359296 | tf_op jit(solution)/shard_map/reduce_scatter | solution.py:62
  8.0 62.2 %copy-start.3 = (s32[1,1,192,2]{2,3,1,0:T(2,128)S(1)}, s32[1,1,192,2]{2,3,1,0:T(2,128)}, u32[]{:S(2)}) copy-start(s32[1,1,192,2]{2,3,1,0:T(2,128)} %param.13) | copy-start | bytes 4612
  229.4 5.9 copy-start.1
  235.3 78.6 %all-gather.3.cloned.1.call-start = ((), (), s32[]{:S(2)}) async-start(), calls=%async_computation.2 | async-start | bytes 2359296 | tf_op jit(solution)/shard_map/all_gather | solution.py:52
  236.4 269.1 %all-reduce.2.cloned.1.call-start = ((), (), s32[]{:S(2)}) async-start(), calls=%async_computation.6 | async-start | bytes 2097152 | tf_op jit(solution)/shard_map/psum | solution.py:75
  273.3 313.3 %reduce-scatter.3.cloned.1.call-start = ((), (), s32[]{:S(2)}) async-start(), calls=%async_computation.3 | async-start | bytes 4456448 | tf_op jit(solution)/shard_map/reduce_scatter | solution.py:54
  503.5 0.9 copy-start.2
Sparse Core Ops, SparseCore 0:
  10.4 59.6 all-gather.4
  235.4 35.5 reduce-scatter.4
  273.2 40.5 all-gather.2
  319.1 151.4 all-reduce.1
  503.6 82.9 reduce-scatter.2
where the time goes:
time: 595 us; the launch traced here: 593 us
  matrix products  336 us (56%)
  waiting for transfers between devices  208 us (35%)
  local copies, waits for them, and re-layouts  22 us (4%)
  between operations  13.8 us (2%)
  other arithmetic  13.2 us (2%)
    dot_general x12, matrix products, add_group(): jnp.einsum('sk,sif->kif', dst_onehot, upper, preferred_element_type=jnp.f...  140 us
    reduce_scatter x1, waiting for transfers between devices, per_device(): lax.psum_scatter(partial_value.reshape(row_tiles * TILE, width).astype(jn...  78.5 us
    dot_general x12, matrix products, add_group(): prod = jnp.einsum(form, vals, picked, preferred_element_type=jnp.float32)  72.1 us
    dot_general x12, matrix products, add_group(): jnp.einsum('sk,sif->kif', dst_onehot, lower, preferred_element_type=jnp.f...  67.7 us
    all_gather x1, waiting for transfers between devices, per_device(): cot_panel = lax.all_gather(cotangent, 'col', axis=0, tiled=True)  53.5 us
    dot_general x12, matrix products, add_group(): jnp.einsum('sk,kjf->sjf', src_onehot, tiles, preferred_element_type=jnp.f...  51.5 us
    all_gather x1, waiting for transfers between devices, per_device(): column_panel = lax.all_gather(projected, 'row', axis=0, tiled=True)  40.5 us
    reduce_scatter x1, waiting for transfers between devices, per_device(): lax.psum_scatter(back.reshape(col_tiles * TILE, width).astype(jnp.bfloat1...  34.6 us
  transfers between devices with their start and end apart: 5, of which 4 were waited for; matrix products, arithmetic and copies ran while one was open for 35% of the time, Pallas kernels for 0%

commit v1 on v0

v1 whole, which is shorter than its diff:
```python
import functools

import jax
import jax.numpy as jnp
from jax import lax
from jax.experimental import pallas as pl
from jax.experimental.pallas import tpu as pltpu
from jax.sharding import PartitionSpec as P

TILE = 128
SPAN = 256
FEAT = 512
PER_ROW = 6
ROW_TILES = 32
COL_TILES = 16
SLOTS = 192
CHUNK = 6
ROW_STEP = 4
CHUNK_STEP = 4
MAX_CHUNKS = 64
BF16 = jnp.bfloat16
F32 = jnp.float32
SMEM = pl.BlockSpec(memory_space=pltpu.SMEM)
VMEM = pl.BlockSpec(memory_space=pltpu.VMEM)


def flat(x, y, z, core):
    return ((z % 2) * 4 + y % 4) * 16 + (x % 4) * 4 + (z // 2) * 2 + core


def permute(value, step):
    pairs = [
        (flat(x, y, z, c), flat(*step(x, y, z, c)))
        for x in range(4)
        for y in range(4)
        for z in range(4)
        for c in range(2)
    ]
    return lax.ppermute(value, ("row", "col"), pairs)


def to_core(x, y, z, c):
    return x, y, z, 1 - c


def to_z_near(x, y, z, c):
    return x, y, z ^ 1, c


def to_z_far(x, y, z, c):
    return x, y, z ^ 2, c


def along_x(k):
    return lambda x, y, z, c: (x + k, y, z, c)


def along_y(k):
    return lambda x, y, z, c: (x, y + k, z, c)


def block(i):
    return pl.ds(pl.multiple_of(i * TILE, TILE), TILE)


def ring_place(distance):
    return jnp.where(distance == 0, 0, jnp.where(distance == 3, 1, distance + 1))


def lists_kernel(coords, count, row_slot, row_col, chunk_col, chunk_slot, chunk_row, n_chunks, row_fill, col_fill, col_chunk):
    row, col = lax.axis_index("row"), lax.axis_index("col")
    my_y, my_near = row % 4, row // 4
    my_x, my_far, my_core = col // 4, (col // 2) % 2, col % 2
    live = count[0, 0]

    def col_place(b):
        owner = b // 2
        place = ring_place((owner % 4 - my_y + 4) % 4) * 2 + (owner // 4 + my_near) % 2
        return place * 2 + b % 2

    def place_of_row(a):
        owner = a // 2
        place = ((owner % 2 + my_core) % 2) * 8 + ring_place((owner // 4 - my_x + 4) % 4) * 2
        return (place + ((owner // 2) % 2 + my_far) % 2) * 2 + a % 2

    def clear_row(a, carry):
        row_fill[a] = 0
        return carry

    def clear_col(b, carry):
        col_fill[b] = CHUNK
        col_chunk[b] = 0
        return carry

    lax.fori_loop(0, ROW_TILES, clear_row, 0)
    lax.fori_loop(0, COL_TILES, clear_col, 0)

    def slot(s, used):
        a = place_of_row(coords[0, 0, s, 0])
        b = col_place(coords[0, 0, s, 1])
        n = row_fill[a]
        row_fill[a] = n + 1
        is_live = s < live
        row_slot[a * PER_ROW + n] = jnp.where(is_live, s, -1)
        row_col[a * PER_ROW + n] = b
        m = col_fill[b]
        opens = jnp.logical_and(is_live, m == CHUNK)

        @pl.when(opens)
        def _():
            col_chunk[b] = used
            chunk_col[used] = b
            for i in range(CHUNK):
                chunk_slot[used * CHUNK + i] = -1
                chunk_row[used * CHUNK + i] = 0

        @pl.when(is_live)
        def _():
            k = jnp.where(opens, 0, m)
            place = col_chunk[b] * CHUNK + k
            chunk_slot[place] = s
            chunk_row[place] = a
            col_fill[b] = k + 1

        return jnp.where(opens, used + 1, used)

    used = lax.fori_loop(0, SLOTS, slot, 0)
    n_chunks[0] = (used + CHUNK_STEP - 1) // CHUNK_STEP
    for k in range(CHUNK_STEP):
        chunk_col[used + k] = 0
        for i in range(CHUNK):
            chunk_slot[(used + k) * CHUNK + i] = -1
            chunk_row[(used + k) * CHUNK + i] = 0


def make_lists(coords, count):
    def ints(n):
        return jax.ShapeDtypeStruct((n,), jnp.int32)

    return pl.pallas_call(
        lists_kernel,
        out_shape=(
            ints(SLOTS),
            ints(SLOTS),
            ints(MAX_CHUNKS),
            ints(MAX_CHUNKS * CHUNK),
            ints(MAX_CHUNKS * CHUNK),
            ints(1),
        ),
        in_specs=[SMEM, SMEM],
        out_specs=(SMEM,) * 6,
        scratch_shapes=[pltpu.SMEM((ROW_TILES,), jnp.int32), pltpu.SMEM((COL_TILES,), jnp.int32), pltpu.SMEM((COL_TILES,), jnp.int32)],
    )(coords, count)


def live_tile(values, slot):
    tile = values[jnp.maximum(slot, 0)]
    return tile * jnp.where(slot >= 0, 1.0, 0.0).astype(BF16)


def tiles_kernel(row_slot, row_col, chunk_col, chunk_slot, chunk_row, n_chunks, values, feats, cots, rows_out, cols_out, total):
    def row_step(q, carry):
        for k in range(ROW_STEP):
            a = q * ROW_STEP + k
            tiles = [live_tile(values, row_slot[a * PER_ROW + i]) for i in range(PER_ROW)]
            source = [feats[block(row_col[a * PER_ROW + i]), :] for i in range(PER_ROW)]
            rows_out[block(a), :] = jnp.dot(
                jnp.concatenate(tiles, axis=1), jnp.concatenate(source, axis=0), preferred_element_type=F32
            ).astype(BF16)
        return carry

    lax.fori_loop(0, ROW_TILES // ROW_STEP, row_step, 0)
    total[...] = jnp.zeros_like(total)

    def chunk_step(q, carry):
        products = []
        for k in range(CHUNK_STEP):
            first = (q * CHUNK_STEP + k) * CHUNK
            tiles = [live_tile(values, chunk_slot[first + i]) for i in range(CHUNK)]
            source = [cots[block(chunk_row[first + i]), :] for i in range(CHUNK)]
            products.append(
                lax.dot_general(
                    jnp.concatenate(tiles, axis=0),
                    jnp.concatenate(source, axis=0),
                    (((0,), (0,)), ((), ())),
                    preferred_element_type=F32,
                )
            )
        for k in range(CHUNK_STEP):
            total[block(chunk_col[q * CHUNK_STEP + k]), :] += products[k]
        return carry

    lax.fori_loop(0, n_chunks[0], chunk_step, 0)
    cols_out[...] = total[...].astype(BF16)


def tile_sums(lists, values, feats, cots):
    return pl.pallas_call(
        tiles_kernel,
        out_shape=(
            jax.ShapeDtypeStruct((ROW_TILES * TILE, FEAT), BF16),
            jax.ShapeDtypeStruct((COL_TILES * TILE, FEAT), BF16),
        ),
        in_specs=[SMEM] * 6 + [VMEM] * 3,
        out_specs=(VMEM, VMEM),
        scratch_shapes=[pltpu.VMEM((COL_TILES * TILE, FEAT), F32)],
        compiler_params=pltpu.CompilerParams(vmem_limit_bytes=40 * 2**20),
    )(*lists, values, feats, cots)


def stack(*parts):
    return jnp.concatenate(parts, axis=0)


def add(*parts):
    total = parts[0].astype(F32)
    for part in parts[1:]:
        total = total + part.astype(F32)
    return total.astype(BF16)


def gather(own, near, ring):
    pair = stack(own, permute(own, near))
    before, after = permute(pair, ring(1)), permute(pair, ring(-1))
    far = stack(permute(before[:SPAN], ring(1)), permute(after[SPAN:], ring(-1)))
    return stack(pair, before, after, far)


def scatter(parts, near, ring):
    own, before, after, far = (parts[i * 2 * SPAN : (i + 1) * 2 * SPAN] for i in range(4))
    to_after = permute(far[:SPAN], ring(1))
    to_before = permute(far[SPAN:], ring(-1))
    from_before = permute(stack(add(after[:SPAN], to_after), after[SPAN:]), ring(1))
    from_after = permute(stack(before[:SPAN], add(before[SPAN:], to_before)), ring(-1))
    passed = permute(add(own[SPAN:], from_before[SPAN:], from_after[SPAN:]), near)
    return add(own[:SPAN], from_before[:SPAN], from_after[:SPAN], passed)


def per_device(features, weight, cotangent, tile_coords, tile_values, tile_count):
    values = tile_values[0, 0]
    lists = make_lists(tile_coords, tile_count)
    feats = gather(features, to_z_near, along_y)
    half = gather(cotangent, to_z_far, along_x)
    cots = stack(half, permute(half, to_core))
    row_part, col_part = tile_sums(lists, values, feats, cots)
    term = lax.dot_general(feats, col_part, (((0,), (0,)), ((), ())), preferred_element_type=F32).astype(BF16)
    mine, other = row_part[: 8 * SPAN], row_part[8 * SPAN :]
    aggregated = scatter(add(mine, permute(other, to_core)), to_z_far, along_x)
    agg_grad = scatter(col_part, to_z_near, along_y)
    output = jnp.dot(aggregated, weight, preferred_element_type=F32).astype(BF16)
    features_grad = lax.dot_general(agg_grad, weight, (((1,), (1,)), ((), ())), preferred_element_type=F32).astype(BF16)
    devices = lax.axis_size("row") * lax.axis_size("col")
    pieces = lax.all_to_all(term.reshape(devices, FEAT // devices, FEAT), ("row", "col"), 0, 0)
    piece = jnp.sum(pieces.astype(F32), axis=0).astype(BF16)
    spread = jnp.broadcast_to(piece[None], (devices,) + piece.shape)
    whole = lax.all_to_all(spread, ("row", "col"), 0, 0)
    weight_grad = whole.reshape(FEAT, FEAT).astype(F32) * (devices * SPAN) ** (-0.5)
    return output, features_grad, weight_grad


def solution(mesh):
    return jax.shard_map(
        per_device,
        mesh=mesh,
        in_specs=(
            P(("row", "col"), None),
            P(),
            P(("row", "col"), None),
            P("row", "col", None, None),
            P("row", "col", None, None, None),
            P("row", "col"),
        ),
        out_specs=(P(("row", "col"), None), P(("row", "col"), None), P()),
        check_vma=False,
    )
```

time: 595 us -> 185 us (0.31)
  matrix products: 336 us -> 5.55 us
  waiting for transfers between devices: 208 us -> 50.6 us
  starting transfers between devices: 0.2 us -> 57 us
  Pallas kernels: 0 us -> 29.4 us
  between operations: 13.8 us -> 1.54 us
  local copies, waits for them, and re-layouts: 22 us -> 28 us
    dot_general x51 -> x3, matrix products: 336 us -> 5.55 us  [the longest x1 2.16 us: per_device(): lax.dot_general(agg_grad, weight, (((1,), (1,)), ((), ())), preferred_ele...]
    reduce_scatter x2 -> x0, waiting for transfers between devices: 113 us -> none  [the longest x1 78.5 us: per_device(): lax.psum_scatter(partial_value.reshape(row_tiles * TILE, width).astype(jn...]
    all_gather x2 -> x0, waiting for transfers between devices: 94 us -> none  [the longest x1 53.5 us: per_device(): cot_panel = lax.all_gather(cotangent, 'col', axis=0, tiled=True)]
    ppermute x0 -> x22, waiting for transfers between devices: none -> 46.3 us  [permute(): return lax.ppermute(value, ('row', 'col'), pairs)]
    ppermute x0 -> x22, starting transfers between devices: none -> 38.7 us  [permute(): return lax.ppermute(value, ('row', 'col'), pairs)]
    pallas_call x0 -> x2, Pallas kernels: none -> 29.5 us  [the longest x1 17.2 us: make_lists(): pl.pallas_call(lists_kernel, out_shape=(ints(SLOTS), ints(SLOTS), ints(MA...]
    all_to_all x0 -> x2, starting transfers between devices: none -> 18.3 us  [the longest x1 9.99 us: per_device(): lax.all_to_all(term.reshape(devices, FEAT // devices, FEAT), ('row', 'col...]
    lt x12 -> x0, other arithmetic: 7.8 us -> none  [add_group(): live = start + jnp.arange(slot_group, dtype=jnp.int32) < count]
  transfers between devices with their start and end apart: 5 -> 24, of which waited for: 4 -> 10; matrix products, arithmetic and copies ran while one was open for 35% -> 17% of each run, Pallas kernels for 0% -> 9%
where the time goes in v1:
time: 185 us
  starting transfers between devices  57 us (31%)
  waiting for transfers between devices  50.6 us (27%)
  Pallas kernels  29.4 us (16%)
  local copies, waits for them, and re-layouts  28 us (15%)
  other arithmetic  12.4 us (7%)
  matrix products  5.55 us (3%)
    ppermute x22, waiting for transfers between devices, permute(): return lax.ppermute(value, ('row', 'col'), pairs)  46.3 us
    ppermute x22, starting transfers between devices, permute(): return lax.ppermute(value, ('row', 'col'), pairs)  38.7 us
    pallas_call x1, Pallas kernels, make_lists(): pl.pallas_call(lists_kernel, out_shape=(ints(SLOTS), ints(SLOTS), ints(MA...  17.2 us
    pallas_call x1, Pallas kernels, tile_sums(): pl.pallas_call(tiles_kernel, out_shape=(jax.ShapeDtypeStruct((ROW_TILES *...  12.3 us
    unnamed x36, local copies, waits for them, and re-layouts  11.3 us
    all_to_all x1, starting transfers between devices, per_device(): lax.all_to_all(term.reshape(devices, FEAT // devices, FEAT), ('row', 'col...  9.99 us
    all_to_all x1, starting transfers between devices, per_device(): whole = lax.all_to_all(spread, ('row', 'col'), 0, 0)  8.28 us
    convert_element_type x5, other arithmetic, add(): return total.astype(BF16)  6.61 us
  transfers between devices with their start and end apart: 24, of which 10 were waited for; matrix products, arithmetic and copies ran while one was open for 17% of the time, Pallas kernels for 9%

profile of v1, /device:TPU:1, one launch (start us, length us, event | category | flops | bytes accessed | tf_op | source)
XLA Modules:
  0.0 184.6 jit_solution(11302978900910305342)
XLA Ops:
  0.6 4.5 %collective-permute-start.5 = (bf16[256,512]{1,0:T(8,128)(2,1)}, bf16[256,512]{1,0:T(8,128)(2,1)S(1)}, u32[]{:S(2)}, u32[]{:S(2)}) collective-permute-start(bf16[256,512]{1,0:T(8,128)(2,1)} %param.8), channel_id=1, source_target_pairs={{0,2},{1,3},{64,66},{65,67},{2,0},{3,1},{66,64},{67,65},{16,18},{1... | collective-permute-start | bytes 786440 | tf_op jit(solution)/shard_map/ppermute | solution.py:39
  5.2 1.8 constant_dynamic-update-slice_fusion.15
  6.9 4.5 %collective-permute-done.5 = bf16[256,512]{1,0:T(8,128)(2,1)S(1)} collective-permute-done((bf16[256,512]{1,0:T(8,128)(2,1)}, bf16[256,512]{1,0:T(8,128)(2,1)S(1)}, u32[]{:S(2)}, u32[]{:S(2)}) %collective-permute-start.5) | collective-permute-done | bytes 262176 | tf_op jit(solution)/shard_map/ppermute | solution.py:39
  12.1 1.2 collective-permute-start.6
  13.4 1.5 collective-permute-start.7
  14.8 10.7 %collective-permute-done.6 = bf16[512,512]{1,0:T(8,128)(2,1)S(1)} collective-permute-done((bf16[512,512]{1,0:T(8,128)(2,1)S(1)}, bf16[512,512]{1,0:T(8,128)(2,1)S(1)}, u32[]{:S(2)}, u32[]{:S(2)}) %collective-permute-start.6) | collective-permute-done | bytes 524320 | tf_op jit(solution)/shard_map/ppermute | solution.py:39
  25.7 2.7 %collective-permute-start.9 = (bf16[256,512]{1,0:T(8,128)(2,1)S(1)}, bf16[256,512]{1,0:T(8,128)(2,1)S(1)}, u32[]{:S(2)}, u32[]{:S(2)}) collective-permute-start(bf16[256,512]{1,0:T(8,128)(2,1)S(1)} %slice.147), channel_id=1, source_target_pairs={{0,12},{1,13},{64,76},{65,77},{2,14},{3,15},{66,78},{67,79},{16,28... | collective-permute-start | bytes 786440 | tf_op jit(solution)/shard_map/ppermute | solution.py:39
  30.2 2.3 %collective-permute-done.8 = bf16[256,512]{1,0:T(8,128)(2,1)S(1)} collective-permute-done((bf16[256,512]{1,0:T(8,128)(2,1)S(1)}, bf16[256,512]{1,0:T(8,128)(2,1)S(1)}, u32[]{:S(2)}, u32[]{:S(2)}) %collective-permute-start.8) | collective-permute-done | bytes 262176 | tf_op jit(solution)/shard_map/ppermute | solution.py:39
  34.0 3.1 %collective-permute-start.10 = (bf16[2048,512]{1,0:T(8,128)(2,1)}, bf16[2048,512]{1,0:T(8,128)(2,1)}, u32[]{:S(2)}, u32[]{:S(2)}) collective-permute-start(bf16[2048,512]{1,0:T(8,128)(2,1)} %get-tuple-element.35), channel_id=1, source_target_pairs={{0,1},{1,0},{64,65},{65,64},{2,3},{3,2},{66,67},{67,66},{16,17},{1... | collective-permute-start | bytes 6291464 | tf_op jit(solution)/shard_map/ppermute | solution.py:39
  38.3 6.6 %collective-permute-done = bf16[256,512]{1,0:T(8,128)(2,1)S(1)} collective-permute-done((bf16[256,512]{1,0:T(8,128)(2,1)S(1)}, bf16[256,512]{1,0:T(8,128)(2,1)S(1)}, u32[]{:S(2)}, u32[]{:S(2)}) %collective-permute-start) | collective-permute-done | bytes 262176 | tf_op jit(solution)/shard_map/ppermute | solution.py:39
  45.7 1.3 collective-permute-start.1
  47.0 1.4 collective-permute-start.2
  48.5 11.4 %collective-permute-done.1 = bf16[512,512]{1,0:T(8,128)(2,1)S(1)} collective-permute-done((bf16[512,512]{1,0:T(8,128)(2,1)}, bf16[512,512]{1,0:T(8,128)(2,1)S(1)}, u32[]{:S(2)}, u32[]{:S(2)}) %collective-permute-start.1) | collective-permute-done | bytes 524320 | tf_op jit(solution)/shard_map/ppermute | solution.py:39
  62.1 17.2 %shard_map.85 = (s32[192]{0:T(256)}, s32[192]{0:T(256)}, s32[64]{0:T(128)}, s32[384]{0:T(512)}, s32[384]{0:T(512)}, /*index=5*/s32[1]{0:T(128)}) custom-call(s32[1,1,192,2]{3,2,1,0:T(8,128)} %copy.9.coords, s32[1,1]{1,0:T(1,128)S(6)} %copy.28.count), custom_call_target="tpu_custom_call" | custom-call | tf_op jit(solution)/shard_map/pallas_call | solution.py:140
  80.3 2.7 %collective-permute-start.4 = (bf16[256,512]{1,0:T(8,128)(2,1)S(1)}, bf16[256,512]{1,0:T(8,128)(2,1)S(1)}, u32[]{:S(2)}, u32[]{:S(2)}) collective-permute-start(bf16[256,512]{1,0:T(8,128)(2,1)S(1)} %slice.145), channel_id=1, source_target_pairs={{0,48},{1,49},{64,112},{65,113},{2,50},{3,51},{66,114},{67,115},{1... | collective-permute-start | bytes 786440 | tf_op jit(solution)/shard_map/ppermute | solution.py:39
  84.1 2.5 %collective-permute-done.4 = bf16[256,512]{1,0:T(8,128)(2,1)S(1)} collective-permute-done((bf16[256,512]{1,0:T(8,128)(2,1)S(1)}, bf16[256,512]{1,0:T(8,128)(2,1)S(1)}, u32[]{:S(2)}, u32[]{:S(2)}) %collective-permute-start.4) | collective-permute-done | bytes 262176 | tf_op jit(solution)/shard_map/ppermute | solution.py:39
  86.7 3.1 %constant_dynamic-update-slice_fusion.16.cots = bf16[4096,512]{1,0:T(8,128)(2,1)} fusion(bf16[4096,512]{1,0:T(8,128)(2,1)} %copy-done.3, bf16[2048,512]{1,0:T(8,128)(2,1)} %collective-permute-done.10), kind=kLoop, calls=%fused_computation.39 | loop fusion | bytes 4194304 | tf_op jit(solution)/shard_map/concatenate | solution.py:212
  89.8 2.2 %copy-done.4 = bf16[4096,512]{1,0:T(8,128)(2,1)S(1)} copy-done((bf16[4096,512]{1,0:T(8,128)(2,1)S(1)}, bf16[4096,512]{1,0:T(8,128)(2,1)}, u32[]{:S(2)}) %copy-start.4) | copy-done | bytes 4194328
  91.9 12.3 %shard_map.86 = (bf16[4096,512]{1,0:T(8,128)(2,1)}, bf16[2048,512]{1,0:T(8,128)(2,1)S(1)}) custom-call(s32[192]{0:T(256)S(1)} %copy-done.7, s32[192]{0:T(256)S(1)} %copy-done.8, s32[64]{0:T(128)S(1)} %copy-done.9, s32[384]{0:T(512)S(1)} %copy-done.5, s32[384]{0:T(512)S(1)} %copy-done.6, s32[1]{0:T(128)} %get-tuple-element.16.n_chunks, ...), custom_call_target="tpu_custom_call" | custom-call | tf_op jit(solution)/shard_map/pallas_call | solution.py:198
  104.2 3.8 %slice.119 = bf16[2048,512]{1,0:T(8,128)(2,1)} slice(bf16[4096,512]{1,0:T(8,128)(2,1)} %get-tuple-element.17), slice={[2048:4096], [0:512]} | slice | bytes 4194304 | tf_op jit(solution)/shard_map/slice | solution.py:247
  108.0 4.1 %collective-permute-start.11 = (bf16[2048,512]{1,0:T(8,128)(2,1)}, bf16[2048,512]{1,0:T(8,128)(2,1)}, u32[]{:S(2)}, u32[]{:S(2)}) collective-permute-start(bf16[2048,512]{1,0:T(8,128)(2,1)} %slice.119), channel_id=1, source_target_pairs={{0,1},{1,0},{64,65},{65,64},{2,3},{3,2},{66,67},{67,66},{16,17},{1... | collective-permute-start | bytes 6291464 | tf_op jit(solution)/shard_map/ppermute | solution.py:39
  112.1 1.3 convolution_convert_fusion
  114.3 10.0 %all-to-all-start = ((bf16[128,4,512]{2,1,0:T(4,128)(2,1)}), bf16[128,4,512]{2,1,0:T(4,128)(2,1)S(1)}, u32[]{:S(2)}, u32[]{:S(2)}) async-start(bf16[128,4,512]{2,1,0:T(4,128)(2,1)} %reshape.14), calls=%async_computation | async-start | bytes 1048576 | tf_op jit(solution)/shard_map/all_to_all | solution.py:253
  124.3 1.3 fusion.6
  125.6 1.5 collective-permute-start.17
  127.0 1.3 collective-permute-start.19
  128.4 2.8 %add_convert_fusion = bf16[2048,512]{1,0:T(8,128)(2,1)S(1)} fusion(bf16[2048,512]{1,0:T(8,128)(2,1)} %collective-permute-done.11, bf16[4096,512]{1,0:T(8,128)(2,1)} %get-tuple-element.17), kind=kLoop, calls=%fused_computation | loop fusion | flops 4194304 | bytes 6291456 | tf_op jit(solution)/shard_map/convert_element_type | solution.py:219
  131.2 1.3 copy-done.10
  133.4 1.3 collective-permute-start.12
  134.8 1.3 collective-permute-start.14
  136.1 2.3 %collective-permute-done.17 = bf16[256,512]{1,0:T(8,128)(2,1)S(1)} collective-permute-done((bf16[256,512]{1,0:T(8,128)(2,1)S(1)}, bf16[256,512]{1,0:T(8,128)(2,1)S(1)}, u32[]{:S(2)}, u32[]{:S(2)}) %collective-permute-start.17) | collective-permute-done | bytes 262176 | tf_op jit(solution)/shard_map/ppermute | solution.py:39
  140.7 2.2 %collective-permute-start.20 = (bf16[512,512]{1,0:T(8,128)(2,1)}, bf16[512,512]{1,0:T(8,128)(2,1)}, u32[]{:S(2)}, u32[]{:S(2)}) collective-permute-start(bf16[512,512]{1,0:T(8,128)(2,1)} %pad_maximum_fusion.3), channel_id=1, source_target_pairs={{0,48},{1,49},{64,112},{65,113},{2,50},{3,51},{66,114},{67,115},{1... | collective-permute-start | bytes 1572872 | tf_op jit(solution)/shard_map/ppermute | solution.py:39
  144.1 8.3 %all-to-all-start.1 = ((bf16[128,4,512]{2,1,0:T(4,128)(2,1)}), bf16[128,4,512]{2,1,0:T(4,128)(2,1)S(1)}, u32[]{:S(2)}, u32[]{:S(2)}) async-start(bf16[128,4,512]{2,1,0:T(4,128)(2,1)} %broadcast_in_dim.2), calls=%async_computation.1 | async-start | bytes 1048576 | tf_op jit(solution)/shard_map/all_to_all | solution.py:256
  152.4 1.3 add_convert_fusion.8
  153.8 1.8 pad_maximum_fusion
  155.6 1.4 collective-permute-start.13
  157.8 1.3 collective-permute-start.15
  159.1 1.1 add_convert_fusion.2
  160.2 1.6 collective-permute-start.21
  161.8 4.4 %all-to-all-done.1 = bf16[128,4,512]{2,1,0:T(4,128)(2,1)S(1)} async-done(((bf16[128,4,512]{2,1,0:T(4,128)(2,1)}), bf16[128,4,512]{2,1,0:T(4,128)(2,1)S(1)}, u32[]{:S(2)}, u32[]{:S(2)}) %all-to-all-start.1) | async-done | bytes 524320 | tf_op jit(solution)/shard_map/all_to_all | solution.py:256
  166.1 1.2 convert_multiply_fusion
  167.4 2.6 %mul.11 = f32[512,512]{1,0:T(8,128)} reshape(f32[128,4,512]{2,1,0:T(4,128)} %convert_multiply_fusion) | data formatting | bytes 2097152 | tf_op jit(solution)/shard_map/mul | solution.py:257
  169.9 2.3 %collective-permute-done.13 = bf16[512,512]{1,0:T(8,128)(2,1)} collective-permute-done((bf16[512,512]{1,0:T(8,128)(2,1)}, bf16[512,512]{1,0:T(8,128)(2,1)}, u32[]{:S(2)}, u32[]{:S(2)}) %collective-permute-start.13) | collective-permute-done | bytes 524320 | tf_op jit(solution)/shard_map/ppermute | solution.py:39
  172.2 1.2 add_convert_fusion.6
  173.4 3.2 %collective-permute-start.16 = (bf16[256,512]{1,0:T(8,128)(2,1)S(1)}, bf16[256,512]{1,0:T(8,128)(2,1)S(1)}, u32[]{:S(2)}, u32[]{:S(2)}) collective-permute-start(bf16[256,512]{1,0:T(8,128)(2,1)S(1)} %add_convert_fusion.6), channel_id=1, source_target_pairs={{0,2},{1,3},{64,66},{65,67},{2,0},{3,1},{66,64},{67,65},{16,18},{1... | collective-permute-start | bytes 786440 | tf_op jit(solution)/shard_map/ppermute | solution.py:39
  176.6 2.2 %convolution_convert_fusion.1 = bf16[256,512]{1,0:T(8,128)(2,1)} fusion(bf16[512,512]{1,0:T(8,128)(2,1)S(1)} %copy-done, bf16[256,512]{1,0:T(8,128)(2,1)} %collective-permute-done.21, bf16[512,512]{1,0:T(8,128)(2,1)} %collective-permute-done.20, bf16[512,512]{1,0:T(8,128)(2,1)} %collective-permute-done.18, bf16[2048,512]{1,0:T(8,128)(2,1)S(1)} %copy-done.2), kind=kOutput, calls=%fused_computation.2 | convolution fusion | flops 135397376 | bytes 1835008 | tf_op jit(solution)/shard_map/dot_general | solution.py:251
  178.8 3.7 %collective-permute-done.16 = bf16[256,512]{1,0:T(8,128)(2,1)S(1)} collective-permute-done((bf16[256,512]{1,0:T(8,128)(2,1)S(1)}, bf16[256,512]{1,0:T(8,128)(2,1)S(1)}, u32[]{:S(2)}, u32[]{:S(2)}) %collective-permute-start.16) | collective-permute-done | bytes 262176 | tf_op jit(solution)/shard_map/ppermute | solution.py:39
  182.4 2.1 %convolution_convert_fusion.2 = bf16[256,512]{1,0:T(8,128)(2,1)} fusion(bf16[512,512]{1,0:T(8,128)(2,1)S(1)} %copy-done, bf16[256,512]{1,0:T(8,128)(2,1)S(1)} %collective-permute-done.16, bf16[512,512]{1,0:T(8,128)(2,1)} %collective-permute-done.15, bf16[512,512]{1,0:T(8,128)(2,1)} %collective-permute-done.13, bf16[2048,512]{1,0:T(8,128)(2,1)} %copy-done.10), kind=kOutput, calls=%fused_computation.3 | convolution fusion | flops 135397376 | bytes 1835008 | tf_op jit(solution)/shard_map/dot_general | solution.py:250
  (66 shorter events, 16.1 us)
Async XLA Ops:
  0.6 176.0 %copy-start = (bf16[512,512]{1,0:T(8,128)(2,1)S(1)}, bf16[512,512]{1,0:T(8,128)(2,1)}, u32[]{:S(2)}) copy-start(bf16[512,512]{1,0:T(8,128)(2,1)} %param.7) | copy-start | bytes 1572868
  0.6 10.7 %collective-permute-start.5 = (bf16[256,512]{1,0:T(8,128)(2,1)}, bf16[256,512]{1,0:T(8,128)(2,1)S(1)}, u32[]{:S(2)}, u32[]{:S(2)}) collective-permute-start(bf16[256,512]{1,0:T(8,128)(2,1)} %param.8), channel_id=1, source_target_pairs={{0,2},{1,3},{64,66},{65,67},{2,0},{3,1},{66,64},{67,65},{16,18},{1... | collective-permute-start | bytes 786440 | tf_op jit(solution)/shard_map/ppermute | solution.py:39
  12.1 13.4 %collective-permute-start.6 = (bf16[512,512]{1,0:T(8,128)(2,1)S(1)}, bf16[512,512]{1,0:T(8,128)(2,1)S(1)}, u32[]{:S(2)}, u32[]{:S(2)}) collective-permute-start(bf16[512,512]{1,0:T(8,128)(2,1)S(1)} %get-tuple-element.41), channel_id=1, source_target_pairs={{0,4},{1,5},{64,68},{65,69},{2,6},{3,7},{66,70},{67,71},{16,20},{1... | collective-permute-start | bytes 1572872 | tf_op jit(solution)/shard_map/ppermute | solution.py:39
  13.4 12.3 %collective-permute-start.7 = (bf16[512,512]{1,0:T(8,128)(2,1)S(1)}, bf16[512,512]{1,0:T(8,128)(2,1)S(1)}, u32[]{:S(2)}, u32[]{:S(2)}) collective-permute-start(bf16[512,512]{1,0:T(8,128)(2,1)S(1)} %get-tuple-element.41), channel_id=1, source_target_pairs={{0,12},{1,13},{64,76},{65,77},{2,14},{3,15},{66,78},{67,79},{16,28... | collective-permute-start | bytes 1572872 | tf_op jit(solution)/shard_map/ppermute | solution.py:39
  25.6 6.9 %collective-permute-start.8 = (bf16[256,512]{1,0:T(8,128)(2,1)S(1)}, bf16[256,512]{1,0:T(8,128)(2,1)S(1)}, u32[]{:S(2)}, u32[]{:S(2)}) collective-permute-start(bf16[256,512]{1,0:T(8,128)(2,1)S(1)} %slice.146), channel_id=1, source_target_pairs={{0,4},{1,5},{64,68},{65,69},{2,6},{3,7},{66,70},{67,71},{16,20},{1... | collective-permute-start | bytes 786440 | tf_op jit(solution)/shard_map/ppermute | solution.py:39
  25.7 7.6 %collective-permute-start.9 = (bf16[256,512]{1,0:T(8,128)(2,1)S(1)}, bf16[256,512]{1,0:T(8,128)(2,1)S(1)}, u32[]{:S(2)}, u32[]{:S(2)}) collective-permute-start(bf16[256,512]{1,0:T(8,128)(2,1)S(1)} %slice.147), channel_id=1, source_target_pairs={{0,12},{1,13},{64,76},{65,77},{2,14},{3,15},{66,78},{67,79},{16,28... | collective-permute-start | bytes 786440 | tf_op jit(solution)/shard_map/ppermute | solution.py:39
  28.4 8.7 %copy-start.11 = (bf16[256,512]{1,0:T(8,128)(2,1)S(1)}, bf16[256,512]{1,0:T(8,128)(2,1)}, u32[]{:S(2)}) copy-start(bf16[256,512]{1,0:T(8,128)(2,1)} %param.6) | copy-start | bytes 786436
  30.2 30.4 %copy-start.12 = (s32[1,1,192,2]{2,3,1,0:T(2,128)S(1)}, s32[1,1,192,2]{2,3,1,0:T(2,128)}, u32[]{:S(2)}) copy-start(s32[1,1,192,2]{2,3,1,0:T(2,128)} %param.9) | copy-start | bytes 4612
  34.0 11.7 %copy-start.3 = (bf16[4096,512]{1,0:T(8,128)(2,1)}, bf16[4096,512]{1,0:T(8,128)(2,1)S(1)}, u32[]{:S(2)}) copy-start(bf16[4096,512]{1,0:T(8,128)(2,1)S(1)} %get-tuple-element.36) | copy-start | bytes 12582916
  34.0 52.6 %collective-permute-start.10 = (bf16[2048,512]{1,0:T(8,128)(2,1)}, bf16[2048,512]{1,0:T(8,128)(2,1)}, u32[]{:S(2)}, u32[]{:S(2)}) collective-permute-start(bf16[2048,512]{1,0:T(8,128)(2,1)} %get-tuple-element.35), channel_id=1, source_target_pairs={{0,1},{1,0},{64,65},{65,64},{2,3},{3,2},{66,67},{67,66},{16,17},{1... | collective-permute-start | bytes 6291464 | tf_op jit(solution)/shard_map/ppermute | solution.py:39
  37.1 7.9 %collective-permute-start = (bf16[256,512]{1,0:T(8,128)(2,1)S(1)}, bf16[256,512]{1,0:T(8,128)(2,1)S(1)}, u32[]{:S(2)}, u32[]{:S(2)}) collective-permute-start(bf16[256,512]{1,0:T(8,128)(2,1)S(1)} %copy-done.11), channel_id=1, source_target_pairs={{0,64},{1,65},{64,0},{65,1},{2,66},{3,67},{66,2},{67,3},{16,80},{1... | collective-permute-start | bytes 786440 | tf_op jit(solution)/shard_map/ppermute | solution.py:39
  45.7 14.1 %collective-permute-start.1 = (bf16[512,512]{1,0:T(8,128)(2,1)}, bf16[512,512]{1,0:T(8,128)(2,1)S(1)}, u32[]{:S(2)}, u32[]{:S(2)}) collective-permute-start(bf16[512,512]{1,0:T(8,128)(2,1)} %get-tuple-element.45), channel_id=1, source_target_pairs={{0,16},{1,17},{64,80},{65,81},{2,18},{3,19},{66,82},{67,83},{16,32... | collective-permute-start | bytes 1572872 | tf_op jit(solution)/shard_map/ppermute | solution.py:39
  47.0 32.3 %collective-permute-start.2 = (bf16[512,512]{1,0:T(8,128)(2,1)}, bf16[512,512]{1,0:T(8,128)(2,1)}, u32[]{:S(2)}, u32[]{:S(2)}) collective-permute-start(bf16[512,512]{1,0:T(8,128)(2,1)} %get-tuple-element.45), channel_id=1, source_target_pairs={{0,48},{1,49},{64,112},{65,113},{2,50},{3,51},{66,114},{67,115},{1... | collective-permute-start | bytes 1572872 | tf_op jit(solution)/shard_map/ppermute | solution.py:39
  60.6 23.5 %collective-permute-start.3 = (bf16[256,512]{1,0:T(8,128)(2,1)}, bf16[256,512]{1,0:T(8,128)(2,1)S(1)}, u32[]{:S(2)}, u32[]{:S(2)}) collective-permute-start(bf16[256,512]{1,0:T(8,128)(2,1)} %slice.144), channel_id=1, source_target_pairs={{0,16},{1,17},{64,80},{65,81},{2,18},{3,19},{66,82},{67,83},{16,32... | collective-permute-start | bytes 786440 | tf_op jit(solution)/shard_map/ppermute | solution.py:39
  80.3 6.3 %collective-permute-start.4 = (bf16[256,512]{1,0:T(8,128)(2,1)S(1)}, bf16[256,512]{1,0:T(8,128)(2,1)S(1)}, u32[]{:S(2)}, u32[]{:S(2)}) collective-permute-start(bf16[256,512]{1,0:T(8,128)(2,1)S(1)} %slice.145), channel_id=1, source_target_pairs={{0,48},{1,49},{64,112},{65,113},{2,50},{3,51},{66,114},{67,115},{1... | collective-permute-start | bytes 786440 | tf_op jit(solution)/shard_map/ppermute | solution.py:39
  86.6 3.1 %copy-start.5 = (s32[384]{0:T(512)S(1)}, s32[384]{0:T(512)}, u32[]{:S(2)}) copy-start(s32[384]{0:T(512)} %get-tuple-element.14.chunk_slot) | copy-start | bytes 4612
  86.6 3.1 %copy-start.6 = (s32[384]{0:T(512)S(1)}, s32[384]{0:T(512)}, u32[]{:S(2)}) copy-start(s32[384]{0:T(512)} %get-tuple-element.15.chunk_row) | copy-start | bytes 4612
  86.6 3.1 %copy-start.7 = (s32[192]{0:T(256)S(1)}, s32[192]{0:T(256)}, u32[]{:S(2)}) copy-start(s32[192]{0:T(256)} %get-tuple-element.11.row_slot) | copy-start | bytes 2308
  86.6 3.1 %copy-start.8 = (s32[192]{0:T(256)S(1)}, s32[192]{0:T(256)}, u32[]{:S(2)}) copy-start(s32[192]{0:T(256)} %get-tuple-element.12.row_col) | copy-start | bytes 2308
  86.6 3.1 %copy-start.9 = (s32[64]{0:T(128)S(1)}, s32[64]{0:T(128)}, u32[]{:S(2)}) copy-start(s32[64]{0:T(128)} %get-tuple-element.13.chunk_col) | copy-start | bytes 772
  89.7 2.2 %copy-start.4 = (bf16[4096,512]{1,0:T(8,128)(2,1)S(1)}, bf16[4096,512]{1,0:T(8,128)(2,1)}, u32[]{:S(2)}) copy-start(bf16[4096,512]{1,0:T(8,128)(2,1)} %constant_dynamic-update-slice_fusion.16.cots) | copy-start | bytes 12582916
  104.2 7.9 %copy-start.1 = (bf16[2048,512]{1,0:T(8,128)(2,1)}, bf16[2048,512]{1,0:T(8,128)(2,1)S(1)}, u32[]{:S(2)}) copy-start(bf16[2048,512]{1,0:T(8,128)(2,1)S(1)} %get-tuple-element.18) | copy-start | bytes 6291460
  108.0 20.4 %collective-permute-start.11 = (bf16[2048,512]{1,0:T(8,128)(2,1)}, bf16[2048,512]{1,0:T(8,128)(2,1)}, u32[]{:S(2)}, u32[]{:S(2)}) collective-permute-start(bf16[2048,512]{1,0:T(8,128)(2,1)} %slice.119), channel_id=1, source_target_pairs={{0,1},{1,0},{64,65},{65,64},{2,3},{3,2},{66,67},{67,66},{16,17},{1... | collective-permute-start | bytes 6291464 | tf_op jit(solution)/shard_map/ppermute | solution.py:39
  114.3 28.6 %all-to-all-start = ((bf16[128,4,512]{2,1,0:T(4,128)(2,1)}), bf16[128,4,512]{2,1,0:T(4,128)(2,1)S(1)}, u32[]{:S(2)}, u32[]{:S(2)}) async-start(bf16[128,4,512]{2,1,0:T(4,128)(2,1)} %reshape.14), calls=%async_computation | async-start | bytes 1048576 | tf_op jit(solution)/shard_map/all_to_all | solution.py:253
  125.6 12.9 %collective-permute-start.17 = (bf16[256,512]{1,0:T(8,128)(2,1)S(1)}, bf16[256,512]{1,0:T(8,128)(2,1)S(1)}, u32[]{:S(2)}, u32[]{:S(2)}) collective-permute-start(bf16[256,512]{1,0:T(8,128)(2,1)S(1)} %get-tuple-element.21), channel_id=1, source_target_pairs={{0,16},{1,17},{64,80},{65,81},{2,18},{3,19},{66,82},{67,83},{16,32... | collective-permute-start | bytes 786440 | tf_op jit(solution)/shard_map/ppermute | solution.py:39
  127.0 11.4 %collective-permute-start.19 = (bf16[256,512]{1,0:T(8,128)(2,1)S(1)}, bf16[256,512]{1,0:T(8,128)(2,1)S(1)}, u32[]{:S(2)}, u32[]{:S(2)}) collective-permute-start(bf16[256,512]{1,0:T(8,128)(2,1)S(1)} %get-tuple-element.22), channel_id=1, source_target_pairs={{0,48},{1,49},{64,112},{65,113},{2,50},{3,51},{66,114},{67,115},{1... | collective-permute-start | bytes 786440 | tf_op jit(solution)/shard_map/ppermute | solution.py:39
  131.2 1.3 copy-start.10
  132.5 5.9 %copy-start.2 = (bf16[2048,512]{1,0:T(8,128)(2,1)S(1)}, bf16[2048,512]{1,0:T(8,128)(2,1)}, u32[]{:S(2)}) copy-start(bf16[2048,512]{1,0:T(8,128)(2,1)} %copy-done.1) | copy-start | bytes 6291460
  133.4 19.0 %collective-permute-start.12 = (bf16[256,512]{1,0:T(8,128)(2,1)}, bf16[256,512]{1,0:T(8,128)(2,1)}, u32[]{:S(2)}, u32[]{:S(2)}) collective-permute-start(bf16[256,512]{1,0:T(8,128)(2,1)} %get-tuple-element.27), channel_id=1, source_target_pairs={{0,4},{1,5},{64,68},{65,69},{2,6},{3,7},{66,70},{67,71},{16,20},{1... | collective-permute-start | bytes 786440 | tf_op jit(solution)/shard_map/ppermute | solution.py:39
  134.8 17.6 %collective-permute-start.14 = (bf16[256,512]{1,0:T(8,128)(2,1)}, bf16[256,512]{1,0:T(8,128)(2,1)}, u32[]{:S(2)}, u32[]{:S(2)}) collective-permute-start(bf16[256,512]{1,0:T(8,128)(2,1)} %get-tuple-element.28), channel_id=1, source_target_pairs={{0,12},{1,13},{64,76},{65,77},{2,14},{3,15},{66,78},{67,79},{16,28... | collective-permute-start | bytes 786440 | tf_op jit(solution)/shard_map/ppermute | solution.py:39
  139.4 19.7 %collective-permute-start.18 = (bf16[512,512]{1,0:T(8,128)(2,1)}, bf16[512,512]{1,0:T(8,128)(2,1)}, u32[]{:S(2)}, u32[]{:S(2)}) collective-permute-start(bf16[512,512]{1,0:T(8,128)(2,1)} %pad_maximum_fusion.2), channel_id=1, source_target_pairs={{0,16},{1,17},{64,80},{65,81},{2,18},{3,19},{66,82},{67,83},{16,32... | collective-permute-start | bytes 1572872 | tf_op jit(solution)/shard_map/ppermute | solution.py:39
  140.7 18.4 %collective-permute-start.20 = (bf16[512,512]{1,0:T(8,128)(2,1)}, bf16[512,512]{1,0:T(8,128)(2,1)}, u32[]{:S(2)}, u32[]{:S(2)}) collective-permute-start(bf16[512,512]{1,0:T(8,128)(2,1)} %pad_maximum_fusion.3), channel_id=1, source_target_pairs={{0,48},{1,49},{64,112},{65,113},{2,50},{3,51},{66,114},{67,115},{1... | collective-permute-start | bytes 1572872 | tf_op jit(solution)/shard_map/ppermute | solution.py:39
  144.1 22.0 %all-to-all-start.1 = ((bf16[128,4,512]{2,1,0:T(4,128)(2,1)}), bf16[128,4,512]{2,1,0:T(4,128)(2,1)S(1)}, u32[]{:S(2)}, u32[]{:S(2)}) async-start(bf16[128,4,512]{2,1,0:T(4,128)(2,1)} %broadcast_in_dim.2), calls=%async_computation.1 | async-start | bytes 1048576 | tf_op jit(solution)/shard_map/all_to_all | solution.py:256
  155.6 16.7 %collective-permute-start.13 = (bf16[512,512]{1,0:T(8,128)(2,1)}, bf16[512,512]{1,0:T(8,128)(2,1)}, u32[]{:S(2)}, u32[]{:S(2)}) collective-permute-start(bf16[512,512]{1,0:T(8,128)(2,1)} %pad_maximum_fusion), channel_id=1, source_target_pairs={{0,4},{1,5},{64,68},{65,69},{2,6},{3,7},{66,70},{67,71},{16,20},{1... | collective-permute-start | bytes 1572872 | tf_op jit(solution)/shard_map/ppermute | solution.py:39
  157.8 14.4 %collective-permute-start.15 = (bf16[512,512]{1,0:T(8,128)(2,1)}, bf16[512,512]{1,0:T(8,128)(2,1)}, u32[]{:S(2)}, u32[]{:S(2)}) collective-permute-start(bf16[512,512]{1,0:T(8,128)(2,1)} %pad_maximum_fusion.1), channel_id=1, source_target_pairs={{0,12},{1,13},{64,76},{65,77},{2,14},{3,15},{66,78},{67,79},{16,28... | collective-permute-start | bytes 1572872 | tf_op jit(solution)/shard_map/ppermute | solution.py:39
  160.2 16.4 %collective-permute-start.21 = (bf16[256,512]{1,0:T(8,128)(2,1)S(1)}, bf16[256,512]{1,0:T(8,128)(2,1)}, u32[]{:S(2)}, u32[]{:S(2)}) collective-permute-start(bf16[256,512]{1,0:T(8,128)(2,1)S(1)} %add_convert_fusion.2), channel_id=1, source_target_pairs={{0,64},{1,65},{64,0},{65,1},{2,66},{3,67},{66,2},{67,3},{16,80},{1... | collective-permute-start | bytes 786440 | tf_op jit(solution)/shard_map/ppermute | solution.py:39
  173.4 9.0 %collective-permute-start.16 = (bf16[256,512]{1,0:T(8,128)(2,1)S(1)}, bf16[256,512]{1,0:T(8,128)(2,1)S(1)}, u32[]{:S(2)}, u32[]{:S(2)}) collective-permute-start(bf16[256,512]{1,0:T(8,128)(2,1)S(1)} %add_convert_fusion.6), channel_id=1, source_target_pairs={{0,2},{1,3},{64,66},{65,67},{2,0},{3,1},{66,64},{67,65},{16,18},{1... | collective-permute-start | bytes 786440 | tf_op jit(solution)/shard_map/ppermute | solution.py:39

commit v2 on v0

v2 whole, which is shorter than its diff:
```python
import functools

import jax
import jax.numpy as jnp
from jax import lax
from jax.experimental import pallas as pl
from jax.experimental.pallas import tpu as pltpu
from jax.sharding import PartitionSpec as P

TILE = 128
SPAN = 256
FEAT = 512
PER_ROW = 6
SLOTS = 192
CHUNK = 6
STEP = 4
WIDE = 384
PART = 64
HALF_ROWS = 8 * SPAN
BF16 = jnp.bfloat16
F32 = jnp.float32
SMEM = pl.BlockSpec(memory_space=pltpu.SMEM)
VMEM = pl.BlockSpec(memory_space=pltpu.VMEM)
DISTANCE = (0, 3, 1, 2)


def flat(x, y, z, core):
    return ((z % 2) * 4 + y % 4) * 16 + (x % 4) * 4 + (z // 2) * 2 + core


def permute(value, step):
    pairs = [
        (flat(x, y, z, c), flat(*step(x, y, z, c)))
        for x in range(4)
        for y in range(4)
        for z in range(4)
        for c in range(2)
    ]
    return lax.ppermute(value, ("row", "col"), pairs)


def to_core(x, y, z, c):
    return x, y, z, 1 - c


def ring(k):
    return lambda x, y, z, c: (x, y + k, z, c) if c == 0 else (x + k, y, z, c)


def to_z(x, y, z, c):
    return x, y, z ^ (1 if c == 0 else 2), c


def cross_ring(k):
    return lambda x, y, z, c: (x + k, y, z, c) if c == 0 else (x, y + k, z, c)


def along_z(k):
    return lambda x, y, z, c: (x, y, (z + k) % 4, c)


def rows(first, count):
    return pl.ds(pl.multiple_of(first, count), count)


def block(i):
    return rows(i * TILE, TILE)


def ring_place(distance):
    return jnp.where(distance == 0, 0, jnp.where(distance == 3, 1, distance + 1))


def coordinates():
    row, col = lax.axis_index("row"), lax.axis_index("col")
    return col // 4, row % 4, row // 4, (col // 2) % 2, col % 2


def part_at(place):
    near, far = coordinates()[2:4]
    return (far * 2 + near + DISTANCE[place]) % 4


def lists_kernel(coords, count, lists):
    my_x, my_y, my_near, my_far, my_core = coordinates()
    live = count[0, 0]
    sublane = lax.broadcasted_iota(jnp.int32, (SLOTS, SLOTS), 0)
    lane = lax.broadcasted_iota(jnp.int32, (SLOTS, SLOTS), 1)
    wide = lax.broadcasted_iota(jnp.int32, (SLOTS, WIDE), 1)
    same = sublane == lane

    def picked(mask, value):
        return jnp.where(mask, value, 0.0)

    def column(line):
        return jnp.sum(picked(same, line.astype(F32)), axis=1, keepdims=True).astype(jnp.int32)

    row_line, col_line = coords[0:1, :], coords[1:2, :]
    a, b = column(row_line), column(col_line)
    a_owner, b_owner = a >> 1, b >> 1
    a_place = (1 - (((a_owner >> 1) & 1) ^ my_far)) * 4 + ring_place(((a_owner >> 2) - my_x) & 3)
    b_place = (1 - ((b_owner >> 2) ^ my_near)) * 4 + ring_place(((b_owner & 3) - my_y) & 3)
    a_from, b_from = a_place ^ 4, b_place ^ 4
    a_tile = a_place * 4 + (a_owner & 1) * 2 + (a & 1)
    b_tile = b_place * 2 + (b & 1)
    a_source = a_from * 4 + (a_owner & 1) * 2 + (a & 1) + (1 - my_core) * 32
    b_source = b_from * 4 + my_core * 2 + (b & 1) + my_core * 32
    slot = sublane[:, 0:1]
    is_live = slot < live

    row_rank = jnp.sum(picked((a == row_line) & (lane < sublane), 1.0), axis=1, keepdims=True).astype(jnp.int32)
    at_row = wide == a_tile * PER_ROW + row_rank
    named = jnp.where(is_live, slot, -1).astype(F32)
    lists[0:1, :] = jnp.sum(picked(at_row, named), axis=0, keepdims=True).astype(jnp.int32)
    lists[1:2, :] = jnp.sum(picked(at_row, b_source.astype(F32)), axis=0, keepdims=True).astype(jnp.int32)

    earlier = (b == col_line) & (lane < sublane) & (lane < live)
    col_rank = jnp.sum(picked(earlier, 1.0), axis=1, keepdims=True).astype(jnp.int32)
    filled = jnp.sum(picked((b_tile == wide) & is_live, 1.0), axis=0, keepdims=True).astype(jnp.int32)
    chunks = ((filled + (CHUNK - 1)) * 43) >> 8
    used = jnp.sum(chunks.astype(F32), axis=1, keepdims=True).astype(jnp.int32)
    base = jnp.sum(picked(wide < b_tile, chunks.astype(F32)), axis=1, keepdims=True).astype(jnp.int32)
    which = (col_rank * 43) >> 8
    chunk = base + which
    place = col_rank - which * CHUNK
    at_chunk = (wide == chunk * CHUNK + place) & is_live
    opens = (wide == chunk) & is_live & (place == 0)
    lists[2:3, :] = jnp.sum(picked(at_chunk, (slot + 1).astype(F32)), axis=0, keepdims=True).astype(jnp.int32) - 1
    lists[3:4, :] = jnp.sum(picked(at_chunk, a_source.astype(F32)), axis=0, keepdims=True).astype(jnp.int32)
    lists[4:5, :] = jnp.sum(picked(opens, b_tile.astype(F32)), axis=0, keepdims=True).astype(jnp.int32)
    lists[5:6, :] = jnp.broadcast_to((used + (STEP - 1)) >> 2, (1, WIDE))
    lists[6:8, :] = jnp.zeros((2, WIDE), jnp.int32)


def make_lists(coords, count):
    return pl.pallas_call(
        lists_kernel,
        out_shape=jax.ShapeDtypeStruct((8, WIDE), jnp.int32),
        in_specs=[VMEM, SMEM],
        out_specs=VMEM,
        compiler_params=pltpu.CompilerParams(vmem_limit_bytes=12 * 2**20),
    )(coords, count)


def live_tile(values, slot):
    tile = values[jnp.maximum(slot, 0)]
    return tile * jnp.where(slot >= 0, 1.0, 0.0).astype(BF16)


def backward_kernel(lists, values, panels, far, near, term_keep, term_send, total, whole, term):
    core = coordinates()[4]
    total[...] = jnp.zeros_like(total)

    def chunk_step(q, carry):
        products = []
        for k in range(STEP):
            first = (q * STEP + k) * CHUNK
            tiles = [live_tile(values, lists[2, first + i]) for i in range(CHUNK)]
            source = [panels[block(lists[3, first + i]), :] for i in range(CHUNK)]
            products.append(
                lax.dot_general(
                    jnp.concatenate(tiles, axis=0),
                    jnp.concatenate(source, axis=0),
                    (((0,), (0,)), ((), ())),
                    preferred_element_type=F32,
                )
            )
        for k in range(STEP):
            total[block(lists[4, q * STEP + k]), :] += products[k]
        return carry

    lax.fori_loop(0, lists[5, 0], chunk_step, 0)
    whole[...] = total[...].astype(BF16)
    for half, target in ((0, far), (1, near)):
        for q in range(4):
            from_here = (half * 4 + q) * SPAN
            target[rows(q * 2 * SPAN + core * SPAN, SPAN), :] = whole[from_here : from_here + SPAN, :]
            target[rows(q * 2 * SPAN + (1 - core) * SPAN, SPAN), :] = jnp.zeros((SPAN, FEAT), BF16)
    start = core * 16 * SPAN + core * SPAN
    feats = jnp.concatenate([panels[rows(start + (q ^ 4) * 2 * SPAN, SPAN), :] for q in range(8)], axis=0)
    term[...] = lax.dot_general(
        feats, whole[...], (((0,), (0,)), ((), ())), preferred_element_type=F32
    ).astype(BF16)
    for place in range(4):
        for target, side in ((term_keep, core), (term_send, 1 - core)):
            first = side * SPAN + part_at(place) * PART
            target[place * PART : (place + 1) * PART, :] = term[rows(first, PART), :]


def forward_kernel(half, lists, values, panels, back, keep, send):
    core = coordinates()[4]

    def row_step(q, carry):
        products = []
        for k in range(STEP):
            first = (half * 16 + q * STEP + k) * PER_ROW
            tiles = [live_tile(values, lists[0, first + i]) for i in range(PER_ROW)]
            source = [panels[block(lists[1, first + i]), :] for i in range(PER_ROW)]
            products.append(
                jnp.dot(
                    jnp.concatenate(tiles, axis=1), jnp.concatenate(source, axis=0), preferred_element_type=F32
                ).astype(BF16)
            )
        here = rows(q * STEP * TILE, STEP * TILE)

        @pl.when(core == half)
        def _():
            send[here, :] = jnp.concatenate(products, axis=0)
            keep[here, :] = back[here, :]

        @pl.when(core == 1 - half)
        def _():
            keep[here, :] = jnp.concatenate(products, axis=0)
            send[here, :] = back[here, :]

        return carry

    lax.fori_loop(0, 16 // STEP, row_step, 0)


def shape(n, dtype=BF16):
    return jax.ShapeDtypeStruct((n, FEAT), dtype)


def backward_sums(lists, values, panels):
    return pl.pallas_call(
        backward_kernel,
        out_shape=(shape(HALF_ROWS), shape(HALF_ROWS), shape(SPAN), shape(SPAN)),
        in_specs=[SMEM, VMEM, VMEM],
        out_specs=[VMEM] * 4,
        scratch_shapes=[
            pltpu.VMEM((8 * SPAN, FEAT), F32),
            pltpu.VMEM((8 * SPAN, FEAT), BF16),
            pltpu.VMEM((FEAT, FEAT), BF16),
        ],
        compiler_params=pltpu.CompilerParams(vmem_limit_bytes=12 * 2**20),
    )(lists, values, panels)


def forward_sums(half, lists, values, panels, back):
    return pl.pallas_call(
        functools.partial(forward_kernel, half),
        out_shape=(shape(HALF_ROWS), shape(HALF_ROWS)),
        in_specs=[SMEM, VMEM, VMEM, VMEM],
        out_specs=[VMEM] * 2,
        compiler_params=pltpu.CompilerParams(vmem_limit_bytes=8 * 2**20),
    )(lists, values, panels, back)


def finish_kernel(final, got, weight, output, grad):
    core = coordinates()[4]

    def both(summed, agg):
        output[...] = jnp.dot(summed, weight[...], preferred_element_type=F32).astype(BF16)
        grad[...] = lax.dot_general(
            agg, weight[...], (((1,), (1,)), ((), ())), preferred_element_type=F32
        ).astype(BF16)

    @pl.when(core == 0)
    def _():
        both(final[0:SPAN, :], got[...])

    @pl.when(core == 1)
    def _():
        both(got[...], final[SPAN : 2 * SPAN, :])


def finish(final, got, weight):
    return pl.pallas_call(
        finish_kernel,
        out_shape=(shape(SPAN), shape(SPAN)),
        in_specs=[VMEM] * 3,
        out_specs=(VMEM, VMEM),
        compiler_params=pltpu.CompilerParams(vmem_limit_bytes=8 * 2**20),
    )(final, got, weight)


def place_kernel(scale, mine, other, grad):
    core = coordinates()[4]
    for place in range(4):
        for source, side in ((mine, core), (other, 1 - core)):
            first = side * SPAN + part_at(place) * PART
            grad[rows(first, PART), :] = source[place * PART : (place + 1) * PART, :].astype(F32) * scale


def place_parts(scale, mine, other):
    return pl.pallas_call(
        functools.partial(place_kernel, scale),
        out_shape=shape(FEAT, F32),
        in_specs=[VMEM, VMEM],
        out_specs=VMEM,
        compiler_params=pltpu.CompilerParams(vmem_limit_bytes=8 * 2**20),
    )(mine, other)


def stack(*parts):
    return jnp.concatenate(parts, axis=0)


def add(*parts):
    total = parts[0].astype(F32)
    for part in parts[1:]:
        total = total + part.astype(F32)
    return total.astype(BF16)


def ring_gather(own, step):
    opposite = permute(own, step(2))
    return own, permute(own, step(1)), permute(own, step(-1)), opposite


def ring_sum(pieces, step):
    own, before, after, opposite = pieces
    opposite = permute(opposite, step(2))
    return own, permute(after, step(1)), permute(before, step(-1)), opposite


def split(whole, size):
    return [whole[i * size : (i + 1) * size] for i in range(4)]


def per_device(features, weight, cotangent, tile_coords, tile_values, tile_count):
    values = tile_values[0, 0]
    lists = make_lists(jnp.transpose(tile_coords[0, 0]), tile_count)
    first = lax.axis_index("col") % 2 == 0
    other_features, other_cotangent = permute(features, to_core), permute(cotangent, to_core)
    own = jnp.where(first, stack(features, other_features), stack(other_cotangent, cotangent))
    from_z = permute(own, to_z)
    near = list(ring_gather(own, ring))
    from_z, *near, lists = lax.optimization_barrier((from_z, *near, lists))
    near = stack(*near, from_z)
    other_near = permute(near, to_core)
    far = stack(*ring_gather(from_z, ring)[1:])
    far, other_near = lax.optimization_barrier((far, other_near))
    panels = stack(near, far, other_near, permute(far, to_core))

    back_far, back_near, term_keep, term_send = backward_sums(lists, values, panels)
    part = add(term_keep, permute(term_send, to_core))
    part, back_far = lax.optimization_barrier((part, back_far))
    keep_far, send_far = forward_sums(0, lists, values, panels, back_far)
    sum_far = add(keep_far, permute(send_far, to_core))
    part = add(*ring_sum(split(part, PART), along_z))
    keep_near, send_near = forward_sums(1, lists, values, panels, back_near)
    sum_near = add(keep_near, permute(send_near, to_core))
    far = [stack(piece, part) for piece in split(sum_far, 2 * SPAN)]
    far = add(*ring_sum(far, ring))
    far, part = far[: 2 * SPAN], far[2 * SPAN :]
    near = add(*ring_sum([stack(piece, part) for piece in split(sum_near, 2 * SPAN)], cross_ring))
    near, part = near[: 2 * SPAN], near[2 * SPAN :]
    passed = permute(permute(far, to_z), to_core)
    mine = stack(*ring_gather(part, along_z))
    other = permute(mine, to_core)
    final = add(near, passed)
    got = permute(jnp.where(first, final[SPAN:], final[:SPAN]), to_core)
    output, features_grad = finish(final, got, weight)
    nodes = lax.axis_size("row") * lax.axis_size("col") * SPAN
    weight_grad = place_parts(nodes ** (-0.5), mine, other)
    return output, features_grad, weight_grad


def solution(mesh):
    return jax.shard_map(
        per_device,
        mesh=mesh,
        in_specs=(
            P(("row", "col"), None),
            P(),
            P(("row", "col"), None),
            P("row", "col", None, None),
            P("row", "col", None, None, None),
            P("row", "col"),
        ),
        out_specs=(P(("row", "col"), None), P(("row", "col"), None), P()),
        check_vma=False,
    )
```

time: 595 us -> 122 us (0.21)
  matrix products: 336 us -> 0 us
  waiting for transfers between devices: 208 us -> 59 us
  starting transfers between devices: 0.2 us -> 39.8 us
  local copies, waits for them, and re-layouts: 22 us -> 1.8 us
  Pallas kernels: 0 us -> 15.7 us
  between operations: 13.8 us -> 1.57 us
  other arithmetic: 13.2 us -> 3.76 us
    dot_general x51 -> x0, matrix products: 336 us -> none  [the longest x12 140 us: add_group(): jnp.einsum('sk,sif->kif', dst_onehot, upper, preferred_element_type=jnp.f...]
    reduce_scatter x2 -> x0, waiting for transfers between devices: 113 us -> none  [the longest x1 78.5 us: per_device(): lax.psum_scatter(partial_value.reshape(row_tiles * TILE, width).astype(jn...]
    all_gather x2 -> x0, waiting for transfers between devices: 94 us -> none  [the longest x1 53.5 us: per_device(): cot_panel = lax.all_gather(cotangent, 'col', axis=0, tiled=True)]
    ppermute x0 -> x30, waiting for transfers between devices: none -> 59 us  [permute(): return lax.ppermute(value, ('row', 'col'), pairs)]
    ppermute x0 -> x30, starting transfers between devices: none -> 39.8 us  [permute(): return lax.ppermute(value, ('row', 'col'), pairs)]
    pallas_call x0 -> x6, Pallas kernels: none -> 15.7 us  [the longest x2 7.02 us: forward_sums(): pl.pallas_call(functools.partial(forward_kernel, half), out_shape=(shape(...]
    unnamed x10 -> x14, local copies, waits for them, and re-layouts: 10.9 us -> 1.28 us
    lt x12 -> x0, other arithmetic: 7.8 us -> none  [add_group(): live = start + jnp.arange(slot_group, dtype=jnp.int32) < count]
  transfers between devices with their start and end apart: 5 -> 30, of which waited for: 4 -> 17; matrix products, arithmetic and copies ran while one was open for 35% -> 2% of each run, Pallas kernels for 0% -> 4%
where the time goes in v2:
time: 122 us
  waiting for transfers between devices  59 us (48%)
  starting transfers between devices  39.8 us (33%)
  Pallas kernels  15.7 us (13%)
  other arithmetic  3.76 us (3%)
  local copies, waits for them, and re-layouts  1.8 us (1%)
  between operations  1.57 us (1%)
    ppermute x30, waiting for transfers between devices, permute(): return lax.ppermute(value, ('row', 'col'), pairs)  59 us
    ppermute x30, starting transfers between devices, permute(): return lax.ppermute(value, ('row', 'col'), pairs)  39.8 us
    pallas_call x2, Pallas kernels, forward_sums(): pl.pallas_call(functools.partial(forward_kernel, half), out_shape=(shape(...  7.02 us
    pallas_call x1, Pallas kernels, backward_sums(): pl.pallas_call(backward_kernel, out_shape=(shape(HALF_ROWS), shape(HALF_R...  5.79 us
  transfers between devices with their start and end apart: 30, of which 17 were waited for; matrix products, arithmetic and copies ran while one was open for 2% of the time, Pallas kernels for 4%

profile of v2, /device:TPU:1, one launch (start us, length us, event | category | flops | bytes accessed | tf_op | source)
XLA Modules:
  0.0 121.7 jit_solution(11816413466777937771)
XLA Ops:
  0.6 1.5 %collective-permute-start = (bf16[256,512]{1,0:T(8,128)(2,1)}, bf16[256,512]{1,0:T(8,128)(2,1)S(1)}, u32[]{:S(2)}, u32[]{:S(2)}) collective-permute-start(bf16[256,512]{1,0:T(8,128)(2,1)} %param.6), channel_id=1, source_target_pairs={{0,1},{1,0},{64,65},{65,64},{2,3},{3,2},{66,67},{67,66},{16,17},{1... | collective-permute-start | bytes 786440 | tf_op jit(solution)/shard_map/ppermute | solution.py:39
  2.2 1.3 %collective-permute-done = bf16[256,512]{1,0:T(8,128)(2,1)S(1)} collective-permute-done((bf16[256,512]{1,0:T(8,128)(2,1)}, bf16[256,512]{1,0:T(8,128)(2,1)S(1)}, u32[]{:S(2)}, u32[]{:S(2)}) %collective-permute-start) | collective-permute-done | bytes 262176 | tf_op jit(solution)/shard_map/ppermute | solution.py:39
  3.9 1.2 maximum_select_fusion
  5.0 3.8 %collective-permute-start.2 = (bf16[512,512]{1,0:T(8,128)(2,1)S(1)}, bf16[512,512]{1,0:T(8,128)(2,1)S(1)}, u32[]{:S(2)}, u32[]{:S(2)}) collective-permute-start(bf16[512,512]{1,0:T(8,128)(2,1)S(1)} %maximum_select_fusion), channel_id=1, source_target_pairs={{0,64},{1,3},{64,0},{65,67},{2,66},{3,1},{66,2},{67,65},{16,80},{1... | collective-permute-start | bytes 1572872 | tf_op jit(solution)/shard_map/ppermute | solution.py:39
  8.8 1.2 collective-permute-start.3
  10.0 1.5 %collective-permute-start.4 = (bf16[512,512]{1,0:T(8,128)(2,1)S(1)}, bf16[512,512]{1,0:T(8,128)(2,1)S(1)}, u32[]{:S(2)}, u32[]{:S(2)}) collective-permute-start(bf16[512,512]{1,0:T(8,128)(2,1)S(1)} %maximum_select_fusion), channel_id=1, source_target_pairs={{0,48},{1,13},{64,112},{65,77},{2,50},{3,15},{66,114},{67,79},{16,... | collective-permute-start | bytes 1572872 | tf_op jit(solution)/shard_map/ppermute | solution.py:39
  11.5 1.5 %collective-permute-start.5 = (bf16[512,512]{1,0:T(8,128)(2,1)S(1)}, bf16[512,512]{1,0:T(8,128)(2,1)S(1)}, u32[]{:S(2)}, u32[]{:S(2)}) collective-permute-start(bf16[512,512]{1,0:T(8,128)(2,1)S(1)} %maximum_select_fusion), channel_id=1, source_target_pairs={{0,32},{1,9},{64,96},{65,73},{2,34},{3,11},{66,98},{67,75},{16,48}... | collective-permute-start | bytes 1572872 | tf_op jit(solution)/shard_map/ppermute | solution.py:39
  13.7 0.7 copy-done.1
  14.4 0.6 shard_map.85.lists
  15.0 4.4 %collective-permute-done.2 = bf16[512,512]{1,0:T(8,128)(2,1)S(1)} collective-permute-done((bf16[512,512]{1,0:T(8,128)(2,1)S(1)}, bf16[512,512]{1,0:T(8,128)(2,1)S(1)}, u32[]{:S(2)}, u32[]{:S(2)}) %collective-permute-start.2) | collective-permute-done | bytes 524320 | tf_op jit(solution)/shard_map/ppermute | solution.py:39
  19.4 5.2 %collective-permute-done.5 = bf16[512,512]{1,0:T(8,128)(2,1)S(1)} collective-permute-done((bf16[512,512]{1,0:T(8,128)(2,1)S(1)}, bf16[512,512]{1,0:T(8,128)(2,1)S(1)}, u32[]{:S(2)}, u32[]{:S(2)}) %collective-permute-start.5) | collective-permute-done | bytes 524320 | tf_op jit(solution)/shard_map/ppermute | solution.py:39
  25.3 1.2 collective-permute-start.6
  26.5 1.5 %collective-permute-start.7 = (bf16[512,512]{1,0:T(8,128)(2,1)S(1)}, bf16[512,512]{1,0:T(8,128)(2,1)S(1)}, u32[]{:S(2)}, u32[]{:S(2)}) collective-permute-start(bf16[512,512]{1,0:T(8,128)(2,1)S(1)} %collective-permute-done.2), channel_id=1, source_target_pairs={{0,48},{1,13},{64,112},{65,77},{2,50},{3,15},{66,114},{67,79},{16,... | collective-permute-start | bytes 1572872 | tf_op jit(solution)/shard_map/ppermute | solution.py:39
  27.9 1.5 %collective-permute-start.8 = (bf16[512,512]{1,0:T(8,128)(2,1)S(1)}, bf16[512,512]{1,0:T(8,128)(2,1)S(1)}, u32[]{:S(2)}, u32[]{:S(2)}) collective-permute-start(bf16[512,512]{1,0:T(8,128)(2,1)S(1)} %collective-permute-done.2), channel_id=1, source_target_pairs={{0,32},{1,9},{64,96},{65,73},{2,34},{3,11},{66,98},{67,75},{16,48}... | collective-permute-start | bytes 1572872 | tf_op jit(solution)/shard_map/ppermute | solution.py:39
  29.5 5.3 %collective-permute-done.6 = bf16[512,512]{1,0:T(8,128)(2,1)S(1)} collective-permute-done((bf16[512,512]{1,0:T(8,128)(2,1)S(1)}, bf16[512,512]{1,0:T(8,128)(2,1)S(1)}, u32[]{:S(2)}, u32[]{:S(2)}) %collective-permute-start.6) | collective-permute-done | bytes 524320 | tf_op jit(solution)/shard_map/ppermute | solution.py:39
  34.8 6.6 %collective-permute-done.8 = bf16[512,512]{1,0:T(8,128)(2,1)S(1)} collective-permute-done((bf16[512,512]{1,0:T(8,128)(2,1)S(1)}, bf16[512,512]{1,0:T(8,128)(2,1)S(1)}, u32[]{:S(2)}, u32[]{:S(2)}) %collective-permute-start.8) | collective-permute-done | bytes 524320 | tf_op jit(solution)/shard_map/ppermute | solution.py:39
  41.5 1.6 %collective-permute-start.10 = (bf16[1536,512]{1,0:T(8,128)(2,1)S(1)}, bf16[1536,512]{1,0:T(8,128)(2,1)S(1)}, u32[]{:S(2)}, u32[]{:S(2)}) collective-permute-start(bf16[1536,512]{1,0:T(8,128)(2,1)S(1)} %pad_maximum_fusion), channel_id=1, source_target_pairs={{0,1},{1,0},{64,65},{65,64},{2,3},{3,2},{66,67},{67,66},{16,17},{1... | collective-permute-start | bytes 4718600 | tf_op jit(solution)/shard_map/ppermute | solution.py:39
  43.4 2.7 %collective-permute-done.10 = bf16[1536,512]{1,0:T(8,128)(2,1)S(1)} collective-permute-done((bf16[1536,512]{1,0:T(8,128)(2,1)S(1)}, bf16[1536,512]{1,0:T(8,128)(2,1)S(1)}, u32[]{:S(2)}, u32[]{:S(2)}) %collective-permute-start.10) | collective-permute-done | bytes 1572896 | tf_op jit(solution)/shard_map/ppermute | solution.py:39
  46.3 5.8 %shard_map.86 = (bf16[2048,512]{1,0:T(8,128)(2,1)S(1)}, bf16[2048,512]{1,0:T(8,128)(2,1)S(1)}, bf16[256,512]{1,0:T(8,128)(2,1)S(1)}, bf16[256,512]{1,0:T(8,128)(2,1)S(1)}) custom-call(s32[8,384]{1,0:T(8,128)S(1)} %shard_map.85.lists, bf16[192,128,128]{2,1,0:T(8,128)(2,1)S(1)} %bitcast.6, bf16[8192,512]{1,0:T(8,128)(2,1)S(1)} %constant_dynamic-update-slice_fusion.5.panels), custom_call_target="tpu_custom_call" | custom-call | tf_op jit(solution)/shard_map/pallas_call | solution.py:226
  52.2 1.5 %collective-permute-done.12 = bf16[256,512]{1,0:T(8,128)(2,1)S(1)} collective-permute-done((bf16[256,512]{1,0:T(8,128)(2,1)S(1)}, bf16[256,512]{1,0:T(8,128)(2,1)S(1)}, u32[]{:S(2)}, u32[]{:S(2)}) %collective-permute-start.12) | collective-permute-done | bytes 262176 | tf_op jit(solution)/shard_map/ppermute | solution.py:39
  53.8 3.5 %shard_map.88 = (bf16[2048,512]{1,0:T(8,128)(2,1)S(1)}, bf16[2048,512]{1,0:T(8,128)(2,1)S(1)}) custom-call(s32[8,384]{1,0:T(8,128)S(1)} %shard_map.85.lists, bf16[192,128,128]{2,1,0:T(8,128)(2,1)S(1)} %bitcast.7, bf16[8192,512]{1,0:T(8,128)(2,1)S(1)} %constant_dynamic-update-slice_fusion.5.panels, bf16[2048,512]{1,0:T(8,128)(2,1)S(1)} %get-tuple-element.37.back), custom_call_target="tpu_custom_call" | custom-call | tf_op jit(solution)/shard_map/pallas_call | solution.py:241
  57.5 3.5 %shard_map.87 = (bf16[2048,512]{1,0:T(8,128)(2,1)S(1)}, bf16[2048,512]{1,0:T(8,128)(2,1)S(1)}) custom-call(s32[8,384]{1,0:T(8,128)S(1)} %shard_map.85.lists, bf16[192,128,128]{2,1,0:T(8,128)(2,1)S(1)} %bitcast.8, bf16[8192,512]{1,0:T(8,128)(2,1)S(1)} %constant_dynamic-update-slice_fusion.5.panels, bf16[2048,512]{1,0:T(8,128)(2,1)S(1)} %get-tuple-element.31.back), custom_call_target="tpu_custom_call" | custom-call | tf_op jit(solution)/shard_map/pallas_call | solution.py:241
  61.6 2.6 %collective-permute-start.15 = (bf16[64,512]{1,0:T(8,128)(2,1)S(1)}, bf16[64,512]{1,0:T(8,128)(2,1)S(1)}, u32[]{:S(2)}, u32[]{:S(2)}) collective-permute-start(bf16[64,512]{1,0:T(8,128)(2,1)S(1)} %get-tuple-element.63), channel_id=1, source_target_pairs={{0,66},{1,67},{64,0},{65,1},{2,64},{3,65},{66,2},{67,3},{16,82},{1... | collective-permute-start | bytes 196616 | tf_op jit(solution)/shard_map/ppermute | solution.py:39
  64.2 0.7 collective-permute-start.16
  64.9 1.3 %collective-permute-done.14 = bf16[64,512]{1,0:T(8,128)(2,1)S(1)} collective-permute-done((bf16[64,512]{1,0:T(8,128)(2,1)S(1)}, bf16[64,512]{1,0:T(8,128)(2,1)S(1)}, u32[]{:S(2)}, u32[]{:S(2)}) %collective-permute-start.14) | collective-permute-done | bytes 65568 | tf_op jit(solution)/shard_map/ppermute | solution.py:39
  66.2 2.6 %collective-permute-done.16 = bf16[64,512]{1,0:T(8,128)(2,1)S(1)} collective-permute-done((bf16[64,512]{1,0:T(8,128)(2,1)S(1)}, bf16[64,512]{1,0:T(8,128)(2,1)S(1)}, u32[]{:S(2)}, u32[]{:S(2)}) %collective-permute-start.16) | collective-permute-done | bytes 65568 | tf_op jit(solution)/shard_map/ppermute | solution.py:39
  68.9 0.6 add_convert_fusion
  69.8 0.9 collective-permute-start.17
  70.7 1.8 %collective-permute-start.18 = (bf16[576,512]{1,0:T(8,128)(2,1)S(1)}, bf16[576,512]{1,0:T(8,128)(2,1)S(1)}, u32[]{:S(2)}, u32[]{:S(2)}) collective-permute-start(bf16[576,512]{1,0:T(8,128)(2,1)S(1)} %get-tuple-element.68), channel_id=1, source_target_pairs={{0,48},{1,13},{64,112},{65,77},{2,50},{3,15},{66,114},{67,79},{16,... | collective-permute-start | bytes 1769480 | tf_op jit(solution)/shard_map/ppermute | solution.py:39
  72.7 0.7 add_convert_fusion.1
  73.6 6.5 %collective-permute-done.17 = bf16[576,512]{1,0:T(8,128)(2,1)S(1)} collective-permute-done((bf16[576,512]{1,0:T(8,128)(2,1)S(1)}, bf16[576,512]{1,0:T(8,128)(2,1)S(1)}, u32[]{:S(2)}, u32[]{:S(2)}) %collective-permute-start.17) | collective-permute-done | bytes 589856 | tf_op jit(solution)/shard_map/ppermute | solution.py:39
  80.1 5.6 %collective-permute-done.18 = bf16[576,512]{1,0:T(8,128)(2,1)S(1)} collective-permute-done((bf16[576,512]{1,0:T(8,128)(2,1)S(1)}, bf16[576,512]{1,0:T(8,128)(2,1)S(1)}, u32[]{:S(2)}, u32[]{:S(2)}) %collective-permute-start.18) | collective-permute-done | bytes 589856 | tf_op jit(solution)/shard_map/ppermute | solution.py:39
  85.7 0.9 collective-permute-done.19
  87.1 0.7 collective-permute-start.20
  87.7 2.6 %collective-permute-start.21 = (bf16[576,512]{1,0:T(8,128)(2,1)S(1)}, bf16[576,512]{1,0:T(8,128)(2,1)S(1)}, u32[]{:S(2)}, u32[]{:S(2)}) collective-permute-start(bf16[576,512]{1,0:T(8,128)(2,1)S(1)} %get-tuple-element.65), channel_id=1, source_target_pairs={{0,12},{1,49},{64,76},{65,113},{2,14},{3,51},{66,78},{67,115},{16,... | collective-permute-start | bytes 1769480 | tf_op jit(solution)/shard_map/ppermute | solution.py:39
  90.4 1.1 collective-permute-start.22
  91.5 1.9 %collective-permute-start.23 = (bf16[512,512]{1,0:T(8,128)(2,1)S(1)}, bf16[512,512]{1,0:T(8,128)(2,1)S(1)}, u32[]{:S(2)}, u32[]{:S(2)}) collective-permute-start(bf16[512,512]{1,0:T(8,128)(2,1)S(1)} %slice.82), channel_id=1, source_target_pairs={{0,64},{1,3},{64,0},{65,67},{2,66},{3,1},{66,2},{67,65},{16,80},{1... | collective-permute-start | bytes 1572872 | tf_op jit(solution)/shard_map/ppermute | solution.py:39
  93.5 9.7 %collective-permute-done.23 = bf16[512,512]{1,0:T(8,128)(2,1)S(1)} collective-permute-done((bf16[512,512]{1,0:T(8,128)(2,1)S(1)}, bf16[512,512]{1,0:T(8,128)(2,1)S(1)}, u32[]{:S(2)}, u32[]{:S(2)}) %collective-permute-start.23) | collective-permute-done | bytes 524320 | tf_op jit(solution)/shard_map/ppermute | solution.py:39
  103.2 3.6 %collective-permute-start.24 = (bf16[512,512]{1,0:T(8,128)(2,1)S(1)}, bf16[512,512]{1,0:T(8,128)(2,1)S(1)}, u32[]{:S(2)}, u32[]{:S(2)}) collective-permute-start(bf16[512,512]{1,0:T(8,128)(2,1)S(1)} %collective-permute-done.23), channel_id=1, source_target_pairs={{0,1},{1,0},{64,65},{65,64},{2,3},{3,2},{66,67},{67,66},{16,17},{1... | collective-permute-start | bytes 1572872 | tf_op jit(solution)/shard_map/ppermute | solution.py:39
  107.2 1.1 collective-permute-start.26
  108.2 1.7 %collective-permute-start.27 = (bf16[64,512]{1,0:T(8,128)(2,1)S(1)}, bf16[64,512]{1,0:T(8,128)(2,1)S(1)}, u32[]{:S(2)}, u32[]{:S(2)}) collective-permute-start(bf16[64,512]{1,0:T(8,128)(2,1)S(1)} %slice.85), channel_id=1, source_target_pairs={{0,66},{1,67},{64,0},{65,1},{2,64},{3,65},{66,2},{67,3},{16,82},{1... | collective-permute-start | bytes 196616 | tf_op jit(solution)/shard_map/ppermute | solution.py:39
  109.9 1.2 collective-permute-start.28
  111.1 0.4 collective-permute-done.26
  111.6 3.6 %collective-permute-done.28 = bf16[64,512]{1,0:T(8,128)(2,1)S(1)} collective-permute-done((bf16[64,512]{1,0:T(8,128)(2,1)S(1)}, bf16[64,512]{1,0:T(8,128)(2,1)S(1)}, u32[]{:S(2)}, u32[]{:S(2)}) %collective-permute-start.28) | collective-permute-done | bytes 65568 | tf_op jit(solution)/shard_map/ppermute | solution.py:39
  115.2 3.0 %collective-permute-start.29 = (bf16[256,512]{1,0:T(8,128)(2,1)S(1)}, bf16[256,512]{1,0:T(8,128)(2,1)S(1)}, u32[]{:S(2)}, u32[]{:S(2)}) collective-permute-start(bf16[256,512]{1,0:T(8,128)(2,1)S(1)} %pad_maximum_fusion.9.mine), channel_id=1, source_target_pairs={{0,1},{1,0},{64,65},{65,64},{2,3},{3,2},{66,67},{67,66},{16,17},{1... | collective-permute-start | bytes 786440 | tf_op jit(solution)/shard_map/ppermute | solution.py:39
  118.5 0.9 collective-permute-done.29.other
  119.4 1.1 shard_map.90
  120.5 1.2 %shard_map.89 = (bf16[256,512]{1,0:T(8,128)(2,1)}, bf16[256,512]{1,0:T(8,128)(2,1)}) custom-call(bf16[512,512]{1,0:T(8,128)(2,1)S(1)} %add_convert_fusion.4.final, bf16[256,512]{1,0:T(8,128)(2,1)S(1)} %collective-permute-done.25.got, bf16[512,512]{1,0:T(8,128)(2,1)S(1)} %copy-done), custom_call_target="tpu_custom_call" | custom-call | tf_op jit(solution)/shard_map/pallas_call | solution.py:269
  (54 shorter events, 4.2 us)
Async XLA Ops:
  0.6 2.9 %collective-permute-start = (bf16[256,512]{1,0:T(8,128)(2,1)}, bf16[256,512]{1,0:T(8,128)(2,1)S(1)}, u32[]{:S(2)}, u32[]{:S(2)}) collective-permute-start(bf16[256,512]{1,0:T(8,128)(2,1)} %param.6), channel_id=1, source_target_pairs={{0,1},{1,0},{64,65},{65,64},{2,3},{3,2},{66,67},{67,66},{16,17},{1... | collective-permute-start | bytes 786440 | tf_op jit(solution)/shard_map/ppermute | solution.py:39
  2.1 1.7 %collective-permute-start.1 = (bf16[256,512]{1,0:T(8,128)(2,1)}, bf16[256,512]{1,0:T(8,128)(2,1)S(1)}, u32[]{:S(2)}, u32[]{:S(2)}) collective-permute-start(bf16[256,512]{1,0:T(8,128)(2,1)} %param.8), channel_id=1, source_target_pairs={{0,1},{1,0},{64,65},{65,64},{2,3},{3,2},{66,67},{67,66},{16,17},{1... | collective-permute-start | bytes 786440 | tf_op jit(solution)/shard_map/ppermute | solution.py:39
  5.0 14.4 %collective-permute-start.2 = (bf16[512,512]{1,0:T(8,128)(2,1)S(1)}, bf16[512,512]{1,0:T(8,128)(2,1)S(1)}, u32[]{:S(2)}, u32[]{:S(2)}) collective-permute-start(bf16[512,512]{1,0:T(8,128)(2,1)S(1)} %maximum_select_fusion), channel_id=1, source_target_pairs={{0,64},{1,3},{64,0},{65,67},{2,66},{3,1},{66,2},{67,65},{16,80},{1... | collective-permute-start | bytes 1572872 | tf_op jit(solution)/shard_map/ppermute | solution.py:39
  8.8 10.6 %collective-permute-start.3 = (bf16[512,512]{1,0:T(8,128)(2,1)S(1)}, bf16[512,512]{1,0:T(8,128)(2,1)S(1)}, u32[]{:S(2)}, u32[]{:S(2)}) collective-permute-start(bf16[512,512]{1,0:T(8,128)(2,1)S(1)} %maximum_select_fusion), channel_id=1, source_target_pairs={{0,16},{1,5},{64,80},{65,69},{2,18},{3,7},{66,82},{67,71},{16,32},... | collective-permute-start | bytes 1572872 | tf_op jit(solution)/shard_map/ppermute | solution.py:39
  10.0 9.4 %collective-permute-start.4 = (bf16[512,512]{1,0:T(8,128)(2,1)S(1)}, bf16[512,512]{1,0:T(8,128)(2,1)S(1)}, u32[]{:S(2)}, u32[]{:S(2)}) collective-permute-start(bf16[512,512]{1,0:T(8,128)(2,1)S(1)} %maximum_select_fusion), channel_id=1, source_target_pairs={{0,48},{1,13},{64,112},{65,77},{2,50},{3,15},{66,114},{67,79},{16,... | collective-permute-start | bytes 1572872 | tf_op jit(solution)/shard_map/ppermute | solution.py:39
  11.5 13.2 %collective-permute-start.5 = (bf16[512,512]{1,0:T(8,128)(2,1)S(1)}, bf16[512,512]{1,0:T(8,128)(2,1)S(1)}, u32[]{:S(2)}, u32[]{:S(2)}) collective-permute-start(bf16[512,512]{1,0:T(8,128)(2,1)S(1)} %maximum_select_fusion), channel_id=1, source_target_pairs={{0,32},{1,9},{64,96},{65,73},{2,34},{3,11},{66,98},{67,75},{16,48}... | collective-permute-start | bytes 1572872 | tf_op jit(solution)/shard_map/ppermute | solution.py:39
  13.7 0.7 copy-start.1
  25.1 16.4 %collective-permute-start.9 = (bf16[2560,512]{1,0:T(8,128)(2,1)S(1)}, bf16[2560,512]{1,0:T(8,128)(2,1)S(1)}, u32[]{:S(2)}, u32[]{:S(2)}) collective-permute-start(bf16[2560,512]{1,0:T(8,128)(2,1)S(1)} %get-tuple-element.51), channel_id=1, source_target_pairs={{0,1},{1,0},{64,65},{65,64},{2,3},{3,2},{66,67},{67,66},{16,17},{1... | collective-permute-start | bytes 7864328 | tf_op jit(solution)/shard_map/ppermute | solution.py:39
  25.3 9.5 %collective-permute-start.6 = (bf16[512,512]{1,0:T(8,128)(2,1)S(1)}, bf16[512,512]{1,0:T(8,128)(2,1)S(1)}, u32[]{:S(2)}, u32[]{:S(2)}) collective-permute-start(bf16[512,512]{1,0:T(8,128)(2,1)S(1)} %collective-permute-done.2), channel_id=1, source_target_pairs={{0,16},{1,5},{64,80},{65,69},{2,18},{3,7},{66,82},{67,71},{16,32},... | collective-permute-start | bytes 1572872 | tf_op jit(solution)/shard_map/ppermute | solution.py:39
  26.5 8.3 %collective-permute-start.7 = (bf16[512,512]{1,0:T(8,128)(2,1)S(1)}, bf16[512,512]{1,0:T(8,128)(2,1)S(1)}, u32[]{:S(2)}, u32[]{:S(2)}) collective-permute-start(bf16[512,512]{1,0:T(8,128)(2,1)S(1)} %collective-permute-done.2), channel_id=1, source_target_pairs={{0,48},{1,13},{64,112},{65,77},{2,50},{3,15},{66,114},{67,79},{16,... | collective-permute-start | bytes 1572872 | tf_op jit(solution)/shard_map/ppermute | solution.py:39
  27.9 13.5 %collective-permute-start.8 = (bf16[512,512]{1,0:T(8,128)(2,1)S(1)}, bf16[512,512]{1,0:T(8,128)(2,1)S(1)}, u32[]{:S(2)}, u32[]{:S(2)}) collective-permute-start(bf16[512,512]{1,0:T(8,128)(2,1)S(1)} %collective-permute-done.2), channel_id=1, source_target_pairs={{0,32},{1,9},{64,96},{65,73},{2,34},{3,11},{66,98},{67,75},{16,48}... | collective-permute-start | bytes 1572872 | tf_op jit(solution)/shard_map/ppermute | solution.py:39
  41.5 4.6 %collective-permute-start.10 = (bf16[1536,512]{1,0:T(8,128)(2,1)S(1)}, bf16[1536,512]{1,0:T(8,128)(2,1)S(1)}, u32[]{:S(2)}, u32[]{:S(2)}) collective-permute-start(bf16[1536,512]{1,0:T(8,128)(2,1)S(1)} %pad_maximum_fusion), channel_id=1, source_target_pairs={{0,1},{1,0},{64,65},{65,64},{2,3},{3,2},{66,67},{67,66},{16,17},{1... | collective-permute-start | bytes 4718600 | tf_op jit(solution)/shard_map/ppermute | solution.py:39
  43.1 3.1 %slice-start = ((s8[6291456]{0:T(1024)(128)(4,1)}), s8[4194304]{0:T(1024)(128)(4,1)S(1)}, s32[]{:S(2)}) async-start(s8[6291456]{0:T(1024)(128)(4,1)} %bitcast.4), calls=%async_computation | async-start | bytes 8388608
  43.2 3.0 %slice-start.1 = ((s8[6291456]{0:T(1024)(128)(4,1)}), s8[2097152]{0:T(1024)(128)(4,1)S(1)}, s32[]{:S(2)}) async-start(s8[6291456]{0:T(1024)(128)(4,1)} %bitcast.4), calls=%async_computation.1 | async-start | bytes 4194304
  52.1 1.6 %collective-permute-start.12 = (bf16[256,512]{1,0:T(8,128)(2,1)S(1)}, bf16[256,512]{1,0:T(8,128)(2,1)S(1)}, u32[]{:S(2)}, u32[]{:S(2)}) collective-permute-start(bf16[256,512]{1,0:T(8,128)(2,1)S(1)} %get-tuple-element.35), channel_id=1, source_target_pairs={{0,1},{1,0},{64,65},{65,64},{2,3},{3,2},{66,67},{67,66},{16,17},{1... | collective-permute-start | bytes 786440 | tf_op jit(solution)/shard_map/ppermute | solution.py:39
  57.3 11.6 %collective-permute-start.13 = (bf16[2048,512]{1,0:T(8,128)(2,1)S(1)}, bf16[2048,512]{1,0:T(8,128)(2,1)S(1)}, u32[]{:S(2)}, u32[]{:S(2)}) collective-permute-start(bf16[2048,512]{1,0:T(8,128)(2,1)S(1)} %get-tuple-element.39), channel_id=1, source_target_pairs={{0,1},{1,0},{64,65},{65,64},{2,3},{3,2},{66,67},{67,66},{16,17},{1... | collective-permute-start | bytes 6291464 | tf_op jit(solution)/shard_map/ppermute | solution.py:39
  61.1 11.7 %collective-permute-start.11 = (bf16[2048,512]{1,0:T(8,128)(2,1)S(1)}, bf16[2048,512]{1,0:T(8,128)(2,1)S(1)}, u32[]{:S(2)}, u32[]{:S(2)}) collective-permute-start(bf16[2048,512]{1,0:T(8,128)(2,1)S(1)} %get-tuple-element.33), channel_id=1, source_target_pairs={{0,1},{1,0},{64,65},{65,64},{2,3},{3,2},{66,67},{67,66},{16,17},{1... | collective-permute-start | bytes 6291464 | tf_op jit(solution)/shard_map/ppermute | solution.py:39
  61.5 4.8 %collective-permute-start.14 = (bf16[64,512]{1,0:T(8,128)(2,1)S(1)}, bf16[64,512]{1,0:T(8,128)(2,1)S(1)}, u32[]{:S(2)}, u32[]{:S(2)}) collective-permute-start(bf16[64,512]{1,0:T(8,128)(2,1)S(1)} %get-tuple-element.61), channel_id=1, source_target_pairs={{0,64},{1,65},{64,2},{65,3},{2,66},{3,67},{66,0},{67,1},{16,80},{1... | collective-permute-start | bytes 196616 | tf_op jit(solution)/shard_map/ppermute | solution.py:39
  61.6 4.7 %collective-permute-start.15 = (bf16[64,512]{1,0:T(8,128)(2,1)S(1)}, bf16[64,512]{1,0:T(8,128)(2,1)S(1)}, u32[]{:S(2)}, u32[]{:S(2)}) collective-permute-start(bf16[64,512]{1,0:T(8,128)(2,1)S(1)} %get-tuple-element.63), channel_id=1, source_target_pairs={{0,66},{1,67},{64,0},{65,1},{2,64},{3,65},{66,2},{67,3},{16,82},{1... | collective-permute-start | bytes 196616 | tf_op jit(solution)/shard_map/ppermute | solution.py:39
  64.2 4.6 %collective-permute-start.16 = (bf16[64,512]{1,0:T(8,128)(2,1)S(1)}, bf16[64,512]{1,0:T(8,128)(2,1)S(1)}, u32[]{:S(2)}, u32[]{:S(2)}) collective-permute-start(bf16[64,512]{1,0:T(8,128)(2,1)S(1)} %get-tuple-element.62), channel_id=1, source_target_pairs={{0,2},{1,3},{64,66},{65,67},{2,0},{3,1},{66,64},{67,65},{16,18},{1... | collective-permute-start | bytes 196616 | tf_op jit(solution)/shard_map/ppermute | solution.py:39
  69.8 10.3 %collective-permute-start.17 = (bf16[576,512]{1,0:T(8,128)(2,1)S(1)}, bf16[576,512]{1,0:T(8,128)(2,1)S(1)}, u32[]{:S(2)}, u32[]{:S(2)}) collective-permute-start(bf16[576,512]{1,0:T(8,128)(2,1)S(1)} %get-tuple-element.67), channel_id=1, source_target_pairs={{0,16},{1,5},{64,80},{65,69},{2,18},{3,7},{66,82},{67,71},{16,32},... | collective-permute-start | bytes 1769480 | tf_op jit(solution)/shard_map/ppermute | solution.py:39
  70.7 15.0 %collective-permute-start.18 = (bf16[576,512]{1,0:T(8,128)(2,1)S(1)}, bf16[576,512]{1,0:T(8,128)(2,1)S(1)}, u32[]{:S(2)}, u32[]{:S(2)}) collective-permute-start(bf16[576,512]{1,0:T(8,128)(2,1)S(1)} %get-tuple-element.68), channel_id=1, source_target_pairs={{0,48},{1,13},{64,112},{65,77},{2,50},{3,15},{66,114},{67,79},{16,... | collective-permute-start | bytes 1769480 | tf_op jit(solution)/shard_map/ppermute | solution.py:39
  72.5 14.1 %collective-permute-start.19 = (bf16[576,512]{1,0:T(8,128)(2,1)S(1)}, bf16[576,512]{1,0:T(8,128)(2,1)S(1)}, u32[]{:S(2)}, u32[]{:S(2)}) collective-permute-start(bf16[576,512]{1,0:T(8,128)(2,1)S(1)} %get-tuple-element.69), channel_id=1, source_target_pairs={{0,32},{1,9},{64,96},{65,73},{2,34},{3,11},{66,98},{67,75},{16,48}... | collective-permute-start | bytes 1769480 | tf_op jit(solution)/shard_map/ppermute | solution.py:39
  87.1 19.7 %collective-permute-start.20 = (bf16[576,512]{1,0:T(8,128)(2,1)S(1)}, bf16[576,512]{1,0:T(8,128)(2,1)S(1)}, u32[]{:S(2)}, u32[]{:S(2)}) collective-permute-start(bf16[576,512]{1,0:T(8,128)(2,1)S(1)} %get-tuple-element.64), channel_id=1, source_target_pairs={{0,4},{1,17},{64,68},{65,81},{2,6},{3,19},{66,70},{67,83},{16,20},... | collective-permute-start | bytes 1769480 | tf_op jit(solution)/shard_map/ppermute | solution.py:39
  87.7 19.1 %collective-permute-start.21 = (bf16[576,512]{1,0:T(8,128)(2,1)S(1)}, bf16[576,512]{1,0:T(8,128)(2,1)S(1)}, u32[]{:S(2)}, u32[]{:S(2)}) collective-permute-start(bf16[576,512]{1,0:T(8,128)(2,1)S(1)} %get-tuple-element.65), channel_id=1, source_target_pairs={{0,12},{1,49},{64,76},{65,113},{2,14},{3,51},{66,78},{67,115},{16,... | collective-permute-start | bytes 1769480 | tf_op jit(solution)/shard_map/ppermute | solution.py:39
  90.4 16.4 %collective-permute-start.22 = (bf16[576,512]{1,0:T(8,128)(2,1)S(1)}, bf16[576,512]{1,0:T(8,128)(2,1)S(1)}, u32[]{:S(2)}, u32[]{:S(2)}) collective-permute-start(bf16[576,512]{1,0:T(8,128)(2,1)S(1)} %get-tuple-element.66), channel_id=1, source_target_pairs={{0,8},{1,33},{64,72},{65,97},{2,10},{3,35},{66,74},{67,99},{16,24}... | collective-permute-start | bytes 1769480 | tf_op jit(solution)/shard_map/ppermute | solution.py:39
  91.5 11.7 %collective-permute-start.23 = (bf16[512,512]{1,0:T(8,128)(2,1)S(1)}, bf16[512,512]{1,0:T(8,128)(2,1)S(1)}, u32[]{:S(2)}, u32[]{:S(2)}) collective-permute-start(bf16[512,512]{1,0:T(8,128)(2,1)S(1)} %slice.82), channel_id=1, source_target_pairs={{0,64},{1,3},{64,0},{65,67},{2,66},{3,1},{66,2},{67,65},{16,80},{1... | collective-permute-start | bytes 1572872 | tf_op jit(solution)/shard_map/ppermute | solution.py:39
  103.2 15.1 %collective-permute-start.24 = (bf16[512,512]{1,0:T(8,128)(2,1)S(1)}, bf16[512,512]{1,0:T(8,128)(2,1)S(1)}, u32[]{:S(2)}, u32[]{:S(2)}) collective-permute-start(bf16[512,512]{1,0:T(8,128)(2,1)S(1)} %collective-permute-done.23), channel_id=1, source_target_pairs={{0,1},{1,0},{64,65},{65,64},{2,3},{3,2},{66,67},{67,66},{16,17},{1... | collective-permute-start | bytes 1572872 | tf_op jit(solution)/shard_map/ppermute | solution.py:39
  107.2 4.4 %collective-permute-start.26 = (bf16[64,512]{1,0:T(8,128)(2,1)S(1)}, bf16[64,512]{1,0:T(8,128)(2,1)S(1)}, u32[]{:S(2)}, u32[]{:S(2)}) collective-permute-start(bf16[64,512]{1,0:T(8,128)(2,1)S(1)} %slice.85), channel_id=1, source_target_pairs={{0,64},{1,65},{64,2},{65,3},{2,66},{3,67},{66,0},{67,1},{16,80},{1... | collective-permute-start | bytes 196616 | tf_op jit(solution)/shard_map/ppermute | solution.py:39
  108.2 3.3 %collective-permute-start.27 = (bf16[64,512]{1,0:T(8,128)(2,1)S(1)}, bf16[64,512]{1,0:T(8,128)(2,1)S(1)}, u32[]{:S(2)}, u32[]{:S(2)}) collective-permute-start(bf16[64,512]{1,0:T(8,128)(2,1)S(1)} %slice.85), channel_id=1, source_target_pairs={{0,66},{1,67},{64,0},{65,1},{2,64},{3,65},{66,2},{67,3},{16,82},{1... | collective-permute-start | bytes 196616 | tf_op jit(solution)/shard_map/ppermute | solution.py:39
  109.9 5.2 %collective-permute-start.28 = (bf16[64,512]{1,0:T(8,128)(2,1)S(1)}, bf16[64,512]{1,0:T(8,128)(2,1)S(1)}, u32[]{:S(2)}, u32[]{:S(2)}) collective-permute-start(bf16[64,512]{1,0:T(8,128)(2,1)S(1)} %slice.85), channel_id=1, source_target_pairs={{0,2},{1,3},{64,66},{65,67},{2,0},{3,1},{66,64},{67,65},{16,18},{1... | collective-permute-start | bytes 196616 | tf_op jit(solution)/shard_map/ppermute | solution.py:39
  115.2 5.3 %copy-start = (bf16[512,512]{1,0:T(8,128)(2,1)S(1)}, bf16[512,512]{1,0:T(8,128)(2,1)}, u32[]{:S(2)}) copy-start(bf16[512,512]{1,0:T(8,128)(2,1)} %weight.1) | copy-start | bytes 1572868
  115.2 4.2 %collective-permute-start.29 = (bf16[256,512]{1,0:T(8,128)(2,1)S(1)}, bf16[256,512]{1,0:T(8,128)(2,1)S(1)}, u32[]{:S(2)}, u32[]{:S(2)}) collective-permute-start(bf16[256,512]{1,0:T(8,128)(2,1)S(1)} %pad_maximum_fusion.9.mine), channel_id=1, source_target_pairs={{0,1},{1,0},{64,65},{65,64},{2,3},{3,2},{66,67},{67,66},{16,17},{1... | collective-permute-start | bytes 786440 | tf_op jit(solution)/shard_map/ppermute | solution.py:39
  118.4 2.1 %collective-permute-start.25 = (bf16[256,512]{1,0:T(8,128)(2,1)S(1)}, bf16[256,512]{1,0:T(8,128)(2,1)S(1)}, u32[]{:S(2)}, u32[]{:S(2)}) collective-permute-start(bf16[256,512]{1,0:T(8,128)(2,1)S(1)} %slice_select_fusion), channel_id=1, source_target_pairs={{0,1},{1,0},{64,65},{65,64},{2,3},{3,2},{66,67},{67,66},{16,17},{1... | collective-permute-start | bytes 786440 | tf_op jit(solution)/shard_map/ppermute | solution.py:39

commit v3 on v2

--- a/solution.py
+++ b/solution.py
@@ -76,9 +76,14 @@
     return col // 4, row % 4, row // 4, (col // 2) % 2, col % 2
 
 
-def part_at(place):
-    near, far = coordinates()[2:4]
-    return (far * 2 + near + DISTANCE[place]) % 4
+def part_at(core, place):
+    x, y = coordinates()[:2]
+    return (jnp.where(core == 0, y, x) + DISTANCE[place]) % 4
+
+
+def panel_place(place):
+    partner = 1 - (place >> 2)
+    return jnp.where((place & 3) == 0, partner, 1 + (place & 3) + 3 * partner)
 
 
 def lists_kernel(coords, count, lists):
@@ -100,7 +105,7 @@
     a_owner, b_owner = a >> 1, b >> 1
     a_place = (1 - (((a_owner >> 1) & 1) ^ my_far)) * 4 + ring_place(((a_owner >> 2) - my_x) & 3)
     b_place = (1 - ((b_owner >> 2) ^ my_near)) * 4 + ring_place(((b_owner & 3) - my_y) & 3)
-    a_from, b_from = a_place ^ 4, b_place ^ 4
+    a_from, b_from = panel_place(a_place), panel_place(b_place)
     a_tile = a_place * 4 + (a_owner & 1) * 2 + (a & 1)
     b_tile = b_place * 2 + (b & 1)
     a_source = a_from * 4 + (a_owner & 1) * 2 + (a & 1) + (1 - my_core) * 32
@@ -144,7 +149,7 @@
 
 def live_tile(values, slot):
     tile = values[jnp.maximum(slot, 0)]
-    return tile * jnp.where(slot >= 0, 1.0, 0.0).astype(BF16)
+    return jnp.where(slot >= 0, tile, jnp.zeros_like(tile))
 
 
 def backward_kernel(lists, values, panels, far, near, term_keep, term_send, total, whole, term):
@@ -177,45 +182,53 @@
             target[rows(q * 2 * SPAN + core * SPAN, SPAN), :] = whole[from_here : from_here + SPAN, :]
             target[rows(q * 2 * SPAN + (1 - core) * SPAN, SPAN), :] = jnp.zeros((SPAN, FEAT), BF16)
     start = core * 16 * SPAN + core * SPAN
-    feats = jnp.concatenate([panels[rows(start + (q ^ 4) * 2 * SPAN, SPAN), :] for q in range(8)], axis=0)
+    feats = jnp.concatenate([panels[rows(start + q * 2 * SPAN, SPAN), :] for q in (1, 5, 6, 7, 0, 2, 3, 4)], axis=0)
     term[...] = lax.dot_general(
         feats, whole[...], (((0,), (0,)), ((), ())), preferred_element_type=F32
     ).astype(BF16)
     for place in range(4):
         for target, side in ((term_keep, core), (term_send, 1 - core)):
-            first = side * SPAN + part_at(place) * PART
+            first = side * SPAN + part_at(side, place) * PART
             target[place * PART : (place + 1) * PART, :] = term[rows(first, PART), :]
 
 
-def forward_kernel(half, lists, values, panels, back, keep, send):
+def forward_kernel(half, lists, values, panels, back, keep, send, rows_out, sems):
     core = coordinates()[4]
 
-    def row_step(q, carry):
-        products = []
+    def move(source, target, sem):
+        return pltpu.make_async_copy(source, target, sem)
+
+    @pl.when(core == half)
+    def _():
+        move(back, keep, sems.at[0]).start()
+
+    @pl.when(core == 1 - half)
+    def _():
+        move(back, send, sems.at[0]).start()
+
+    for q in range(16 // STEP):
+        here = pl.ds(q * STEP * TILE, STEP * TILE)
         for k in range(STEP):
-            first = (half * 16 + q * STEP + k) * PER_ROW
+            tile = q * STEP + k
+            first = (half * 16 + tile) * PER_ROW
             tiles = [live_tile(values, lists[0, first + i]) for i in range(PER_ROW)]
             source = [panels[block(lists[1, first + i]), :] for i in range(PER_ROW)]
-            products.append(
-                jnp.dot(
-                    jnp.concatenate(tiles, axis=1), jnp.concatenate(source, axis=0), preferred_element_type=F32
-                ).astype(BF16)
-            )
-        here = rows(q * STEP * TILE, STEP * TILE)
+            rows_out[tile * TILE : (tile + 1) * TILE, :] = jnp.dot(
+                jnp.concatenate(tiles, axis=1), jnp.concatenate(source, axis=0), preferred_element_type=F32
+            ).astype(BF16)
 
         @pl.when(core == half)
         def _():
-            send[here, :] = jnp.concatenate(products, axis=0)
-            keep[here, :] = back[here, :]
+            move(rows_out.at[here], send.at[here], sems.at[1 + q]).start()
 
         @pl.when(core == 1 - half)
         def _():
-            keep[here, :] = jnp.concatenate(products, axis=0)
-            send[here, :] = back[here, :]
-
-        return carry
-
-    lax.fori_loop(0, 16 // STEP, row_step, 0)
+            move(rows_out.at[here], keep.at[here], sems.at[1 + q]).start()
+
+    move(back, keep, sems.at[0]).wait()
+    for q in range(16 // STEP):
+        here = pl.ds(q * STEP * TILE, STEP * TILE)
+        move(rows_out.at[here], send.at[here], sems.at[1 + q]).wait()
 
 
 def shape(n, dtype=BF16):
@@ -243,6 +256,7 @@
         out_shape=(shape(HALF_ROWS), shape(HALF_ROWS)),
         in_specs=[SMEM, VMEM, VMEM, VMEM],
         out_specs=[VMEM] * 2,
+        scratch_shapes=[pltpu.VMEM((HALF_ROWS, FEAT), BF16), pltpu.SemaphoreType.DMA((5,))],
         compiler_params=pltpu.CompilerParams(vmem_limit_bytes=8 * 2**20),
     )(lists, values, panels, back)
 
@@ -279,7 +293,7 @@
     core = coordinates()[4]
     for place in range(4):
         for source, side in ((mine, core), (other, 1 - core)):
-            first = side * SPAN + part_at(place) * PART
+            first = side * SPAN + part_at(side, place) * PART
             grad[rows(first, PART), :] = source[place * PART : (place + 1) * PART, :].astype(F32) * scale
 
 
@@ -324,35 +338,38 @@
     lists = make_lists(jnp.transpose(tile_coords[0, 0]), tile_count)
     first = lax.axis_index("col") % 2 == 0
     other_features, other_cotangent = permute(features, to_core), permute(cotangent, to_core)
-    own = jnp.where(first, stack(features, other_features), stack(other_cotangent, cotangent))
+    all_features = jnp.where(first, stack(features, other_features), stack(other_features, features))
+    all_cotangent = jnp.where(first, stack(cotangent, other_cotangent), stack(other_cotangent, cotangent))
+    own = jnp.where(first, all_features, all_cotangent)
+    other_own = jnp.where(first, all_cotangent, all_features)
     from_z = permute(own, to_z)
     near = list(ring_gather(own, ring))
-    from_z, *near, lists = lax.optimization_barrier((from_z, *near, lists))
-    near = stack(*near, from_z)
-    other_near = permute(near, to_core)
-    far = stack(*ring_gather(from_z, ring)[1:])
-    far, other_near = lax.optimization_barrier((far, other_near))
-    panels = stack(near, far, other_near, permute(far, to_core))
+    before, after, opposite = near[1:]
+    from_z, opposite, lists = lax.optimization_barrier((from_z, opposite, lists))
+    far = ring_gather(from_z, ring)[1:]
+    ringed = stack(from_z, before, after, opposite, *far)
+    panels = stack(own, ringed, other_own, permute(ringed, to_core))
 
     back_far, back_near, term_keep, term_send = backward_sums(lists, values, panels)
     part = add(term_keep, permute(term_send, to_core))
-    part, back_far = lax.optimization_barrier((part, back_far))
     keep_far, send_far = forward_sums(0, lists, values, panels, back_far)
     sum_far = add(keep_far, permute(send_far, to_core))
-    part = add(*ring_sum(split(part, PART), along_z))
     keep_near, send_near = forward_sums(1, lists, values, panels, back_near)
+    send_near, part = lax.optimization_barrier((send_near, part))
     sum_near = add(keep_near, permute(send_near, to_core))
-    far = [stack(piece, part) for piece in split(sum_far, 2 * SPAN)]
+    far = [stack(*both) for both in zip(split(sum_far, 2 * SPAN), split(part, PART))]
     far = add(*ring_sum(far, ring))
     far, part = far[: 2 * SPAN], far[2 * SPAN :]
     near = add(*ring_sum([stack(piece, part) for piece in split(sum_near, 2 * SPAN)], cross_ring))
     near, part = near[: 2 * SPAN], near[2 * SPAN :]
     passed = permute(permute(far, to_z), to_core)
-    mine = stack(*ring_gather(part, along_z))
+    part = add(*ring_gather(part, along_z))
+    mine = stack(*ring_gather(part, ring))
     other = permute(mine, to_core)
     final = add(near, passed)
     got = permute(jnp.where(first, final[SPAN:], final[:SPAN]), to_core)
     output, features_grad = finish(final, got, weight)
+    other, output, features_grad = lax.optimization_barrier((other, output, features_grad))
     nodes = lax.axis_size("row") * lax.axis_size("col") * SPAN
     weight_grad = place_parts(nodes ** (-0.5), mine, other)
     return output, features_grad, weight_grad

time: 122 us -> 119 us (0.975)
  waiting for transfers between devices: 59 us -> 47.6 us
  starting transfers between devices: 39.8 us -> 47.9 us
    ppermute x30 -> x29, waiting for transfers between devices: 59 us -> 47.6 us  [permute(): return lax.ppermute(value, ('row', 'col'), pairs)]
    ppermute x30 -> x29, starting transfers between devices: 39.8 us -> 47.9 us  [permute(): return lax.ppermute(value, ('row', 'col'), pairs)]
    unnamed x1 -> x3, other arithmetic: 0.01 us -> 1.82 us
  transfers between devices with their start and end apart: 30 -> 29, of which waited for: 17 -> 17; matrix products, arithmetic and copies ran while one was open for 2% -> 3% of each run, Pallas kernels for 4% -> 5%
where the time goes in v3:
time: 119 us; the launch traced here: 118 us
  starting transfers between devices  47.9 us (40%)
  waiting for transfers between devices  47.6 us (40%)
  Pallas kernels  15.1 us (13%)
  other arithmetic  4.32 us (4%)
  local copies, waits for them, and re-layouts  1.76 us (1%)
  between operations  1.53 us (1%)
    ppermute x29, starting transfers between devices, permute(): return lax.ppermute(value, ('row', 'col'), pairs)  47.9 us
    ppermute x29, waiting for transfers between devices, permute(): return lax.ppermute(value, ('row', 'col'), pairs)  47.6 us
    pallas_call x2, Pallas kernels, forward_sums(): pl.pallas_call(functools.partial(forward_kernel, half), out_shape=(shape(...  7.12 us
    pallas_call x1, Pallas kernels, backward_sums(): pl.pallas_call(backward_kernel, out_shape=(shape(HALF_ROWS), shape(HALF_R...  5 us
  transfers between devices with their start and end apart: 29, of which 17 were waited for; matrix products, arithmetic and copies ran while one was open for 3% of the time, Pallas kernels for 5%

profile of v3, /device:TPU:1, one launch (start us, length us, event | category | flops | bytes accessed | tf_op | source)
XLA Modules:
  0.0 118.1 jit_solution(5252900193640172122)
XLA Ops:
  0.6 1.5 %collective-permute-start = (bf16[256,512]{1,0:T(8,128)(2,1)}, bf16[256,512]{1,0:T(8,128)(2,1)S(1)}, u32[]{:S(2)}, u32[]{:S(2)}) collective-permute-start(bf16[256,512]{1,0:T(8,128)(2,1)} %param.6), channel_id=1, source_target_pairs={{0,1},{1,0},{64,65},{65,64},{2,3},{3,2},{66,67},{67,66},{16,17},{1... | collective-permute-start | bytes 786440 | tf_op jit(solution)/shard_map/ppermute | solution.py:39
  2.2 1.3 %collective-permute-done = bf16[256,512]{1,0:T(8,128)(2,1)S(1)} collective-permute-done((bf16[256,512]{1,0:T(8,128)(2,1)}, bf16[256,512]{1,0:T(8,128)(2,1)S(1)}, u32[]{:S(2)}, u32[]{:S(2)}) %collective-permute-start) | collective-permute-done | bytes 262176 | tf_op jit(solution)/shard_map/ppermute | solution.py:39
  3.9 1.5 %constant_dynamic-update-slice_fusion.15 = (bf16[8192,512]{1,0:T(8,128)(2,1)S(1)}, bf16[512,512]{1,0:T(8,128)(2,1)S(1)}) fusion(bf16[256,512]{1,0:T(8,128)(2,1)} %param.8, bf16[256,512]{1,0:T(8,128)(2,1)S(1)} %collective-permute-done.1, bf16[256,512]{1,0:T(8,128)(2,1)} %param.6, bf16[256,512]{1,0:T(8,128)(2,1)S(1)} %collective-permute-done, pred[]{:T(512)S(6)} %eq.5), kind=kLoop, calls=%fused_computation.35 | loop fusion | flops 4980735 | bytes 2097153
  5.3 3.8 %collective-permute-start.2 = (bf16[512,512]{1,0:T(8,128)(2,1)S(1)}, bf16[512,512]{1,0:T(8,128)(2,1)S(1)}, u32[]{:S(2)}, u32[]{:S(2)}) collective-permute-start(bf16[512,512]{1,0:T(8,128)(2,1)S(1)} %get-tuple-element.40), channel_id=1, source_target_pairs={{0,64},{1,3},{64,0},{65,67},{2,66},{3,1},{66,2},{67,65},{16,80},{1... | collective-permute-start | bytes 1572872 | tf_op jit(solution)/shard_map/ppermute | solution.py:39
  9.1 2.7 %collective-permute-start.3 = (bf16[512,512]{1,0:T(8,128)(2,1)S(1)}, bf16[512,512]{1,0:T(8,128)(2,1)S(1)}, u32[]{:S(2)}, u32[]{:S(2)}) collective-permute-start(bf16[512,512]{1,0:T(8,128)(2,1)S(1)} %get-tuple-element.40), channel_id=1, source_target_pairs={{0,32},{1,9},{64,96},{65,73},{2,34},{3,11},{66,98},{67,75},{16,48}... | collective-permute-start | bytes 1572872 | tf_op jit(solution)/shard_map/ppermute | solution.py:39
  12.2 2.4 %collective-permute-start.5 = (bf16[512,512]{1,0:T(8,128)(2,1)S(1)}, bf16[512,512]{1,0:T(8,128)(2,1)S(1)}, u32[]{:S(2)}, u32[]{:S(2)}) collective-permute-start(bf16[512,512]{1,0:T(8,128)(2,1)S(1)} %get-tuple-element.40), channel_id=1, source_target_pairs={{0,48},{1,13},{64,112},{65,77},{2,50},{3,15},{66,114},{67,79},{16,... | collective-permute-start | bytes 1572872 | tf_op jit(solution)/shard_map/ppermute | solution.py:39
  15.2 0.7 copy-done.1
  15.9 0.7 shard_map.85.lists
  16.5 3.2 %collective-permute-done.2 = bf16[512,512]{1,0:T(8,128)(2,1)S(1)} collective-permute-done((bf16[512,512]{1,0:T(8,128)(2,1)S(1)}, bf16[512,512]{1,0:T(8,128)(2,1)S(1)}, u32[]{:S(2)}, u32[]{:S(2)}) %collective-permute-start.2) | collective-permute-done | bytes 524320 | tf_op jit(solution)/shard_map/ppermute | solution.py:39
  19.7 1.2 %collective-permute-start.6 = (bf16[512,512]{1,0:T(8,128)(2,1)S(1)}, bf16[512,512]{1,0:T(8,128)(2,1)S(1)}, u32[]{:S(2)}, u32[]{:S(2)}) collective-permute-start(bf16[512,512]{1,0:T(8,128)(2,1)S(1)} %collective-permute-done.2), channel_id=1, source_target_pairs={{0,16},{1,5},{64,80},{65,69},{2,18},{3,7},{66,82},{67,71},{16,32},... | collective-permute-start | bytes 1572872 | tf_op jit(solution)/shard_map/ppermute | solution.py:39
  20.9 1.5 %collective-permute-start.7 = (bf16[512,512]{1,0:T(8,128)(2,1)S(1)}, bf16[512,512]{1,0:T(8,128)(2,1)S(1)}, u32[]{:S(2)}, u32[]{:S(2)}) collective-permute-start(bf16[512,512]{1,0:T(8,128)(2,1)S(1)} %collective-permute-done.2), channel_id=1, source_target_pairs={{0,48},{1,13},{64,112},{65,77},{2,50},{3,15},{66,114},{67,79},{16,... | collective-permute-start | bytes 1572872 | tf_op jit(solution)/shard_map/ppermute | solution.py:39
  22.4 1.5 %collective-permute-start.8 = (bf16[512,512]{1,0:T(8,128)(2,1)S(1)}, bf16[512,512]{1,0:T(8,128)(2,1)S(1)}, u32[]{:S(2)}, u32[]{:S(2)}) collective-permute-start(bf16[512,512]{1,0:T(8,128)(2,1)S(1)} %collective-permute-done.2), channel_id=1, source_target_pairs={{0,32},{1,9},{64,96},{65,73},{2,34},{3,11},{66,98},{67,75},{16,48}... | collective-permute-start | bytes 1572872 | tf_op jit(solution)/shard_map/ppermute | solution.py:39
  24.0 0.5 collective-permute-done.4
  24.8 5.0 %collective-permute-done.6 = bf16[512,512]{1,0:T(8,128)(2,1)S(1)} collective-permute-done((bf16[512,512]{1,0:T(8,128)(2,1)S(1)}, bf16[512,512]{1,0:T(8,128)(2,1)S(1)}, u32[]{:S(2)}, u32[]{:S(2)}) %collective-permute-start.6) | collective-permute-done | bytes 524320 | tf_op jit(solution)/shard_map/ppermute | solution.py:39
  30.4 5.5 %collective-permute-done.8 = bf16[512,512]{1,0:T(8,128)(2,1)S(1)} collective-permute-done((bf16[512,512]{1,0:T(8,128)(2,1)S(1)}, bf16[512,512]{1,0:T(8,128)(2,1)S(1)}, u32[]{:S(2)}, u32[]{:S(2)}) %collective-permute-start.8) | collective-permute-done | bytes 524320 | tf_op jit(solution)/shard_map/ppermute | solution.py:39
  35.9 0.5 collective-permute-start.9
  36.7 5.7 %collective-permute-done.9 = bf16[3584,512]{1,0:T(8,128)(2,1)S(1)} collective-permute-done((bf16[3584,512]{1,0:T(8,128)(2,1)S(1)}, bf16[3584,512]{1,0:T(8,128)(2,1)S(1)}, u32[]{:S(2)}, u32[]{:S(2)}) %collective-permute-start.9) | collective-permute-done | bytes 3670048 | tf_op jit(solution)/shard_map/ppermute | solution.py:39
  42.7 5.0 %shard_map.86 = (bf16[2048,512]{1,0:T(8,128)(2,1)S(1)}, bf16[2048,512]{1,0:T(8,128)(2,1)S(1)}, bf16[256,512]{1,0:T(8,128)(2,1)S(1)}, bf16[256,512]{1,0:T(8,128)(2,1)S(1)}) custom-call(s32[8,384]{1,0:T(8,128)S(1)} %shard_map.85.lists, bf16[192,128,128]{2,1,0:T(8,128)(2,1)S(1)} %bitcast.6, bf16[8192,512]{1,0:T(8,128)(2,1)S(1)} %constant_dynamic-update-slice_fusion.7.panels), custom_call_target="tpu_custom_call" | custom-call | tf_op jit(solution)/shard_map/pallas_call | solution.py:239
  47.7 3.5 %shard_map.88 = (bf16[2048,512]{1,0:T(8,128)(2,1)S(1)}, bf16[2048,512]{1,0:T(8,128)(2,1)S(1)}) custom-call(s32[8,384]{1,0:T(8,128)S(1)} %shard_map.85.lists, bf16[192,128,128]{2,1,0:T(8,128)(2,1)S(1)} %bitcast.7, bf16[8192,512]{1,0:T(8,128)(2,1)S(1)} %constant_dynamic-update-slice_fusion.7.panels, bf16[2048,512]{1,0:T(8,128)(2,1)S(1)} %get-tuple-element.30.back), custom_call_target="tpu_custom_call" | custom-call | tf_op jit(solution)/shard_map/pallas_call | solution.py:254
  51.1 0.5 collective-permute-start.12
  51.7 3.7 %shard_map.87 = (bf16[2048,512]{1,0:T(8,128)(2,1)S(1)}, bf16[2048,512]{1,0:T(8,128)(2,1)S(1)}) custom-call(s32[8,384]{1,0:T(8,128)S(1)} %shard_map.85.lists, bf16[192,128,128]{2,1,0:T(8,128)(2,1)S(1)} %bitcast.8, bf16[8192,512]{1,0:T(8,128)(2,1)S(1)} %constant_dynamic-update-slice_fusion.7.panels, bf16[2048,512]{1,0:T(8,128)(2,1)S(1)} %get-tuple-element.24.back), custom_call_target="tpu_custom_call" | custom-call | tf_op jit(solution)/shard_map/pallas_call | solution.py:254
  55.8 0.5 collective-permute-start.11
  56.3 0.6 add_convert_fusion
  57.2 2.3 %collective-permute-start.13 = (bf16[576,512]{1,0:T(8,128)(2,1)S(1)}, bf16[576,512]{1,0:T(8,128)(2,1)S(1)}, u32[]{:S(2)}, u32[]{:S(2)}) collective-permute-start(bf16[576,512]{1,0:T(8,128)(2,1)S(1)} %pad_maximum_fusion.4), channel_id=1, source_target_pairs={{0,16},{1,5},{64,80},{65,69},{2,18},{3,7},{66,82},{67,71},{16,32},... | collective-permute-start | bytes 1769480 | tf_op jit(solution)/shard_map/ppermute | solution.py:39
  59.5 1.0 collective-permute-start.14
  60.5 1.5 %collective-permute-start.15 = (bf16[576,512]{1,0:T(8,128)(2,1)S(1)}, bf16[576,512]{1,0:T(8,128)(2,1)S(1)}, u32[]{:S(2)}, u32[]{:S(2)}) collective-permute-start(bf16[576,512]{1,0:T(8,128)(2,1)S(1)} %pad_maximum_fusion.6), channel_id=1, source_target_pairs={{0,32},{1,9},{64,96},{65,73},{2,34},{3,11},{66,98},{67,75},{16,48}... | collective-permute-start | bytes 1769480 | tf_op jit(solution)/shard_map/ppermute | solution.py:39
  62.1 0.7 add_convert_fusion.1
  62.9 5.0 %collective-permute-done.13 = bf16[576,512]{1,0:T(8,128)(2,1)S(1)} collective-permute-done((bf16[576,512]{1,0:T(8,128)(2,1)S(1)}, bf16[576,512]{1,0:T(8,128)(2,1)S(1)}, u32[]{:S(2)}, u32[]{:S(2)}) %collective-permute-start.13) | collective-permute-done | bytes 589856 | tf_op jit(solution)/shard_map/ppermute | solution.py:39
  67.9 0.7 collective-permute-done.14
  68.6 6.8 %collective-permute-done.15 = bf16[576,512]{1,0:T(8,128)(2,1)S(1)} collective-permute-done((bf16[576,512]{1,0:T(8,128)(2,1)S(1)}, bf16[576,512]{1,0:T(8,128)(2,1)S(1)}, u32[]{:S(2)}, u32[]{:S(2)}) %collective-permute-start.15) | collective-permute-done | bytes 589856 | tf_op jit(solution)/shard_map/ppermute | solution.py:39
  75.9 1.6 %collective-permute-start.16 = (bf16[576,512]{1,0:T(8,128)(2,1)S(1)}, bf16[576,512]{1,0:T(8,128)(2,1)S(1)}, u32[]{:S(2)}, u32[]{:S(2)}) collective-permute-start(bf16[576,512]{1,0:T(8,128)(2,1)S(1)} %get-tuple-element.67), channel_id=1, source_target_pairs={{0,4},{1,17},{64,68},{65,81},{2,6},{3,19},{66,70},{67,83},{16,20},... | collective-permute-start | bytes 1769480 | tf_op jit(solution)/shard_map/ppermute | solution.py:39
  77.5 1.2 collective-permute-start.17
  78.6 0.9 collective-permute-start.18
  79.5 4.2 %collective-permute-start.26 = (bf16[512,512]{1,0:T(8,128)(2,1)S(1)}, bf16[512,512]{1,0:T(8,128)(2,1)S(1)}, u32[]{:S(2)}, u32[]{:S(2)}) collective-permute-start(bf16[512,512]{1,0:T(8,128)(2,1)S(1)} %slice.83), channel_id=1, source_target_pairs={{0,64},{1,3},{64,0},{65,67},{2,66},{3,1},{66,2},{67,65},{16,80},{1... | collective-permute-start | bytes 1572872 | tf_op jit(solution)/shard_map/ppermute | solution.py:39
  83.7 9.1 %collective-permute-done.26 = bf16[512,512]{1,0:T(8,128)(2,1)S(1)} collective-permute-done((bf16[512,512]{1,0:T(8,128)(2,1)S(1)}, bf16[512,512]{1,0:T(8,128)(2,1)S(1)}, u32[]{:S(2)}, u32[]{:S(2)}) %collective-permute-start.26) | collective-permute-done | bytes 524320 | tf_op jit(solution)/shard_map/ppermute | solution.py:39
  92.8 4.3 %collective-permute-start.27 = (bf16[512,512]{1,0:T(8,128)(2,1)S(1)}, bf16[512,512]{1,0:T(8,128)(2,1)S(1)}, u32[]{:S(2)}, u32[]{:S(2)}) collective-permute-start(bf16[512,512]{1,0:T(8,128)(2,1)S(1)} %collective-permute-done.26), channel_id=1, source_target_pairs={{0,1},{1,0},{64,65},{65,64},{2,3},{3,2},{66,67},{67,66},{16,17},{1... | collective-permute-start | bytes 1572872 | tf_op jit(solution)/shard_map/ppermute | solution.py:39
  97.5 2.2 %collective-permute-start.19 = (bf16[64,512]{1,0:T(8,128)(2,1)S(1)}, bf16[64,512]{1,0:T(8,128)(2,1)S(1)}, u32[]{:S(2)}, u32[]{:S(2)}) collective-permute-start(bf16[64,512]{1,0:T(8,128)(2,1)S(1)} %slice.81), channel_id=1, source_target_pairs={{0,64},{1,65},{64,2},{65,3},{2,66},{3,67},{66,0},{67,1},{16,80},{1... | collective-permute-start | bytes 196616 | tf_op jit(solution)/shard_map/ppermute | solution.py:39
  99.7 0.6 collective-permute-start.20
  100.2 2.4 %collective-permute-start.21 = (bf16[64,512]{1,0:T(8,128)(2,1)S(1)}, bf16[64,512]{1,0:T(8,128)(2,1)S(1)}, u32[]{:S(2)}, u32[]{:S(2)}) collective-permute-start(bf16[64,512]{1,0:T(8,128)(2,1)S(1)} %slice.81), channel_id=1, source_target_pairs={{0,2},{1,3},{64,66},{65,67},{2,0},{3,1},{66,64},{67,65},{16,18},{1... | collective-permute-start | bytes 196616 | tf_op jit(solution)/shard_map/ppermute | solution.py:39
  102.9 2.0 %collective-permute-done.21 = bf16[64,512]{1,0:T(8,128)(2,1)S(1)} collective-permute-done((bf16[64,512]{1,0:T(8,128)(2,1)S(1)}, bf16[64,512]{1,0:T(8,128)(2,1)S(1)}, u32[]{:S(2)}, u32[]{:S(2)}) %collective-permute-start.21) | collective-permute-done | bytes 65568 | tf_op jit(solution)/shard_map/ppermute | solution.py:39
  104.9 1.0 collective-permute-start.22
  105.9 1.7 %collective-permute-start.23 = (bf16[64,512]{1,0:T(8,128)(2,1)S(1)}, bf16[64,512]{1,0:T(8,128)(2,1)S(1)}, u32[]{:S(2)}, u32[]{:S(2)}) collective-permute-start(bf16[64,512]{1,0:T(8,128)(2,1)S(1)} %add_convert_fusion.6), channel_id=1, source_target_pairs={{0,48},{1,13},{64,112},{65,77},{2,50},{3,15},{66,114},{67,79},{16,... | collective-permute-start | bytes 196616 | tf_op jit(solution)/shard_map/ppermute | solution.py:39
  107.6 0.4 collective-permute-start.24
  108.2 2.6 %collective-permute-start.28 = (bf16[256,512]{1,0:T(8,128)(2,1)S(1)}, bf16[256,512]{1,0:T(8,128)(2,1)S(1)}, u32[]{:S(2)}, u32[]{:S(2)}) collective-permute-start(bf16[256,512]{1,0:T(8,128)(2,1)S(1)} %slice_select_fusion), channel_id=1, source_target_pairs={{0,1},{1,0},{64,65},{65,64},{2,3},{3,2},{66,67},{67,66},{16,17},{1... | collective-permute-start | bytes 786440 | tf_op jit(solution)/shard_map/ppermute | solution.py:39
  110.9 1.4 %collective-permute-done.24 = bf16[64,512]{1,0:T(8,128)(2,1)S(1)} collective-permute-done((bf16[64,512]{1,0:T(8,128)(2,1)S(1)}, bf16[64,512]{1,0:T(8,128)(2,1)S(1)}, u32[]{:S(2)}, u32[]{:S(2)}) %collective-permute-start.24) | collective-permute-done | bytes 65568 | tf_op jit(solution)/shard_map/ppermute | solution.py:39
  112.3 3.6 %collective-permute-start.25 = (bf16[256,512]{1,0:T(8,128)(2,1)S(1)}, bf16[256,512]{1,0:T(8,128)(2,1)S(1)}, u32[]{:S(2)}, u32[]{:S(2)}) collective-permute-start(bf16[256,512]{1,0:T(8,128)(2,1)S(1)} %pad_maximum_fusion.7.mine), channel_id=1, source_target_pairs={{0,1},{1,0},{64,65},{65,64},{2,3},{3,2},{66,67},{67,66},{16,17},{1... | collective-permute-start | bytes 786440 | tf_op jit(solution)/shard_map/ppermute | solution.py:39
  115.8 1.2 %shard_map.89 = (bf16[256,512]{1,0:T(8,128)(2,1)}, bf16[256,512]{1,0:T(8,128)(2,1)}) custom-call(bf16[512,512]{1,0:T(8,128)(2,1)S(1)} %add_convert_fusion.4.final, bf16[256,512]{1,0:T(8,128)(2,1)S(1)} %collective-permute-done.28.got, bf16[512,512]{1,0:T(8,128)(2,1)S(1)} %copy-done), custom_call_target="tpu_custom_call" | custom-call | tf_op jit(solution)/shard_map/pallas_call | solution.py:283
  117.1 1.1 shard_map.90
  (58 shorter events, 4.6 us)
Async XLA Ops:
  0.6 2.9 %collective-permute-start = (bf16[256,512]{1,0:T(8,128)(2,1)}, bf16[256,512]{1,0:T(8,128)(2,1)S(1)}, u32[]{:S(2)}, u32[]{:S(2)}) collective-permute-start(bf16[256,512]{1,0:T(8,128)(2,1)} %param.6), channel_id=1, source_target_pairs={{0,1},{1,0},{64,65},{65,64},{2,3},{3,2},{66,67},{67,66},{16,17},{1... | collective-permute-start | bytes 786440 | tf_op jit(solution)/shard_map/ppermute | solution.py:39
  2.1 1.7 %collective-permute-start.1 = (bf16[256,512]{1,0:T(8,128)(2,1)}, bf16[256,512]{1,0:T(8,128)(2,1)S(1)}, u32[]{:S(2)}, u32[]{:S(2)}) collective-permute-start(bf16[256,512]{1,0:T(8,128)(2,1)} %param.8), channel_id=1, source_target_pairs={{0,1},{1,0},{64,65},{65,64},{2,3},{3,2},{66,67},{67,66},{16,17},{1... | collective-permute-start | bytes 786440 | tf_op jit(solution)/shard_map/ppermute | solution.py:39
  5.3 14.4 %collective-permute-start.2 = (bf16[512,512]{1,0:T(8,128)(2,1)S(1)}, bf16[512,512]{1,0:T(8,128)(2,1)S(1)}, u32[]{:S(2)}, u32[]{:S(2)}) collective-permute-start(bf16[512,512]{1,0:T(8,128)(2,1)S(1)} %get-tuple-element.40), channel_id=1, source_target_pairs={{0,64},{1,3},{64,0},{65,67},{2,66},{3,1},{66,2},{67,65},{16,80},{1... | collective-permute-start | bytes 1572872 | tf_op jit(solution)/shard_map/ppermute | solution.py:39
  9.1 10.6 %collective-permute-start.3 = (bf16[512,512]{1,0:T(8,128)(2,1)S(1)}, bf16[512,512]{1,0:T(8,128)(2,1)S(1)}, u32[]{:S(2)}, u32[]{:S(2)}) collective-permute-start(bf16[512,512]{1,0:T(8,128)(2,1)S(1)} %get-tuple-element.40), channel_id=1, source_target_pairs={{0,32},{1,9},{64,96},{65,73},{2,34},{3,11},{66,98},{67,75},{16,48}... | collective-permute-start | bytes 1572872 | tf_op jit(solution)/shard_map/ppermute | solution.py:39
  11.8 12.7 %collective-permute-start.4 = (bf16[512,512]{1,0:T(8,128)(2,1)S(1)}, bf16[512,512]{1,0:T(8,128)(2,1)S(1)}, u32[]{:S(2)}, u32[]{:S(2)}) collective-permute-start(bf16[512,512]{1,0:T(8,128)(2,1)S(1)} %get-tuple-element.40), channel_id=1, source_target_pairs={{0,16},{1,5},{64,80},{65,69},{2,18},{3,7},{66,82},{67,71},{16,32},... | collective-permute-start | bytes 1572872 | tf_op jit(solution)/shard_map/ppermute | solution.py:39
  12.2 12.5 %collective-permute-start.5 = (bf16[512,512]{1,0:T(8,128)(2,1)S(1)}, bf16[512,512]{1,0:T(8,128)(2,1)S(1)}, u32[]{:S(2)}, u32[]{:S(2)}) collective-permute-start(bf16[512,512]{1,0:T(8,128)(2,1)S(1)} %get-tuple-element.40), channel_id=1, source_target_pairs={{0,48},{1,13},{64,112},{65,77},{2,50},{3,15},{66,114},{67,79},{16,... | collective-permute-start | bytes 1572872 | tf_op jit(solution)/shard_map/ppermute | solution.py:39
  15.2 0.7 copy-start.1
  19.7 10.2 %collective-permute-start.6 = (bf16[512,512]{1,0:T(8,128)(2,1)S(1)}, bf16[512,512]{1,0:T(8,128)(2,1)S(1)}, u32[]{:S(2)}, u32[]{:S(2)}) collective-permute-start(bf16[512,512]{1,0:T(8,128)(2,1)S(1)} %collective-permute-done.2), channel_id=1, source_target_pairs={{0,16},{1,5},{64,80},{65,69},{2,18},{3,7},{66,82},{67,71},{16,32},... | collective-permute-start | bytes 1572872 | tf_op jit(solution)/shard_map/ppermute | solution.py:39
  20.9 9.4 %collective-permute-start.7 = (bf16[512,512]{1,0:T(8,128)(2,1)S(1)}, bf16[512,512]{1,0:T(8,128)(2,1)S(1)}, u32[]{:S(2)}, u32[]{:S(2)}) collective-permute-start(bf16[512,512]{1,0:T(8,128)(2,1)S(1)} %collective-permute-done.2), channel_id=1, source_target_pairs={{0,48},{1,13},{64,112},{65,77},{2,50},{3,15},{66,114},{67,79},{16,... | collective-permute-start | bytes 1572872 | tf_op jit(solution)/shard_map/ppermute | solution.py:39
  22.4 13.4 %collective-permute-start.8 = (bf16[512,512]{1,0:T(8,128)(2,1)S(1)}, bf16[512,512]{1,0:T(8,128)(2,1)S(1)}, u32[]{:S(2)}, u32[]{:S(2)}) collective-permute-start(bf16[512,512]{1,0:T(8,128)(2,1)S(1)} %collective-permute-done.2), channel_id=1, source_target_pairs={{0,32},{1,9},{64,96},{65,73},{2,34},{3,11},{66,98},{67,75},{16,48}... | collective-permute-start | bytes 1572872 | tf_op jit(solution)/shard_map/ppermute | solution.py:39
  24.7 11.7 %copy-start.2 = (bf16[256,512]{1,0:T(8,128)(2,1)S(1)}, bf16[256,512]{1,0:T(8,128)(2,1)}, u32[]{:S(2)}) copy-start(bf16[256,512]{1,0:T(8,128)(2,1)} %param.8) | copy-start | bytes 786436
  24.7 11.7 %copy-start.3 = (bf16[256,512]{1,0:T(8,128)(2,1)S(1)}, bf16[256,512]{1,0:T(8,128)(2,1)}, u32[]{:S(2)}) copy-start(bf16[256,512]{1,0:T(8,128)(2,1)} %param.6) | copy-start | bytes 786436
  24.8 17.9 %slice-start = ((s8[6291456]{0:T(1024)(128)(4,1)}), s8[4194304]{0:T(1024)(128)(4,1)S(1)}, s32[]{:S(2)}) async-start(s8[6291456]{0:T(1024)(128)(4,1)} %bitcast.4), calls=%async_computation | async-start | bytes 8388608
  35.9 6.5 %collective-permute-start.9 = (bf16[3584,512]{1,0:T(8,128)(2,1)S(1)}, bf16[3584,512]{1,0:T(8,128)(2,1)S(1)}, u32[]{:S(2)}, u32[]{:S(2)}) collective-permute-start(bf16[3584,512]{1,0:T(8,128)(2,1)S(1)} %get-tuple-element.49), channel_id=1, source_target_pairs={{0,1},{1,0},{64,65},{65,64},{2,3},{3,2},{66,67},{67,66},{16,17},{1... | collective-permute-start | bytes 11010056 | tf_op jit(solution)/shard_map/ppermute | solution.py:39
  36.4 6.3 %slice-start.1 = ((s8[6291456]{0:T(1024)(128)(4,1)}), s8[2097152]{0:T(1024)(128)(4,1)S(1)}, s32[]{:S(2)}) async-start(s8[6291456]{0:T(1024)(128)(4,1)} %bitcast.4), calls=%async_computation.1 | async-start | bytes 4194304
  51.1 5.2 %collective-permute-start.12 = (bf16[2048,512]{1,0:T(8,128)(2,1)S(1)}, bf16[2048,512]{1,0:T(8,128)(2,1)S(1)}, u32[]{:S(2)}, u32[]{:S(2)}) collective-permute-start(bf16[2048,512]{1,0:T(8,128)(2,1)S(1)} %get-tuple-element.32), channel_id=1, source_target_pairs={{0,1},{1,0},{64,65},{65,64},{2,3},{3,2},{66,67},{67,66},{16,17},{1... | collective-permute-start | bytes 6291464 | tf_op jit(solution)/shard_map/ppermute | solution.py:39
  51.6 4.2 %collective-permute-start.10 = (bf16[256,512]{1,0:T(8,128)(2,1)S(1)}, bf16[256,512]{1,0:T(8,128)(2,1)S(1)}, u32[]{:S(2)}, u32[]{:S(2)}) collective-permute-start(bf16[256,512]{1,0:T(8,128)(2,1)S(1)} %get-tuple-element.28), channel_id=1, source_target_pairs={{0,1},{1,0},{64,65},{65,64},{2,3},{3,2},{66,67},{67,66},{16,17},{1... | collective-permute-start | bytes 786440 | tf_op jit(solution)/shard_map/ppermute | solution.py:39
  55.8 6.2 %collective-permute-start.11 = (bf16[2048,512]{1,0:T(8,128)(2,1)S(1)}, bf16[2048,512]{1,0:T(8,128)(2,1)S(1)}, u32[]{:S(2)}, u32[]{:S(2)}) collective-permute-start(bf16[2048,512]{1,0:T(8,128)(2,1)S(1)} %get-tuple-element.29), channel_id=1, source_target_pairs={{0,1},{1,0},{64,65},{65,64},{2,3},{3,2},{66,67},{67,66},{16,17},{1... | collective-permute-start | bytes 6291464 | tf_op jit(solution)/shard_map/ppermute | solution.py:39
  57.2 10.8 %collective-permute-start.13 = (bf16[576,512]{1,0:T(8,128)(2,1)S(1)}, bf16[576,512]{1,0:T(8,128)(2,1)S(1)}, u32[]{:S(2)}, u32[]{:S(2)}) collective-permute-start(bf16[576,512]{1,0:T(8,128)(2,1)S(1)} %pad_maximum_fusion.4), channel_id=1, source_target_pairs={{0,16},{1,5},{64,80},{65,69},{2,18},{3,7},{66,82},{67,71},{16,32},... | collective-permute-start | bytes 1769480 | tf_op jit(solution)/shard_map/ppermute | solution.py:39
  59.5 9.1 %collective-permute-start.14 = (bf16[576,512]{1,0:T(8,128)(2,1)S(1)}, bf16[576,512]{1,0:T(8,128)(2,1)S(1)}, u32[]{:S(2)}, u32[]{:S(2)}) collective-permute-start(bf16[576,512]{1,0:T(8,128)(2,1)S(1)} %pad_maximum_fusion.5), channel_id=1, source_target_pairs={{0,48},{1,13},{64,112},{65,77},{2,50},{3,15},{66,114},{67,79},{16,... | collective-permute-start | bytes 1769480 | tf_op jit(solution)/shard_map/ppermute | solution.py:39
  60.5 14.9 %collective-permute-start.15 = (bf16[576,512]{1,0:T(8,128)(2,1)S(1)}, bf16[576,512]{1,0:T(8,128)(2,1)S(1)}, u32[]{:S(2)}, u32[]{:S(2)}) collective-permute-start(bf16[576,512]{1,0:T(8,128)(2,1)S(1)} %pad_maximum_fusion.6), channel_id=1, source_target_pairs={{0,32},{1,9},{64,96},{65,73},{2,34},{3,11},{66,98},{67,75},{16,48}... | collective-permute-start | bytes 1769480 | tf_op jit(solution)/shard_map/ppermute | solution.py:39
  75.9 21.2 %collective-permute-start.16 = (bf16[576,512]{1,0:T(8,128)(2,1)S(1)}, bf16[576,512]{1,0:T(8,128)(2,1)S(1)}, u32[]{:S(2)}, u32[]{:S(2)}) collective-permute-start(bf16[576,512]{1,0:T(8,128)(2,1)S(1)} %get-tuple-element.67), channel_id=1, source_target_pairs={{0,4},{1,17},{64,68},{65,81},{2,6},{3,19},{66,70},{67,83},{16,20},... | collective-permute-start | bytes 1769480 | tf_op jit(solution)/shard_map/ppermute | solution.py:39
  77.5 19.6 %collective-permute-start.17 = (bf16[576,512]{1,0:T(8,128)(2,1)S(1)}, bf16[576,512]{1,0:T(8,128)(2,1)S(1)}, u32[]{:S(2)}, u32[]{:S(2)}) collective-permute-start(bf16[576,512]{1,0:T(8,128)(2,1)S(1)} %get-tuple-element.68), channel_id=1, source_target_pairs={{0,12},{1,49},{64,76},{65,113},{2,14},{3,51},{66,78},{67,115},{16,... | collective-permute-start | bytes 1769480 | tf_op jit(solution)/shard_map/ppermute | solution.py:39
  78.6 37.2 %copy-start = (bf16[512,512]{1,0:T(8,128)(2,1)S(1)}, bf16[512,512]{1,0:T(8,128)(2,1)}, u32[]{:S(2)}) copy-start(bf16[512,512]{1,0:T(8,128)(2,1)} %weight.1) | copy-start | bytes 1572868
  78.6 18.5 %collective-permute-start.18 = (bf16[576,512]{1,0:T(8,128)(2,1)S(1)}, bf16[576,512]{1,0:T(8,128)(2,1)S(1)}, u32[]{:S(2)}, u32[]{:S(2)}) collective-permute-start(bf16[576,512]{1,0:T(8,128)(2,1)S(1)} %get-tuple-element.69), channel_id=1, source_target_pairs={{0,8},{1,33},{64,72},{65,97},{2,10},{3,35},{66,74},{67,99},{16,24}... | collective-permute-start | bytes 1769480 | tf_op jit(solution)/shard_map/ppermute | solution.py:39
  79.5 13.3 %collective-permute-start.26 = (bf16[512,512]{1,0:T(8,128)(2,1)S(1)}, bf16[512,512]{1,0:T(8,128)(2,1)S(1)}, u32[]{:S(2)}, u32[]{:S(2)}) collective-permute-start(bf16[512,512]{1,0:T(8,128)(2,1)S(1)} %slice.83), channel_id=1, source_target_pairs={{0,64},{1,3},{64,0},{65,67},{2,66},{3,1},{66,2},{67,65},{16,80},{1... | collective-permute-start | bytes 1572872 | tf_op jit(solution)/shard_map/ppermute | solution.py:39
  92.8 15.2 %collective-permute-start.27 = (bf16[512,512]{1,0:T(8,128)(2,1)S(1)}, bf16[512,512]{1,0:T(8,128)(2,1)S(1)}, u32[]{:S(2)}, u32[]{:S(2)}) collective-permute-start(bf16[512,512]{1,0:T(8,128)(2,1)S(1)} %collective-permute-done.26), channel_id=1, source_target_pairs={{0,1},{1,0},{64,65},{65,64},{2,3},{3,2},{66,67},{67,66},{16,17},{1... | collective-permute-start | bytes 1572872 | tf_op jit(solution)/shard_map/ppermute | solution.py:39
  97.5 5.1 %collective-permute-start.19 = (bf16[64,512]{1,0:T(8,128)(2,1)S(1)}, bf16[64,512]{1,0:T(8,128)(2,1)S(1)}, u32[]{:S(2)}, u32[]{:S(2)}) collective-permute-start(bf16[64,512]{1,0:T(8,128)(2,1)S(1)} %slice.81), channel_id=1, source_target_pairs={{0,64},{1,65},{64,2},{65,3},{2,66},{3,67},{66,0},{67,1},{16,80},{1... | collective-permute-start | bytes 196616 | tf_op jit(solution)/shard_map/ppermute | solution.py:39
  99.7 3.2 %collective-permute-start.20 = (bf16[64,512]{1,0:T(8,128)(2,1)S(1)}, bf16[64,512]{1,0:T(8,128)(2,1)S(1)}, u32[]{:S(2)}, u32[]{:S(2)}) collective-permute-start(bf16[64,512]{1,0:T(8,128)(2,1)S(1)} %slice.81), channel_id=1, source_target_pairs={{0,66},{1,67},{64,0},{65,1},{2,64},{3,65},{66,2},{67,3},{16,82},{1... | collective-permute-start | bytes 196616 | tf_op jit(solution)/shard_map/ppermute | solution.py:39
  100.2 4.6 %collective-permute-start.21 = (bf16[64,512]{1,0:T(8,128)(2,1)S(1)}, bf16[64,512]{1,0:T(8,128)(2,1)S(1)}, u32[]{:S(2)}, u32[]{:S(2)}) collective-permute-start(bf16[64,512]{1,0:T(8,128)(2,1)S(1)} %slice.81), channel_id=1, source_target_pairs={{0,2},{1,3},{64,66},{65,67},{2,0},{3,1},{66,64},{67,65},{16,18},{1... | collective-permute-start | bytes 196616 | tf_op jit(solution)/shard_map/ppermute | solution.py:39
  104.9 6.0 %collective-permute-start.22 = (bf16[64,512]{1,0:T(8,128)(2,1)S(1)}, bf16[64,512]{1,0:T(8,128)(2,1)S(1)}, u32[]{:S(2)}, u32[]{:S(2)}) collective-permute-start(bf16[64,512]{1,0:T(8,128)(2,1)S(1)} %add_convert_fusion.6), channel_id=1, source_target_pairs={{0,16},{1,5},{64,80},{65,69},{2,18},{3,7},{66,82},{67,71},{16,32},... | collective-permute-start | bytes 196616 | tf_op jit(solution)/shard_map/ppermute | solution.py:39
  105.9 4.9 %collective-permute-start.23 = (bf16[64,512]{1,0:T(8,128)(2,1)S(1)}, bf16[64,512]{1,0:T(8,128)(2,1)S(1)}, u32[]{:S(2)}, u32[]{:S(2)}) collective-permute-start(bf16[64,512]{1,0:T(8,128)(2,1)S(1)} %add_convert_fusion.6), channel_id=1, source_target_pairs={{0,48},{1,13},{64,112},{65,77},{2,50},{3,15},{66,114},{67,79},{16,... | collective-permute-start | bytes 196616 | tf_op jit(solution)/shard_map/ppermute | solution.py:39
  107.6 4.6 %collective-permute-start.24 = (bf16[64,512]{1,0:T(8,128)(2,1)S(1)}, bf16[64,512]{1,0:T(8,128)(2,1)S(1)}, u32[]{:S(2)}, u32[]{:S(2)}) collective-permute-start(bf16[64,512]{1,0:T(8,128)(2,1)S(1)} %add_convert_fusion.6), channel_id=1, source_target_pairs={{0,32},{1,9},{64,96},{65,73},{2,34},{3,11},{66,98},{67,75},{16,48}... | collective-permute-start | bytes 196616 | tf_op jit(solution)/shard_map/ppermute | solution.py:39
  108.2 7.6 %collective-permute-start.28 = (bf16[256,512]{1,0:T(8,128)(2,1)S(1)}, bf16[256,512]{1,0:T(8,128)(2,1)S(1)}, u32[]{:S(2)}, u32[]{:S(2)}) collective-permute-start(bf16[256,512]{1,0:T(8,128)(2,1)S(1)} %slice_select_fusion), channel_id=1, source_target_pairs={{0,1},{1,0},{64,65},{65,64},{2,3},{3,2},{66,67},{67,66},{16,17},{1... | collective-permute-start | bytes 786440 | tf_op jit(solution)/shard_map/ppermute | solution.py:39
  112.3 4.8 %collective-permute-start.25 = (bf16[256,512]{1,0:T(8,128)(2,1)S(1)}, bf16[256,512]{1,0:T(8,128)(2,1)S(1)}, u32[]{:S(2)}, u32[]{:S(2)}) collective-permute-start(bf16[256,512]{1,0:T(8,128)(2,1)S(1)} %pad_maximum_fusion.7.mine), channel_id=1, source_target_pairs={{0,1},{1,0},{64,65},{65,64},{2,3},{3,2},{66,67},{67,66},{16,17},{1... | collective-permute-start | bytes 786440 | tf_op jit(solution)/shard_map/ppermute | solution.py:39

commit v4 on v3

--- a/solution.py
+++ b/solution.py
@@ -362,8 +362,11 @@
     far, part = far[: 2 * SPAN], far[2 * SPAN :]
     near = add(*ring_sum([stack(piece, part) for piece in split(sum_near, 2 * SPAN)], cross_ring))
     near, part = near[: 2 * SPAN], near[2 * SPAN :]
-    passed = permute(permute(far, to_z), to_core)
-    part = add(*ring_gather(part, along_z))
+    passed = permute(far, to_z)
+    around = ring_gather(part, along_z)
+    passed, *around = lax.optimization_barrier((passed, *around))
+    part = add(*around)
+    passed = permute(passed, to_core)
     mine = stack(*ring_gather(part, ring))
     other = permute(mine, to_core)
     final = add(near, passed)

time: 119 us -> 117 us (0.983)
  starting transfers between devices: 47.9 us -> 45.1 us
    ppermute x29, starting transfers between devices: 47.9 us -> 45.1 us  [permute(): return lax.ppermute(value, ('row', 'col'), pairs)]
  transfers between devices with their start and end apart: 29 -> 29, of which waited for: 17 -> 19; matrix products, arithmetic and copies ran while one was open for 3% -> 3% of each run, Pallas kernels for 5% -> 5%
where the time goes in v4:
time: 117 us
  waiting for transfers between devices  48.2 us (41%)
  starting transfers between devices  45.1 us (39%)
  Pallas kernels  15.7 us (13%)
  other arithmetic  4.31 us (4%)
  local copies, waits for them, and re-layouts  1.76 us (2%)
  between operations  1.54 us (1%)
    ppermute x29, waiting for transfers between devices, permute(): return lax.ppermute(value, ('row', 'col'), pairs)  48.2 us
    ppermute x29, starting transfers between devices, permute(): return lax.ppermute(value, ('row', 'col'), pairs)  45.1 us
    pallas_call x2, Pallas kernels, forward_sums(): pl.pallas_call(functools.partial(forward_kernel, half), out_shape=(shape(...  7.12 us
    pallas_call x1, Pallas kernels, backward_sums(): pl.pallas_call(backward_kernel, out_shape=(shape(HALF_ROWS), shape(HALF_R...  5.65 us
  transfers between devices with their start and end apart: 29, of which 19 were waited for; matrix products, arithmetic and copies ran while one was open for 3% of the time, Pallas kernels for 5%

profile of v4, /device:TPU:1, one launch (start us, length us, event | category | flops | bytes accessed | tf_op | source)
XLA Modules:
  0.0 116.7 jit_solution(9309897849271407855)
XLA Ops:
  0.6 1.5 %collective-permute-start = (bf16[256,512]{1,0:T(8,128)(2,1)}, bf16[256,512]{1,0:T(8,128)(2,1)S(1)}, u32[]{:S(2)}, u32[]{:S(2)}) collective-permute-start(bf16[256,512]{1,0:T(8,128)(2,1)} %param.6), channel_id=1, source_target_pairs={{0,1},{1,0},{64,65},{65,64},{2,3},{3,2},{66,67},{67,66},{16,17},{1... | collective-permute-start | bytes 786440 | tf_op jit(solution)/shard_map/ppermute | solution.py:39
  2.2 1.3 %collective-permute-done = bf16[256,512]{1,0:T(8,128)(2,1)S(1)} collective-permute-done((bf16[256,512]{1,0:T(8,128)(2,1)}, bf16[256,512]{1,0:T(8,128)(2,1)S(1)}, u32[]{:S(2)}, u32[]{:S(2)}) %collective-permute-start) | collective-permute-done | bytes 262176 | tf_op jit(solution)/shard_map/ppermute | solution.py:39
  3.9 1.5 %constant_dynamic-update-slice_fusion.15 = (bf16[8192,512]{1,0:T(8,128)(2,1)S(1)}, bf16[512,512]{1,0:T(8,128)(2,1)S(1)}) fusion(bf16[256,512]{1,0:T(8,128)(2,1)} %param.8, bf16[256,512]{1,0:T(8,128)(2,1)S(1)} %collective-permute-done.1, bf16[256,512]{1,0:T(8,128)(2,1)} %param.6, bf16[256,512]{1,0:T(8,128)(2,1)S(1)} %collective-permute-done, pred[]{:T(512)S(6)} %eq.5), kind=kLoop, calls=%fused_computation.35 | loop fusion | flops 4980735 | bytes 2097153
  5.3 3.8 %collective-permute-start.2 = (bf16[512,512]{1,0:T(8,128)(2,1)S(1)}, bf16[512,512]{1,0:T(8,128)(2,1)S(1)}, u32[]{:S(2)}, u32[]{:S(2)}) collective-permute-start(bf16[512,512]{1,0:T(8,128)(2,1)S(1)} %get-tuple-element.50), channel_id=1, source_target_pairs={{0,64},{1,3},{64,0},{65,67},{2,66},{3,1},{66,2},{67,65},{16,80},{1... | collective-permute-start | bytes 1572872 | tf_op jit(solution)/shard_map/ppermute | solution.py:39
  9.1 2.7 %collective-permute-start.3 = (bf16[512,512]{1,0:T(8,128)(2,1)S(1)}, bf16[512,512]{1,0:T(8,128)(2,1)S(1)}, u32[]{:S(2)}, u32[]{:S(2)}) collective-permute-start(bf16[512,512]{1,0:T(8,128)(2,1)S(1)} %get-tuple-element.50), channel_id=1, source_target_pairs={{0,32},{1,9},{64,96},{65,73},{2,34},{3,11},{66,98},{67,75},{16,48}... | collective-permute-start | bytes 1572872 | tf_op jit(solution)/shard_map/ppermute | solution.py:39
  12.2 2.4 %collective-permute-start.5 = (bf16[512,512]{1,0:T(8,128)(2,1)S(1)}, bf16[512,512]{1,0:T(8,128)(2,1)S(1)}, u32[]{:S(2)}, u32[]{:S(2)}) collective-permute-start(bf16[512,512]{1,0:T(8,128)(2,1)S(1)} %get-tuple-element.50), channel_id=1, source_target_pairs={{0,48},{1,13},{64,112},{65,77},{2,50},{3,15},{66,114},{67,79},{16,... | collective-permute-start | bytes 1572872 | tf_op jit(solution)/shard_map/ppermute | solution.py:39
  15.2 0.7 copy-done.1
  15.9 0.7 shard_map.85.lists
  16.5 3.2 %collective-permute-done.2 = bf16[512,512]{1,0:T(8,128)(2,1)S(1)} collective-permute-done((bf16[512,512]{1,0:T(8,128)(2,1)S(1)}, bf16[512,512]{1,0:T(8,128)(2,1)S(1)}, u32[]{:S(2)}, u32[]{:S(2)}) %collective-permute-start.2) | collective-permute-done | bytes 524320 | tf_op jit(solution)/shard_map/ppermute | solution.py:39
  19.7 1.2 %collective-permute-start.6 = (bf16[512,512]{1,0:T(8,128)(2,1)S(1)}, bf16[512,512]{1,0:T(8,128)(2,1)S(1)}, u32[]{:S(2)}, u32[]{:S(2)}) collective-permute-start(bf16[512,512]{1,0:T(8,128)(2,1)S(1)} %collective-permute-done.2), channel_id=1, source_target_pairs={{0,16},{1,5},{64,80},{65,69},{2,18},{3,7},{66,82},{67,71},{16,32},... | collective-permute-start | bytes 1572872 | tf_op jit(solution)/shard_map/ppermute | solution.py:39
  20.9 1.5 %collective-permute-start.7 = (bf16[512,512]{1,0:T(8,128)(2,1)S(1)}, bf16[512,512]{1,0:T(8,128)(2,1)S(1)}, u32[]{:S(2)}, u32[]{:S(2)}) collective-permute-start(bf16[512,512]{1,0:T(8,128)(2,1)S(1)} %collective-permute-done.2), channel_id=1, source_target_pairs={{0,48},{1,13},{64,112},{65,77},{2,50},{3,15},{66,114},{67,79},{16,... | collective-permute-start | bytes 1572872 | tf_op jit(solution)/shard_map/ppermute | solution.py:39
  22.4 1.5 %collective-permute-start.8 = (bf16[512,512]{1,0:T(8,128)(2,1)S(1)}, bf16[512,512]{1,0:T(8,128)(2,1)S(1)}, u32[]{:S(2)}, u32[]{:S(2)}) collective-permute-start(bf16[512,512]{1,0:T(8,128)(2,1)S(1)} %collective-permute-done.2), channel_id=1, source_target_pairs={{0,32},{1,9},{64,96},{65,73},{2,34},{3,11},{66,98},{67,75},{16,48}... | collective-permute-start | bytes 1572872 | tf_op jit(solution)/shard_map/ppermute | solution.py:39
  24.0 0.5 collective-permute-done.4
  24.8 5.0 %collective-permute-done.6 = bf16[512,512]{1,0:T(8,128)(2,1)S(1)} collective-permute-done((bf16[512,512]{1,0:T(8,128)(2,1)S(1)}, bf16[512,512]{1,0:T(8,128)(2,1)S(1)}, u32[]{:S(2)}, u32[]{:S(2)}) %collective-permute-start.6) | collective-permute-done | bytes 524320 | tf_op jit(solution)/shard_map/ppermute | solution.py:39
  30.4 5.5 %collective-permute-done.8 = bf16[512,512]{1,0:T(8,128)(2,1)S(1)} collective-permute-done((bf16[512,512]{1,0:T(8,128)(2,1)S(1)}, bf16[512,512]{1,0:T(8,128)(2,1)S(1)}, u32[]{:S(2)}, u32[]{:S(2)}) %collective-permute-start.8) | collective-permute-done | bytes 524320 | tf_op jit(solution)/shard_map/ppermute | solution.py:39
  35.9 0.5 collective-permute-start.9
  36.7 5.7 %collective-permute-done.9 = bf16[3584,512]{1,0:T(8,128)(2,1)S(1)} collective-permute-done((bf16[3584,512]{1,0:T(8,128)(2,1)S(1)}, bf16[3584,512]{1,0:T(8,128)(2,1)S(1)}, u32[]{:S(2)}, u32[]{:S(2)}) %collective-permute-start.9) | collective-permute-done | bytes 3670048 | tf_op jit(solution)/shard_map/ppermute | solution.py:39
  42.7 5.6 %shard_map.86 = (bf16[2048,512]{1,0:T(8,128)(2,1)S(1)}, bf16[2048,512]{1,0:T(8,128)(2,1)S(1)}, bf16[256,512]{1,0:T(8,128)(2,1)S(1)}, bf16[256,512]{1,0:T(8,128)(2,1)S(1)}) custom-call(s32[8,384]{1,0:T(8,128)S(1)} %shard_map.85.lists, bf16[192,128,128]{2,1,0:T(8,128)(2,1)S(1)} %bitcast.6, bf16[8192,512]{1,0:T(8,128)(2,1)S(1)} %constant_dynamic-update-slice_fusion.7.panels), custom_call_target="tpu_custom_call" | custom-call | tf_op jit(solution)/shard_map/pallas_call | solution.py:239
  48.3 3.5 %shard_map.87 = (bf16[2048,512]{1,0:T(8,128)(2,1)S(1)}, bf16[2048,512]{1,0:T(8,128)(2,1)S(1)}) custom-call(s32[8,384]{1,0:T(8,128)S(1)} %shard_map.85.lists, bf16[192,128,128]{2,1,0:T(8,128)(2,1)S(1)} %bitcast.7, bf16[8192,512]{1,0:T(8,128)(2,1)S(1)} %constant_dynamic-update-slice_fusion.7.panels, bf16[2048,512]{1,0:T(8,128)(2,1)S(1)} %get-tuple-element.29.back), custom_call_target="tpu_custom_call" | custom-call | tf_op jit(solution)/shard_map/pallas_call | solution.py:254
  51.9 0.5 collective-permute-start.11
  52.4 3.7 %shard_map.88 = (bf16[2048,512]{1,0:T(8,128)(2,1)S(1)}, bf16[2048,512]{1,0:T(8,128)(2,1)S(1)}) custom-call(s32[8,384]{1,0:T(8,128)S(1)} %shard_map.85.lists, bf16[192,128,128]{2,1,0:T(8,128)(2,1)S(1)} %bitcast.8, bf16[8192,512]{1,0:T(8,128)(2,1)S(1)} %constant_dynamic-update-slice_fusion.7.panels, bf16[2048,512]{1,0:T(8,128)(2,1)S(1)} %get-tuple-element.32.back), custom_call_target="tpu_custom_call" | custom-call | tf_op jit(solution)/shard_map/pallas_call | solution.py:254
  56.7 0.6 add_convert_fusion.1
  57.6 2.2 %collective-permute-start.12 = (bf16[576,512]{1,0:T(8,128)(2,1)S(1)}, bf16[576,512]{1,0:T(8,128)(2,1)S(1)}, u32[]{:S(2)}, u32[]{:S(2)}) collective-permute-start(bf16[576,512]{1,0:T(8,128)(2,1)S(1)} %pad_maximum_fusion.4), channel_id=1, source_target_pairs={{0,16},{1,5},{64,80},{65,69},{2,18},{3,7},{66,82},{67,71},{16,32},... | collective-permute-start | bytes 1769480 | tf_op jit(solution)/shard_map/ppermute | solution.py:39
  59.8 0.6 collective-permute-start.13
  60.5 1.9 %collective-permute-start.14 = (bf16[576,512]{1,0:T(8,128)(2,1)S(1)}, bf16[576,512]{1,0:T(8,128)(2,1)S(1)}, u32[]{:S(2)}, u32[]{:S(2)}) collective-permute-start(bf16[576,512]{1,0:T(8,128)(2,1)S(1)} %pad_maximum_fusion.6), channel_id=1, source_target_pairs={{0,32},{1,9},{64,96},{65,73},{2,34},{3,11},{66,98},{67,75},{16,48}... | collective-permute-start | bytes 1769480 | tf_op jit(solution)/shard_map/ppermute | solution.py:39
  62.3 0.7 add_convert_fusion
  63.2 4.7 %collective-permute-done.12 = bf16[576,512]{1,0:T(8,128)(2,1)S(1)} collective-permute-done((bf16[576,512]{1,0:T(8,128)(2,1)S(1)}, bf16[576,512]{1,0:T(8,128)(2,1)S(1)}, u32[]{:S(2)}, u32[]{:S(2)}) %collective-permute-start.12) | collective-permute-done | bytes 589856 | tf_op jit(solution)/shard_map/ppermute | solution.py:39
  67.9 1.0 collective-permute-done.13
  68.9 5.9 %collective-permute-done.14 = bf16[576,512]{1,0:T(8,128)(2,1)S(1)} collective-permute-done((bf16[576,512]{1,0:T(8,128)(2,1)S(1)}, bf16[576,512]{1,0:T(8,128)(2,1)S(1)}, u32[]{:S(2)}, u32[]{:S(2)}) %collective-permute-start.14) | collective-permute-done | bytes 589856 | tf_op jit(solution)/shard_map/ppermute | solution.py:39
  75.2 0.9 collective-permute-start.17
  76.2 2.1 %collective-permute-start.18 = (bf16[576,512]{1,0:T(8,128)(2,1)S(1)}, bf16[576,512]{1,0:T(8,128)(2,1)S(1)}, u32[]{:S(2)}, u32[]{:S(2)}) collective-permute-start(bf16[576,512]{1,0:T(8,128)(2,1)S(1)} %get-tuple-element.78), channel_id=1, source_target_pairs={{0,12},{1,49},{64,76},{65,113},{2,14},{3,51},{66,78},{67,115},{16,... | collective-permute-start | bytes 1769480 | tf_op jit(solution)/shard_map/ppermute | solution.py:39
  78.2 1.1 collective-permute-start.19
  79.4 4.7 %collective-permute-start.15 = (bf16[512,512]{1,0:T(8,128)(2,1)S(1)}, bf16[512,512]{1,0:T(8,128)(2,1)S(1)}, u32[]{:S(2)}, u32[]{:S(2)}) collective-permute-start(bf16[512,512]{1,0:T(8,128)(2,1)S(1)} %slice.76), channel_id=1, source_target_pairs={{0,64},{1,3},{64,0},{65,67},{2,66},{3,1},{66,2},{67,65},{16,80},{1... | collective-permute-start | bytes 1572872 | tf_op jit(solution)/shard_map/ppermute | solution.py:39
  84.1 1.6 %collective-permute-done.17 = bf16[576,512]{1,0:T(8,128)(2,1)S(1)} collective-permute-done((bf16[576,512]{1,0:T(8,128)(2,1)S(1)}, bf16[576,512]{1,0:T(8,128)(2,1)S(1)}, u32[]{:S(2)}, u32[]{:S(2)}) %collective-permute-start.17) | collective-permute-done | bytes 589856 | tf_op jit(solution)/shard_map/ppermute | solution.py:39
  85.7 5.7 %collective-permute-done.18 = bf16[576,512]{1,0:T(8,128)(2,1)S(1)} collective-permute-done((bf16[576,512]{1,0:T(8,128)(2,1)S(1)}, bf16[576,512]{1,0:T(8,128)(2,1)S(1)}, u32[]{:S(2)}, u32[]{:S(2)}) %collective-permute-start.18) | collective-permute-done | bytes 589856 | tf_op jit(solution)/shard_map/ppermute | solution.py:39
  91.4 1.8 %collective-permute-done.19 = bf16[576,512]{1,0:T(8,128)(2,1)S(1)} collective-permute-done((bf16[576,512]{1,0:T(8,128)(2,1)S(1)}, bf16[576,512]{1,0:T(8,128)(2,1)S(1)}, u32[]{:S(2)}, u32[]{:S(2)}) %collective-permute-start.19) | collective-permute-done | bytes 589856 | tf_op jit(solution)/shard_map/ppermute | solution.py:39
  93.6 1.9 %collective-permute-start.20 = (bf16[64,512]{1,0:T(8,128)(2,1)S(1)}, bf16[64,512]{1,0:T(8,128)(2,1)S(1)}, u32[]{:S(2)}, u32[]{:S(2)}) collective-permute-start(bf16[64,512]{1,0:T(8,128)(2,1)S(1)} %slice.82), channel_id=1, source_target_pairs={{0,64},{1,65},{64,2},{65,3},{2,66},{3,67},{66,0},{67,1},{16,80},{1... | collective-permute-start | bytes 196616 | tf_op jit(solution)/shard_map/ppermute | solution.py:39
  95.5 1.6 %collective-permute-start.21 = (bf16[64,512]{1,0:T(8,128)(2,1)S(1)}, bf16[64,512]{1,0:T(8,128)(2,1)S(1)}, u32[]{:S(2)}, u32[]{:S(2)}) collective-permute-start(bf16[64,512]{1,0:T(8,128)(2,1)S(1)} %slice.82), channel_id=1, source_target_pairs={{0,66},{1,67},{64,0},{65,1},{2,64},{3,65},{66,2},{67,3},{16,82},{1... | collective-permute-start | bytes 196616 | tf_op jit(solution)/shard_map/ppermute | solution.py:39
  97.0 2.3 %collective-permute-start.22 = (bf16[64,512]{1,0:T(8,128)(2,1)S(1)}, bf16[64,512]{1,0:T(8,128)(2,1)S(1)}, u32[]{:S(2)}, u32[]{:S(2)}) collective-permute-start(bf16[64,512]{1,0:T(8,128)(2,1)S(1)} %slice.82), channel_id=1, source_target_pairs={{0,2},{1,3},{64,66},{65,67},{2,0},{3,1},{66,64},{67,65},{16,18},{1... | collective-permute-start | bytes 196616 | tf_op jit(solution)/shard_map/ppermute | solution.py:39
  99.4 2.4 %collective-permute-done.22 = bf16[64,512]{1,0:T(8,128)(2,1)S(1)} collective-permute-done((bf16[64,512]{1,0:T(8,128)(2,1)S(1)}, bf16[64,512]{1,0:T(8,128)(2,1)S(1)}, u32[]{:S(2)}, u32[]{:S(2)}) %collective-permute-start.22) | collective-permute-done | bytes 65568 | tf_op jit(solution)/shard_map/ppermute | solution.py:39
  101.7 3.4 %collective-permute-start.27 = (bf16[512,512]{1,0:T(8,128)(2,1)S(1)}, bf16[512,512]{1,0:T(8,128)(2,1)S(1)}, u32[]{:S(2)}, u32[]{:S(2)}) collective-permute-start(bf16[512,512]{1,0:T(8,128)(2,1)S(1)} %collective-permute-done.15), channel_id=1, source_target_pairs={{0,1},{1,0},{64,65},{65,64},{2,3},{3,2},{66,67},{67,66},{16,17},{1... | collective-permute-start | bytes 1572872 | tf_op jit(solution)/shard_map/ppermute | solution.py:39
  105.2 1.2 %collective-permute-start.23 = (bf16[64,512]{1,0:T(8,128)(2,1)S(1)}, bf16[64,512]{1,0:T(8,128)(2,1)S(1)}, u32[]{:S(2)}, u32[]{:S(2)}) collective-permute-start(bf16[64,512]{1,0:T(8,128)(2,1)S(1)} %add_convert_fusion.6), channel_id=1, source_target_pairs={{0,16},{1,5},{64,80},{65,69},{2,18},{3,7},{66,82},{67,71},{16,32},... | collective-permute-start | bytes 196616 | tf_op jit(solution)/shard_map/ppermute | solution.py:39
  106.4 1.5 %collective-permute-start.24 = (bf16[64,512]{1,0:T(8,128)(2,1)S(1)}, bf16[64,512]{1,0:T(8,128)(2,1)S(1)}, u32[]{:S(2)}, u32[]{:S(2)}) collective-permute-start(bf16[64,512]{1,0:T(8,128)(2,1)S(1)} %add_convert_fusion.6), channel_id=1, source_target_pairs={{0,48},{1,13},{64,112},{65,77},{2,50},{3,15},{66,114},{67,79},{16,... | collective-permute-start | bytes 196616 | tf_op jit(solution)/shard_map/ppermute | solution.py:39
  108.5 1.3 %collective-permute-start.28 = (bf16[256,512]{1,0:T(8,128)(2,1)S(1)}, bf16[256,512]{1,0:T(8,128)(2,1)S(1)}, u32[]{:S(2)}, u32[]{:S(2)}) collective-permute-start(bf16[256,512]{1,0:T(8,128)(2,1)S(1)} %slice_select_fusion), channel_id=1, source_target_pairs={{0,1},{1,0},{64,65},{65,64},{2,3},{3,2},{66,67},{67,66},{16,17},{1... | collective-permute-start | bytes 786440 | tf_op jit(solution)/shard_map/ppermute | solution.py:39
  109.9 2.7 %collective-permute-done.25 = bf16[64,512]{1,0:T(8,128)(2,1)S(1)} collective-permute-done((bf16[64,512]{1,0:T(8,128)(2,1)S(1)}, bf16[64,512]{1,0:T(8,128)(2,1)S(1)}, u32[]{:S(2)}, u32[]{:S(2)}) %collective-permute-start.25) | collective-permute-done | bytes 65568 | tf_op jit(solution)/shard_map/ppermute | solution.py:39
  112.6 1.8 %collective-permute-start.26 = (bf16[256,512]{1,0:T(8,128)(2,1)S(1)}, bf16[256,512]{1,0:T(8,128)(2,1)S(1)}, u32[]{:S(2)}, u32[]{:S(2)}) collective-permute-start(bf16[256,512]{1,0:T(8,128)(2,1)S(1)} %pad_maximum_fusion.7.mine), channel_id=1, source_target_pairs={{0,1},{1,0},{64,65},{65,64},{2,3},{3,2},{66,67},{67,66},{16,17},{1... | collective-permute-start | bytes 786440 | tf_op jit(solution)/shard_map/ppermute | solution.py:39
  114.4 1.2 %shard_map.89 = (bf16[256,512]{1,0:T(8,128)(2,1)}, bf16[256,512]{1,0:T(8,128)(2,1)}) custom-call(bf16[512,512]{1,0:T(8,128)(2,1)S(1)} %add_convert_fusion.4.final, bf16[256,512]{1,0:T(8,128)(2,1)S(1)} %collective-permute-done.28.got, bf16[512,512]{1,0:T(8,128)(2,1)S(1)} %copy-done), custom_call_target="tpu_custom_call" | custom-call | tf_op jit(solution)/shard_map/pallas_call | solution.py:283
  115.6 1.1 shard_map.90
  (58 shorter events, 5.0 us)
Async XLA Ops:
  0.6 2.9 %collective-permute-start = (bf16[256,512]{1,0:T(8,128)(2,1)}, bf16[256,512]{1,0:T(8,128)(2,1)S(1)}, u32[]{:S(2)}, u32[]{:S(2)}) collective-permute-start(bf16[256,512]{1,0:T(8,128)(2,1)} %param.6), channel_id=1, source_target_pairs={{0,1},{1,0},{64,65},{65,64},{2,3},{3,2},{66,67},{67,66},{16,17},{1... | collective-permute-start | bytes 786440 | tf_op jit(solution)/shard_map/ppermute | solution.py:39
  2.1 1.7 %collective-permute-start.1 = (bf16[256,512]{1,0:T(8,128)(2,1)}, bf16[256,512]{1,0:T(8,128)(2,1)S(1)}, u32[]{:S(2)}, u32[]{:S(2)}) collective-permute-start(bf16[256,512]{1,0:T(8,128)(2,1)} %param.8), channel_id=1, source_target_pairs={{0,1},{1,0},{64,65},{65,64},{2,3},{3,2},{66,67},{67,66},{16,17},{1... | collective-permute-start | bytes 786440 | tf_op jit(solution)/shard_map/ppermute | solution.py:39
  5.3 14.4 %collective-permute-start.2 = (bf16[512,512]{1,0:T(8,128)(2,1)S(1)}, bf16[512,512]{1,0:T(8,128)(2,1)S(1)}, u32[]{:S(2)}, u32[]{:S(2)}) collective-permute-start(bf16[512,512]{1,0:T(8,128)(2,1)S(1)} %get-tuple-element.50), channel_id=1, source_target_pairs={{0,64},{1,3},{64,0},{65,67},{2,66},{3,1},{66,2},{67,65},{16,80},{1... | collective-permute-start | bytes 1572872 | tf_op jit(solution)/shard_map/ppermute | solution.py:39
  9.1 10.6 %collective-permute-start.3 = (bf16[512,512]{1,0:T(8,128)(2,1)S(1)}, bf16[512,512]{1,0:T(8,128)(2,1)S(1)}, u32[]{:S(2)}, u32[]{:S(2)}) collective-permute-start(bf16[512,512]{1,0:T(8,128)(2,1)S(1)} %get-tuple-element.50), channel_id=1, source_target_pairs={{0,32},{1,9},{64,96},{65,73},{2,34},{3,11},{66,98},{67,75},{16,48}... | collective-permute-start | bytes 1572872 | tf_op jit(solution)/shard_map/ppermute | solution.py:39
  11.8 12.7 %collective-permute-start.4 = (bf16[512,512]{1,0:T(8,128)(2,1)S(1)}, bf16[512,512]{1,0:T(8,128)(2,1)S(1)}, u32[]{:S(2)}, u32[]{:S(2)}) collective-permute-start(bf16[512,512]{1,0:T(8,128)(2,1)S(1)} %get-tuple-element.50), channel_id=1, source_target_pairs={{0,16},{1,5},{64,80},{65,69},{2,18},{3,7},{66,82},{67,71},{16,32},... | collective-permute-start | bytes 1572872 | tf_op jit(solution)/shard_map/ppermute | solution.py:39
  12.2 12.5 %collective-permute-start.5 = (bf16[512,512]{1,0:T(8,128)(2,1)S(1)}, bf16[512,512]{1,0:T(8,128)(2,1)S(1)}, u32[]{:S(2)}, u32[]{:S(2)}) collective-permute-start(bf16[512,512]{1,0:T(8,128)(2,1)S(1)} %get-tuple-element.50), channel_id=1, source_target_pairs={{0,48},{1,13},{64,112},{65,77},{2,50},{3,15},{66,114},{67,79},{16,... | collective-permute-start | bytes 1572872 | tf_op jit(solution)/shard_map/ppermute | solution.py:39
  15.2 0.7 copy-start.1
  19.7 10.2 %collective-permute-start.6 = (bf16[512,512]{1,0:T(8,128)(2,1)S(1)}, bf16[512,512]{1,0:T(8,128)(2,1)S(1)}, u32[]{:S(2)}, u32[]{:S(2)}) collective-permute-start(bf16[512,512]{1,0:T(8,128)(2,1)S(1)} %collective-permute-done.2), channel_id=1, source_target_pairs={{0,16},{1,5},{64,80},{65,69},{2,18},{3,7},{66,82},{67,71},{16,32},... | collective-permute-start | bytes 1572872 | tf_op jit(solution)/shard_map/ppermute | solution.py:39
  20.9 9.4 %collective-permute-start.7 = (bf16[512,512]{1,0:T(8,128)(2,1)S(1)}, bf16[512,512]{1,0:T(8,128)(2,1)S(1)}, u32[]{:S(2)}, u32[]{:S(2)}) collective-permute-start(bf16[512,512]{1,0:T(8,128)(2,1)S(1)} %collective-permute-done.2), channel_id=1, source_target_pairs={{0,48},{1,13},{64,112},{65,77},{2,50},{3,15},{66,114},{67,79},{16,... | collective-permute-start | bytes 1572872 | tf_op jit(solution)/shard_map/ppermute | solution.py:39
  22.4 13.4 %collective-permute-start.8 = (bf16[512,512]{1,0:T(8,128)(2,1)S(1)}, bf16[512,512]{1,0:T(8,128)(2,1)S(1)}, u32[]{:S(2)}, u32[]{:S(2)}) collective-permute-start(bf16[512,512]{1,0:T(8,128)(2,1)S(1)} %collective-permute-done.2), channel_id=1, source_target_pairs={{0,32},{1,9},{64,96},{65,73},{2,34},{3,11},{66,98},{67,75},{16,48}... | collective-permute-start | bytes 1572872 | tf_op jit(solution)/shard_map/ppermute | solution.py:39
  24.7 11.7 %copy-start.2 = (bf16[256,512]{1,0:T(8,128)(2,1)S(1)}, bf16[256,512]{1,0:T(8,128)(2,1)}, u32[]{:S(2)}) copy-start(bf16[256,512]{1,0:T(8,128)(2,1)} %param.8) | copy-start | bytes 786436
  24.7 11.7 %copy-start.3 = (bf16[256,512]{1,0:T(8,128)(2,1)S(1)}, bf16[256,512]{1,0:T(8,128)(2,1)}, u32[]{:S(2)}) copy-start(bf16[256,512]{1,0:T(8,128)(2,1)} %param.6) | copy-start | bytes 786436
  24.8 17.9 %slice-start = ((s8[6291456]{0:T(1024)(128)(4,1)}), s8[4194304]{0:T(1024)(128)(4,1)S(1)}, s32[]{:S(2)}) async-start(s8[6291456]{0:T(1024)(128)(4,1)} %bitcast.4), calls=%async_computation | async-start | bytes 8388608
  35.9 6.5 %collective-permute-start.9 = (bf16[3584,512]{1,0:T(8,128)(2,1)S(1)}, bf16[3584,512]{1,0:T(8,128)(2,1)S(1)}, u32[]{:S(2)}, u32[]{:S(2)}) collective-permute-start(bf16[3584,512]{1,0:T(8,128)(2,1)S(1)} %get-tuple-element.59), channel_id=1, source_target_pairs={{0,1},{1,0},{64,65},{65,64},{2,3},{3,2},{66,67},{67,66},{16,17},{1... | collective-permute-start | bytes 11010056 | tf_op jit(solution)/shard_map/ppermute | solution.py:39
  36.4 6.3 %slice-start.1 = ((s8[6291456]{0:T(1024)(128)(4,1)}), s8[2097152]{0:T(1024)(128)(4,1)S(1)}, s32[]{:S(2)}) async-start(s8[6291456]{0:T(1024)(128)(4,1)} %bitcast.4), calls=%async_computation.1 | async-start | bytes 4194304
  51.8 4.9 %collective-permute-start.10 = (bf16[2048,512]{1,0:T(8,128)(2,1)S(1)}, bf16[2048,512]{1,0:T(8,128)(2,1)S(1)}, u32[]{:S(2)}, u32[]{:S(2)}) collective-permute-start(bf16[2048,512]{1,0:T(8,128)(2,1)S(1)} %get-tuple-element.31), channel_id=1, source_target_pairs={{0,1},{1,0},{64,65},{65,64},{2,3},{3,2},{66,67},{67,66},{16,17},{1... | collective-permute-start | bytes 6291464 | tf_op jit(solution)/shard_map/ppermute | solution.py:39
  51.9 4.5 %collective-permute-start.11 = (bf16[256,512]{1,0:T(8,128)(2,1)S(1)}, bf16[256,512]{1,0:T(8,128)(2,1)S(1)}, u32[]{:S(2)}, u32[]{:S(2)}) collective-permute-start(bf16[256,512]{1,0:T(8,128)(2,1)S(1)} %get-tuple-element.35), channel_id=1, source_target_pairs={{0,1},{1,0},{64,65},{65,64},{2,3},{3,2},{66,67},{67,66},{16,17},{1... | collective-permute-start | bytes 786440 | tf_op jit(solution)/shard_map/ppermute | solution.py:39
  56.5 5.9 %collective-permute-start.16 = (bf16[2048,512]{1,0:T(8,128)(2,1)S(1)}, bf16[2048,512]{1,0:T(8,128)(2,1)S(1)}, u32[]{:S(2)}, u32[]{:S(2)}) collective-permute-start(bf16[2048,512]{1,0:T(8,128)(2,1)S(1)} %get-tuple-element.38), channel_id=1, source_target_pairs={{0,1},{1,0},{64,65},{65,64},{2,3},{3,2},{66,67},{67,66},{16,17},{1... | collective-permute-start | bytes 6291464 | tf_op jit(solution)/shard_map/ppermute | solution.py:39
  57.6 10.3 %collective-permute-start.12 = (bf16[576,512]{1,0:T(8,128)(2,1)S(1)}, bf16[576,512]{1,0:T(8,128)(2,1)S(1)}, u32[]{:S(2)}, u32[]{:S(2)}) collective-permute-start(bf16[576,512]{1,0:T(8,128)(2,1)S(1)} %pad_maximum_fusion.4), channel_id=1, source_target_pairs={{0,16},{1,5},{64,80},{65,69},{2,18},{3,7},{66,82},{67,71},{16,32},... | collective-permute-start | bytes 1769480 | tf_op jit(solution)/shard_map/ppermute | solution.py:39
  59.8 9.1 %collective-permute-start.13 = (bf16[576,512]{1,0:T(8,128)(2,1)S(1)}, bf16[576,512]{1,0:T(8,128)(2,1)S(1)}, u32[]{:S(2)}, u32[]{:S(2)}) collective-permute-start(bf16[576,512]{1,0:T(8,128)(2,1)S(1)} %pad_maximum_fusion.5), channel_id=1, source_target_pairs={{0,48},{1,13},{64,112},{65,77},{2,50},{3,15},{66,114},{67,79},{16,... | collective-permute-start | bytes 1769480 | tf_op jit(solution)/shard_map/ppermute | solution.py:39
  60.5 14.3 %collective-permute-start.14 = (bf16[576,512]{1,0:T(8,128)(2,1)S(1)}, bf16[576,512]{1,0:T(8,128)(2,1)S(1)}, u32[]{:S(2)}, u32[]{:S(2)}) collective-permute-start(bf16[576,512]{1,0:T(8,128)(2,1)S(1)} %pad_maximum_fusion.6), channel_id=1, source_target_pairs={{0,32},{1,9},{64,96},{65,73},{2,34},{3,11},{66,98},{67,75},{16,48}... | collective-permute-start | bytes 1769480 | tf_op jit(solution)/shard_map/ppermute | solution.py:39
  75.2 10.5 %collective-permute-start.17 = (bf16[576,512]{1,0:T(8,128)(2,1)S(1)}, bf16[576,512]{1,0:T(8,128)(2,1)S(1)}, u32[]{:S(2)}, u32[]{:S(2)}) collective-permute-start(bf16[576,512]{1,0:T(8,128)(2,1)S(1)} %get-tuple-element.77), channel_id=1, source_target_pairs={{0,4},{1,17},{64,68},{65,81},{2,6},{3,19},{66,70},{67,83},{16,20},... | collective-permute-start | bytes 1769480 | tf_op jit(solution)/shard_map/ppermute | solution.py:39
  76.2 15.2 %collective-permute-start.18 = (bf16[576,512]{1,0:T(8,128)(2,1)S(1)}, bf16[576,512]{1,0:T(8,128)(2,1)S(1)}, u32[]{:S(2)}, u32[]{:S(2)}) collective-permute-start(bf16[576,512]{1,0:T(8,128)(2,1)S(1)} %get-tuple-element.78), channel_id=1, source_target_pairs={{0,12},{1,49},{64,76},{65,113},{2,14},{3,51},{66,78},{67,115},{16,... | collective-permute-start | bytes 1769480 | tf_op jit(solution)/shard_map/ppermute | solution.py:39
  78.2 36.1 %copy-start = (bf16[512,512]{1,0:T(8,128)(2,1)S(1)}, bf16[512,512]{1,0:T(8,128)(2,1)}, u32[]{:S(2)}) copy-start(bf16[512,512]{1,0:T(8,128)(2,1)} %weight.1) | copy-start | bytes 1572868
  78.2 15.0 %collective-permute-start.19 = (bf16[576,512]{1,0:T(8,128)(2,1)S(1)}, bf16[576,512]{1,0:T(8,128)(2,1)S(1)}, u32[]{:S(2)}, u32[]{:S(2)}) collective-permute-start(bf16[576,512]{1,0:T(8,128)(2,1)S(1)} %get-tuple-element.79), channel_id=1, source_target_pairs={{0,8},{1,33},{64,72},{65,97},{2,10},{3,35},{66,74},{67,99},{16,24}... | collective-permute-start | bytes 1769480 | tf_op jit(solution)/shard_map/ppermute | solution.py:39
  79.4 20.0 %collective-permute-start.15 = (bf16[512,512]{1,0:T(8,128)(2,1)S(1)}, bf16[512,512]{1,0:T(8,128)(2,1)S(1)}, u32[]{:S(2)}, u32[]{:S(2)}) collective-permute-start(bf16[512,512]{1,0:T(8,128)(2,1)S(1)} %slice.76), channel_id=1, source_target_pairs={{0,64},{1,3},{64,0},{65,67},{2,66},{3,1},{66,2},{67,65},{16,80},{1... | collective-permute-start | bytes 1572872 | tf_op jit(solution)/shard_map/ppermute | solution.py:39
  93.6 5.8 %collective-permute-start.20 = (bf16[64,512]{1,0:T(8,128)(2,1)S(1)}, bf16[64,512]{1,0:T(8,128)(2,1)S(1)}, u32[]{:S(2)}, u32[]{:S(2)}) collective-permute-start(bf16[64,512]{1,0:T(8,128)(2,1)S(1)} %slice.82), channel_id=1, source_target_pairs={{0,64},{1,65},{64,2},{65,3},{2,66},{3,67},{66,0},{67,1},{16,80},{1... | collective-permute-start | bytes 196616 | tf_op jit(solution)/shard_map/ppermute | solution.py:39
  95.5 3.9 %collective-permute-start.21 = (bf16[64,512]{1,0:T(8,128)(2,1)S(1)}, bf16[64,512]{1,0:T(8,128)(2,1)S(1)}, u32[]{:S(2)}, u32[]{:S(2)}) collective-permute-start(bf16[64,512]{1,0:T(8,128)(2,1)S(1)} %slice.82), channel_id=1, source_target_pairs={{0,66},{1,67},{64,0},{65,1},{2,64},{3,65},{66,2},{67,3},{16,82},{1... | collective-permute-start | bytes 196616 | tf_op jit(solution)/shard_map/ppermute | solution.py:39
  97.0 4.7 %collective-permute-start.22 = (bf16[64,512]{1,0:T(8,128)(2,1)S(1)}, bf16[64,512]{1,0:T(8,128)(2,1)S(1)}, u32[]{:S(2)}, u32[]{:S(2)}) collective-permute-start(bf16[64,512]{1,0:T(8,128)(2,1)S(1)} %slice.82), channel_id=1, source_target_pairs={{0,2},{1,3},{64,66},{65,67},{2,0},{3,1},{66,64},{67,65},{16,18},{1... | collective-permute-start | bytes 196616 | tf_op jit(solution)/shard_map/ppermute | solution.py:39
  101.7 6.6 %collective-permute-start.27 = (bf16[512,512]{1,0:T(8,128)(2,1)S(1)}, bf16[512,512]{1,0:T(8,128)(2,1)S(1)}, u32[]{:S(2)}, u32[]{:S(2)}) collective-permute-start(bf16[512,512]{1,0:T(8,128)(2,1)S(1)} %collective-permute-done.15), channel_id=1, source_target_pairs={{0,1},{1,0},{64,65},{65,64},{2,3},{3,2},{66,67},{67,66},{16,17},{1... | collective-permute-start | bytes 1572872 | tf_op jit(solution)/shard_map/ppermute | solution.py:39
  105.2 4.7 %collective-permute-start.23 = (bf16[64,512]{1,0:T(8,128)(2,1)S(1)}, bf16[64,512]{1,0:T(8,128)(2,1)S(1)}, u32[]{:S(2)}, u32[]{:S(2)}) collective-permute-start(bf16[64,512]{1,0:T(8,128)(2,1)S(1)} %add_convert_fusion.6), channel_id=1, source_target_pairs={{0,16},{1,5},{64,80},{65,69},{2,18},{3,7},{66,82},{67,71},{16,32},... | collective-permute-start | bytes 196616 | tf_op jit(solution)/shard_map/ppermute | solution.py:39
  106.4 3.5 %collective-permute-start.24 = (bf16[64,512]{1,0:T(8,128)(2,1)S(1)}, bf16[64,512]{1,0:T(8,128)(2,1)S(1)}, u32[]{:S(2)}, u32[]{:S(2)}) collective-permute-start(bf16[64,512]{1,0:T(8,128)(2,1)S(1)} %add_convert_fusion.6), channel_id=1, source_target_pairs={{0,48},{1,13},{64,112},{65,77},{2,50},{3,15},{66,114},{67,79},{16,... | collective-permute-start | bytes 196616 | tf_op jit(solution)/shard_map/ppermute | solution.py:39
  107.9 4.6 %collective-permute-start.25 = (bf16[64,512]{1,0:T(8,128)(2,1)S(1)}, bf16[64,512]{1,0:T(8,128)(2,1)S(1)}, u32[]{:S(2)}, u32[]{:S(2)}) collective-permute-start(bf16[64,512]{1,0:T(8,128)(2,1)S(1)} %add_convert_fusion.6), channel_id=1, source_target_pairs={{0,32},{1,9},{64,96},{65,73},{2,34},{3,11},{66,98},{67,75},{16,48}... | collective-permute-start | bytes 196616 | tf_op jit(solution)/shard_map/ppermute | solution.py:39
  108.5 5.9 %collective-permute-start.28 = (bf16[256,512]{1,0:T(8,128)(2,1)S(1)}, bf16[256,512]{1,0:T(8,128)(2,1)S(1)}, u32[]{:S(2)}, u32[]{:S(2)}) collective-permute-start(bf16[256,512]{1,0:T(8,128)(2,1)S(1)} %slice_select_fusion), channel_id=1, source_target_pairs={{0,1},{1,0},{64,65},{65,64},{2,3},{3,2},{66,67},{67,66},{16,17},{1... | collective-permute-start | bytes 786440 | tf_op jit(solution)/shard_map/ppermute | solution.py:39
  112.6 3.0 %collective-permute-start.26 = (bf16[256,512]{1,0:T(8,128)(2,1)S(1)}, bf16[256,512]{1,0:T(8,128)(2,1)S(1)}, u32[]{:S(2)}, u32[]{:S(2)}) collective-permute-start(bf16[256,512]{1,0:T(8,128)(2,1)S(1)} %pad_maximum_fusion.7.mine), channel_id=1, source_target_pairs={{0,1},{1,0},{64,65},{65,64},{2,3},{3,2},{66,67},{67,66},{16,17},{1... | collective-permute-start | bytes 786440 | tf_op jit(solution)/shard_map/ppermute | solution.py:39
